TPU v7x, 32 devices: a whole 2x2x4 slice. The times are simulated.
32 devices in a mesh: seq: 16 (over z, x, core), ch: 2 (over y).
Axes of the slice: x: 2, y: 2, z: 4, core: 2. Of those that a mesh axis runs over, the one named last changes fastest.
Arguments:
- query_in: bfloat16 [8192, 2048], P('seq', 'ch'), may hold values from -6 to 6
- key_in: bfloat16 [8192, 2048], P('seq', 'ch'), may hold values from -6 to 6
- value_in: bfloat16 [8192, 2048], P('seq', 'ch'), may hold values from -6 to 6
- filter_taps: float32 [8192, 2048], P('seq', 'ch'), may hold values from -1 to 1
- skip_gain: float32 [2048], P('ch'), may hold values from 0.5 to 1.5
- out_weight: bfloat16 [2048, 2048], P('ch'), may hold values from -0.125 to 0.125
- out_grad: bfloat16 [8192, 2048], P('seq', 'ch'), may hold values from -6 to 6
Outputs:
- mixed_out: bfloat16 [8192, 2048], P('seq', 'ch')
- query_grad: bfloat16 [8192, 2048], P('seq', 'ch')
- key_grad: bfloat16 [8192, 2048], P('seq', 'ch')
- value_grad: bfloat16 [8192, 2048], P('seq', 'ch')
All inputs are finite; a program needn't handle non-finite values.
Results may differ from a plain program's by a relative error of at most 0.0049.
Values may be sent and summed in bfloat16 or wider, within the bound.
No kernel may reach another device: no remote copies, remote signals or barrier semaphores. Data moves between devices by JAX's collectives and lax.ppermute only.
A program may use at most 128 MiB of HBM per device.

v0:
```python
import math

import jax
import jax.numpy as jnp
from jax import lax
from jax.sharding import PartitionSpec as P

FULL_PRECISION = lax.Precision.HIGHEST


def phase_table(row_count, col_count, modulus, row_start):
    row_ids = jnp.arange(row_count, dtype=jnp.int32)[:, None] + row_start
    col_ids = jnp.arange(col_count, dtype=jnp.int32)[None, :]
    phase_ids = row_ids * col_ids % modulus
    angles = phase_ids.astype(jnp.float32) * (2.0 * math.pi / modulus)
    return (jnp.cos(angles), jnp.sin(angles))


def forward_spectrum(row_block, row_length, column_start, middle):
    half_rows, columns, channels = row_block.shape
    factor_rows = 2 * half_rows
    modulus = factor_rows * row_length
    cos_small, sin_small = phase_table(factor_rows, half_rows, factor_rows, 0)
    real_part = jnp.einsum("kn,njc->jkc", cos_small, row_block, precision=FULL_PRECISION)
    imag_part = -jnp.einsum("kn,njc->jkc", sin_small, row_block, precision=FULL_PRECISION)
    cos_turn, sin_turn = phase_table(columns, factor_rows, modulus, column_start)
    cos_turn = cos_turn[:, :, None]
    sin_turn = sin_turn[:, :, None]
    turned_real = real_part * cos_turn + imag_part * sin_turn
    turned_imag = imag_part * cos_turn - real_part * sin_turn
    moved_real, moved_imag = middle(turned_real, turned_imag)
    cos_long, sin_long = phase_table(row_length, row_length, row_length, 0)
    spec_real = jnp.einsum(
        "mn,njc->mjc", cos_long, moved_real, precision=FULL_PRECISION
    ) + jnp.einsum("mn,njc->mjc", sin_long, moved_imag, precision=FULL_PRECISION)
    spec_imag = jnp.einsum(
        "mn,njc->mjc", cos_long, moved_imag, precision=FULL_PRECISION
    ) - jnp.einsum("mn,njc->mjc", sin_long, moved_real, precision=FULL_PRECISION)
    return (spec_real, spec_imag)


def inverse_signal(spec_real, spec_imag, factor_rows, block_start, middle, einsum_form):
    row_length, block_count, channels = spec_real.shape
    modulus = factor_rows * row_length
    cos_long, sin_long = phase_table(row_length, row_length, row_length, 0)
    back_real = jnp.einsum(
        "nk,kjc->jnc", cos_long, spec_real, precision=FULL_PRECISION
    ) - jnp.einsum("nk,kjc->jnc", sin_long, spec_imag, precision=FULL_PRECISION)
    back_imag = jnp.einsum(
        "nk,kjc->jnc", cos_long, spec_imag, precision=FULL_PRECISION
    ) + jnp.einsum("nk,kjc->jnc", sin_long, spec_real, precision=FULL_PRECISION)
    cos_turn, sin_turn = phase_table(block_count, row_length, modulus, block_start)
    cos_turn = cos_turn[:, :, None]
    sin_turn = sin_turn[:, :, None]
    turned_real = back_real * cos_turn - back_imag * sin_turn
    turned_imag = back_imag * cos_turn + back_real * sin_turn
    moved_real, moved_imag = middle(turned_real, turned_imag)
    cos_small, sin_small = phase_table(factor_rows // 2, factor_rows, factor_rows, 0)
    result = jnp.einsum(einsum_form, cos_small, moved_real, precision=FULL_PRECISION) - jnp.einsum(
        einsum_form, sin_small, moved_imag, precision=FULL_PRECISION
    )
    return result * (1.0 / modulus)


def regroup_real(values):
    return lax.all_to_all(values, "seq", split_axis=1, concat_axis=0, tiled=True)


def regroup_pair(real_part, imag_part):
    return (
        lax.all_to_all(real_part, "seq", split_axis=1, concat_axis=0, tiled=True),
        lax.all_to_all(imag_part, "seq", split_axis=1, concat_axis=0, tiled=True),
    )


def sequence_forward(signal):
    device_count = lax.axis_size("seq")
    position = lax.axis_index("seq")
    row_length, channels = signal.shape
    row_block = regroup_real(signal.reshape(1, row_length, channels))
    return forward_spectrum(
        row_block, row_length, position * (row_length // device_count), regroup_pair
    )


def sequence_inverse(spectrum):
    device_count = lax.axis_size("seq")
    position = lax.axis_index("seq")
    row_length, block_count, channels = spectrum[0].shape
    values = inverse_signal(
        spectrum[0],
        spectrum[1],
        block_count * device_count,
        position * block_count,
        regroup_pair,
        "nk,kjc->jnc",
    )
    return regroup_real(values).reshape(row_length, channels)


def multiply_spectra(mixed_spec, taps_spec):
    return (
        mixed_spec[0] * taps_spec[0] - mixed_spec[1] * taps_spec[1],
        mixed_spec[0] * taps_spec[1] + mixed_spec[1] * taps_spec[0],
    )


def adjoint_spectra(taps_spec, grad_spec):
    return (
        taps_spec[0] * grad_spec[0] + taps_spec[1] * grad_spec[1],
        taps_spec[0] * grad_spec[1] - taps_spec[1] * grad_spec[0],
    )


def on_device(query_in, key_in, value_in, filter_taps, skip_gain, out_weight, out_grad):
    row_length, channels = key_in.shape
    query_wide = query_in.astype(jnp.float32)
    mixed_in = key_in.astype(jnp.float32) * value_in.astype(jnp.float32)
    spec_real, spec_imag = sequence_forward(jnp.concatenate([mixed_in, filter_taps], axis=1))
    mixed_spec = (spec_real[:, :, :channels], spec_imag[:, :, :channels])
    taps_spec = (spec_real[:, :, channels:], spec_imag[:, :, channels:])
    causal_part = sequence_inverse(multiply_spectra(mixed_spec, taps_spec))
    conv_out = causal_part + skip_gain * mixed_in
    gated_out = (query_wide * conv_out).astype(jnp.bfloat16)
    out_terms = jnp.dot(gated_out, out_weight, preferred_element_type=jnp.float32)
    mixed_out = lax.psum_scatter(out_terms, "ch", scatter_dimension=1, tiled=True).astype(
        jnp.bfloat16
    )
    grad_gated = lax.dot_general(
        lax.all_gather(out_grad, "ch", axis=1, tiled=True),
        out_weight,
        (((1,), (1,)), ((), ())),
        preferred_element_type=jnp.float32,
    )
    query_grad = (grad_gated * conv_out).astype(jnp.bfloat16)
    grad_conv = grad_gated * query_wide
    grad_spec = sequence_forward(grad_conv)
    causal_grad = sequence_inverse(adjoint_spectra(taps_spec, grad_spec))
    grad_mixed = causal_grad + skip_gain * grad_conv
    key_grad = (grad_mixed * value_in.astype(jnp.float32)).astype(jnp.bfloat16)
    value_grad = (grad_mixed * key_in.astype(jnp.float32)).astype(jnp.bfloat16)
    return (mixed_out, query_grad, key_grad, value_grad)


def solution(mesh):
    placed = (
        P("seq", "ch"),
        P("seq", "ch"),
        P("seq", "ch"),
        P("seq", "ch"),
        P("ch"),
        P("ch", None),
        P("seq", "ch"),
    )
    return jax.shard_map(
        on_device,
        mesh=mesh,
        in_specs=placed,
        out_specs=(P("seq", "ch"), P("seq", "ch"), P("seq", "ch"), P("seq", "ch")),
        check_vma=False,
    )
```

profile of v0, /device:TPU:0, one launch (start us, length us, event | category | flops | bytes accessed | tf_op | source)
XLA Modules:
  0.0 1590.9 jit_solution(18050652836206970832)
XLA Ops:
  7.9 37.5 %all-gather.2.cloned.1.call-done = bf16[512,2048]{1,0:T(8,128)(2,1)} async-done(((bf16[512,1024]{1,0:T(8,128)(2,1)}), bf16[512,2048]{1,0:T(8,128)(2,1)}) %all-gather.2.cloned.1.call-update) | async-done | bytes 2097168 | tf_op jit(solution)/shard_map/all_gather | solution.py:130
  45.4 5.2 fusion.215
  55.7 5.6 all-to-all-start.6
  64.1 6.3 copy.89
  70.4 32.1 %all-to-all-done.6 = f32[1,512,1024]{2,0,1:T(1,128)S(1)} async-done(((f32[1,512,1024]{2,0,1:T(1,128)}), f32[1,512,1024]{2,0,1:T(1,128)S(1)}, u32[]{:S(2)}, u32[]{:S(2)}) %all-to-all-start.6) | async-done | bytes 2097184 | tf_op jit(solution)/shard_map/all_to_all | solution.py:66
  102.5 11.7 all-to-all-start
  114.9 6.1 fusion.7
  121.0 8.3 subtract_bitcast_fusion.2
  129.3 4.5 copy.110
  133.8 58.1 %all-to-all-done = f32[1,512,2048]{2,0,1:T(1,128)} async-done(((f32[1,512,2048]{2,0,1:T(1,128)}), f32[1,512,2048]{2,0,1:T(1,128)}, u32[]{:S(2)}, u32[]{:S(2)}) %all-to-all-start) | async-done | bytes 4194336 | tf_op jit(solution)/shard_map/all_to_all | solution.py:66
  191.9 19.7 %all-to-all-start.7 = ((f32[32,32,1024]{2,0,1:T(8,128)}), f32[32,32,1024]{2,0,1:T(8,128)}, u32[]{:S(2)}, u32[]{:S(2)}) async-start(f32[32,32,1024]{2,0,1:T(8,128)} %copy.110), calls=%async_computation.8 | async-start | bytes 8388608 | tf_op jit(solution)/shard_map/all_to_all | solution.py:71
  211.6 6.6 copy.112
  218.2 71.1 %all-to-all-done.7 = f32[32,32,1024]{2,0,1:T(8,128)} async-done(((f32[32,32,1024]{2,0,1:T(8,128)}), f32[32,32,1024]{2,0,1:T(8,128)}, u32[]{:S(2)}, u32[]{:S(2)}) %all-to-all-start.7) | async-done | bytes 4194336 | tf_op jit(solution)/shard_map/all_to_all | solution.py:71
  289.2 19.9 %all-to-all-start.8 = ((f32[32,32,1024]{2,0,1:T(8,128)}), f32[32,32,1024]{2,0,1:T(8,128)}, u32[]{:S(2)}, u32[]{:S(2)}) async-start(f32[32,32,1024]{2,0,1:T(8,128)} %copy.112), calls=%async_computation.9 | async-start | bytes 8388608 | tf_op jit(solution)/shard_map/all_to_all | solution.py:72
  313.3 12.9 fusion
  326.2 15.6 add_bitcast_fusion
  341.8 8.1 copy.92
  349.9 36.9 %all-to-all-done.8 = f32[32,32,1024]{2,0,1:T(8,128)} async-done(((f32[32,32,1024]{2,0,1:T(8,128)}), f32[32,32,1024]{2,0,1:T(8,128)}, u32[]{:S(2)}, u32[]{:S(2)}) %all-to-all-start.8) | async-done | bytes 4194336 | tf_op jit(solution)/shard_map/all_to_all | solution.py:72
  386.8 19.7 %all-to-all-start.1 = ((f32[32,32,2048]{2,0,1:T(8,128)}), f32[32,32,2048]{2,0,1:T(8,128)}, u32[]{:S(2)}, u32[]{:S(2)}) async-start(f32[32,32,2048]{2,0,1:T(8,128)} %copy.92), calls=%async_computation.1 | async-start | bytes 16777216 | tf_op jit(solution)/shard_map/all_to_all | solution.py:71
  406.5 11.6 copy.94
  418.0 139.2 %all-to-all-done.1 = f32[32,32,2048]{2,0,1:T(8,128)} async-done(((f32[32,32,2048]{2,0,1:T(8,128)}), f32[32,32,2048]{2,0,1:T(8,128)}, u32[]{:S(2)}, u32[]{:S(2)}) %all-to-all-start.1) | async-done | bytes 8388640 | tf_op jit(solution)/shard_map/all_to_all | solution.py:71
  557.2 36.7 %all-to-all-start.2 = ((f32[32,32,2048]{2,0,1:T(8,128)}), f32[32,32,2048]{2,0,1:T(8,128)}, u32[]{:S(2)}, u32[]{:S(2)}) async-start(f32[32,32,2048]{2,0,1:T(8,128)} %copy.94), calls=%async_computation.2 | async-start | bytes 16777216 | tf_op jit(solution)/shard_map/all_to_all | solution.py:72
  600.6 10.6 fusion.31
  611.2 13.3 fusion.29
  624.6 13.6 convolution_add_fusion.2
  645.4 23.2 %fusion.39 = f32[512,2,2048]{2,0,1:T(8,128)} fusion(f32[512,2,2048]{2,0,1:T(8,128)S(1)} %bitcast.164), kind=kOutput, calls=%fused_computation.72 | convolution fusion | flops 12888571904 | bytes 16777216 | tf_op jit(solution)/shard_map/mn,njc->mjc/dot_general | solution.py:33
  668.6 76.0 %all-to-all-done.2 = f32[32,32,2048]{2,0,1:T(8,128)} async-done(((f32[32,32,2048]{2,0,1:T(8,128)}), f32[32,32,2048]{2,0,1:T(8,128)}, u32[]{:S(2)}, u32[]{:S(2)}) %all-to-all-start.2) | async-done | bytes 8388640 | tf_op jit(solution)/shard_map/all_to_all | solution.py:72
  748.8 23.4 %fusion.37 = f32[512,2,2048]{2,0,1:T(8,128)} fusion(f32[512,2,2048]{2,0,1:T(8,128)S(1)} %bitcast.168), kind=kOutput, calls=%fused_computation.70 | convolution fusion | flops 12888571904 | bytes 16777216 | tf_op jit(solution)/shard_map/mn,njc->mjc/dot_general | solution.py:36
  772.2 22.1 %convolution_add_fusion = f32[512,2,2048]{2,0,1:T(8,128)} fusion(f32[512,2,2048]{2,0,1:T(8,128)S(1)} %bitcast.177, f32[512,2,2048]{2,0,1:T(8,128)S(1)} %bitcast.169), kind=kOutput, calls=%fused_computation.18 | convolution fusion | flops 12890669056 | bytes 25165824 | tf_op jit(solution)/shard_map/mn,njc->mjc/dot_general | solution.py:35
  794.3 25.9 %convolution_subtract_fusion = f32[512,2,2048]{2,0,1:T(8,128)} fusion(f32[512,2,2048]{2,0,1:T(8,128)} %fusion.37, f32[512,2,2048]{2,0,1:T(8,128)S(1)} %bitcast.167), kind=kOutput, calls=%fused_computation.17 | convolution fusion | flops 12890669056 | bytes 25165824 | tf_op jit(solution)/shard_map/mn,njc->mjc/dot_general | solution.py:38
  820.2 17.2 %multiply_add_fusion = (f32[512,2,1024]{2,0,1:T(8,128)S(1)}, f32[512,2,1024]{2,0,1:T(8,128)S(1)}, f32[512,2,1024]{2,0,1:T(8,128)S(1)}, f32[512,2,1024]{2,0,1:T(8,128)S(1)}) fusion(f32[512,2,1024]{2,0,1:T(8,128)S(1)} %copy-done.3, f32[512,2,2048]{2,0,1:T(8,128)} %convolution_subtract_fusion, f32[512,2,2048]{2,0,1:T(8,128)} %convolution_add_fusion, ...), kind=kOutput, calls=%fused_computation.6 | convolution fusion | flops 6459752448 | bytes 46137344 | tf_op jit(solution)/shard_map/mn,njc->mjc/dot_general | solution.py:38
  837.4 17.0 %fusion.33 = f32[2,1024,512]{2,1,0:T(8,128)S(1)} fusion(f32[512,2,1024]{2,0,1:T(8,128)S(1)} %get-tuple-element.10), kind=kOutput, calls=%fused_computation.66 | convolution fusion | flops 6446120960 | bytes 8388608 | tf_op jit(solution)/shard_map/nk,kjc->jnc/dot_general | solution.py:49
  854.4 17.2 %fusion.35 = f32[2,1024,512]{2,1,0:T(8,128)S(1)} fusion(f32[512,2,1024]{2,0,1:T(8,128)S(1)} %get-tuple-element.11), kind=kOutput, calls=%fused_computation.68 | convolution fusion | flops 6446120960 | bytes 8388608 | tf_op jit(solution)/shard_map/nk,kjc->jnc/dot_general | solution.py:46
  871.6 17.2 %convolution_add_fusion.3 = f32[2,1024,512]{2,1,0:T(8,128)S(1)} fusion(f32[2,1024,512]{2,1,0:T(8,128)S(1)} %fusion.33, f32[512,2,1024]{2,0,1:T(8,128)S(1)} %get-tuple-element.11), kind=kOutput, calls=%fused_computation.28 | convolution fusion | flops 6447169536 | bytes 12582912 | tf_op jit(solution)/shard_map/nk,kjc->jnc/dot_general | solution.py:51
  888.9 17.2 %fusion.25 = f32[2,1024,512]{2,1,0:T(8,128)S(1)} fusion(f32[512,2,1024]{2,0,1:T(8,128)S(1)} %get-tuple-element.7), kind=kOutput, calls=%fused_computation.58 | convolution fusion | flops 6446120960 | bytes 8388608 | tf_op jit(solution)/shard_map/nk,kjc->jnc/dot_general | solution.py:49
  906.1 17.2 %fusion.27 = f32[2,1024,512]{2,1,0:T(8,128)S(1)} fusion(f32[512,2,1024]{2,0,1:T(8,128)S(1)} %get-tuple-element.6), kind=kOutput, calls=%fused_computation.60 | convolution fusion | flops 6446120960 | bytes 8388608 | tf_op jit(solution)/shard_map/nk,kjc->jnc/dot_general | solution.py:46
  923.2 18.4 %convolution_add_fusion.1 = f32[2,1024,512]{2,1,0:T(8,128)} fusion(f32[2,1024,512]{2,1,0:T(8,128)S(1)} %fusion.25, f32[512,2,1024]{2,0,1:T(8,128)S(1)} %get-tuple-element.6), kind=kOutput, calls=%fused_computation.24 | convolution fusion | flops 6447169536 | bytes 12582912 | tf_op jit(solution)/shard_map/nk,kjc->jnc/dot_general | solution.py:51
  941.6 18.7 %convolution_subtract_fusion.1 = f32[2,1024,512]{2,1,0:T(8,128)} fusion(f32[2,1024,512]{2,1,0:T(8,128)S(1)} %fusion.27, f32[512,2,1024]{2,0,1:T(8,128)S(1)} %get-tuple-element.7), kind=kOutput, calls=%fused_computation.25 | convolution fusion | flops 6447169536 | bytes 12582912 | tf_op jit(solution)/shard_map/nk,kjc->jnc/dot_general | solution.py:48
  960.4 23.9 %add_bitcast_fusion.1 = (f32[2,512,1024]{1,2,0:T(8,128)}, f32[2,512,1024]{1,2,0:T(8,128)}, f32[2,512,1024]{1,2,0:T(8,128)}, f32[2,512,1024]{1,2,0:T(8,128)}) fusion(f32[2,1024,512]{2,1,0:T(8,128)} %convolution_subtract_fusion.1, f32[2,1024,512]{2,1,0:T(8,128)} %convolution_add_fusion.1, f32[2,512]{1,0:T(2,128)S(1)} %get-tuple-element.25, ...), kind=kOutput, calls=%fused_computation.3 | convolution fusion | flops 6459752448 | bytes 37756928 | tf_op jit(solution)/shard_map/nk,kjc->jnc/dot_general | solution.py:48
  984.3 7.3 copy.100
  991.6 36.5 %all-to-all-start.3 = ((f32[2,512,1024]{2,0,1:T(2,128)}), f32[2,512,1024]{2,0,1:T(2,128)}, u32[]{:S(2)}, u32[]{:S(2)}) async-start(f32[2,512,1024]{2,0,1:T(2,128)} %copy.100), calls=%async_computation.3 | async-start | bytes 8388608 | tf_op jit(solution)/shard_map/all_to_all | solution.py:71
  1028.2 7.4 copy.103
  1035.6 70.3 %all-to-all-done.3 = f32[2,512,1024]{2,0,1:T(2,128)} async-done(((f32[2,512,1024]{2,0,1:T(2,128)}), f32[2,512,1024]{2,0,1:T(2,128)}, u32[]{:S(2)}, u32[]{:S(2)}) %all-to-all-start.3) | async-done | bytes 4194336 | tf_op jit(solution)/shard_map/all_to_all | solution.py:71
  1105.8 19.7 %all-to-all-start.4 = ((f32[2,512,1024]{2,0,1:T(2,128)}), f32[2,512,1024]{2,0,1:T(2,128)}, u32[]{:S(2)}, u32[]{:S(2)}) async-start(f32[2,512,1024]{2,0,1:T(2,128)} %copy.103), calls=%async_computation.4 | async-start | bytes 8388608 | tf_op jit(solution)/shard_map/all_to_all | solution.py:72
  1125.5 7.5 copy.118
  1133.0 70.2 %all-to-all-done.4 = f32[2,512,1024]{2,0,1:T(2,128)} async-done(((f32[2,512,1024]{2,0,1:T(2,128)}), f32[2,512,1024]{2,0,1:T(2,128)}, u32[]{:S(2)}, u32[]{:S(2)}) %all-to-all-start.4) | async-done | bytes 4194336 | tf_op jit(solution)/shard_map/all_to_all | solution.py:72
  1203.2 19.7 %all-to-all-start.9 = ((f32[2,512,1024]{2,0,1:T(2,128)}), f32[2,512,1024]{2,0,1:T(2,128)}, u32[]{:S(2)}, u32[]{:S(2)}) async-start(f32[2,512,1024]{2,0,1:T(2,128)} %copy.118), calls=%async_computation.10 | async-start | bytes 8388608 | tf_op jit(solution)/shard_map/all_to_all | solution.py:71
  1222.9 7.4 copy.121
  1230.3 70.3 %all-to-all-done.9 = f32[2,512,1024]{2,0,1:T(2,128)} async-done(((f32[2,512,1024]{2,0,1:T(2,128)}), f32[2,512,1024]{2,0,1:T(2,128)}, u32[]{:S(2)}, u32[]{:S(2)}) %all-to-all-start.9) | async-done | bytes 4194336 | tf_op jit(solution)/shard_map/all_to_all | solution.py:71
  1300.6 19.9 %all-to-all-start.10 = ((f32[2,512,1024]{2,0,1:T(2,128)}), f32[2,512,1024]{2,0,1:T(2,128)}, u32[]{:S(2)}, u32[]{:S(2)}) async-start(f32[2,512,1024]{2,0,1:T(2,128)} %copy.121), calls=%async_computation.11 | async-start | bytes 8388608 | tf_op jit(solution)/shard_map/all_to_all | solution.py:72
  1324.0 5.2 copy.102
  1329.3 6.1 all_to_all.157
  1338.9 5.2 copy.105
  1344.1 6.1 all_to_all.161
  1350.2 4.8 fusion.78
  1360.3 37.9 %all-to-all-done.10 = f32[2,512,1024]{2,0,1:T(2,128)} async-done(((f32[2,512,1024]{2,0,1:T(2,128)}), f32[2,512,1024]{2,0,1:T(2,128)}, u32[]{:S(2)}, u32[]{:S(2)}) %all-to-all-start.10) | async-done | bytes 4194336 | tf_op jit(solution)/shard_map/all_to_all | solution.py:72
  1398.2 19.7 %all-to-all-start.5 = ((f32[32,16,1024]{2,0,1:T(8,128)}), f32[32,16,1024]{2,0,1:T(8,128)}, u32[]{:S(2)}, u32[]{:S(2)}) async-start(f32[32,16,1024]{2,0,1:T(8,128)} %copy.106), calls=%async_computation.5 | async-start | bytes 4194304 | tf_op jit(solution)/shard_map/all_to_all | solution.py:66
  1421.4 5.3 copy.120
  1426.8 6.2 all_to_all.178
  1436.5 5.3 copy.123
  1441.8 6.1 all_to_all.182
  1459.0 58.8 %all_to_all.198 = f32[32,16,1024]{2,0,1:T(8,128)S(1)} all-to-all(f32[32,16,1024]{2,0,1:T(8,128)S(1)} %copy.124), channel_id=1, replica_groups=mesh['seq'=16,'ch'=2] {'seq'}, dimensions={1} | all-to-all | bytes 4194304 | tf_op jit(solution)/shard_map/all_to_all | solution.py:66
  1517.9 4.9 fusion.5
  1527.2 53.9 %reduce-scatter.2.cloned.1.call-done = f32[512,1024]{1,0:T(8,128)} async-done(((f32[512,2048]{1,0:T(8,128)}), f32[512,1024]{1,0:T(8,128)}) %reduce-scatter.2.cloned.1.call-update) | async-done | bytes 2097168 | tf_op jit(solution)/shard_map/reduce_scatter | solution.py:126
  (70 shorter events, 68.9 us)
Async XLA Ops:
  7.2 38.2 %all-gather.2.cloned.1.call-start = ((), (), s32[]{:S(2)}) async-start(), calls=%async_computation.14 | async-start | bytes 3145728 | tf_op jit(solution)/shard_map/all_gather | solution.py:130
  7.9 44.0 %copy-start.8 = (bf16[512,1024]{1,0:T(8,128)(2,1)S(1)}, bf16[512,1024]{1,0:T(8,128)(2,1)}, u32[]{:S(2)}) copy-start(bf16[512,1024]{1,0:T(8,128)(2,1)} %param.7) | copy-start | bytes 3145732
  50.6 1.3 copy-start.6
  55.7 46.7 %all-to-all-start.6 = ((f32[1,512,1024]{2,0,1:T(1,128)}), f32[1,512,1024]{2,0,1:T(1,128)S(1)}, u32[]{:S(2)}, u32[]{:S(2)}) async-start(f32[1,512,1024]{2,0,1:T(1,128)} %copy.107), calls=%async_computation.7 | async-start | bytes 4194304 | tf_op jit(solution)/shard_map/all_to_all | solution.py:66
  61.4 2.2 copy-start.12
  102.5 89.4 %all-to-all-start = ((f32[1,512,2048]{2,0,1:T(1,128)}), f32[1,512,2048]{2,0,1:T(1,128)}, u32[]{:S(2)}, u32[]{:S(2)}) async-start(f32[1,512,2048]{2,0,1:T(1,128)} %copy.89), calls=%async_computation | async-start | bytes 8388608 | tf_op jit(solution)/shard_map/all_to_all | solution.py:66
  191.9 97.4 %all-to-all-start.7 = ((f32[32,32,1024]{2,0,1:T(8,128)}), f32[32,32,1024]{2,0,1:T(8,128)}, u32[]{:S(2)}, u32[]{:S(2)}) async-start(f32[32,32,1024]{2,0,1:T(8,128)} %copy.110), calls=%async_computation.8 | async-start | bytes 8388608 | tf_op jit(solution)/shard_map/all_to_all | solution.py:71
  289.2 97.5 %all-to-all-start.8 = ((f32[32,32,1024]{2,0,1:T(8,128)}), f32[32,32,1024]{2,0,1:T(8,128)}, u32[]{:S(2)}, u32[]{:S(2)}) async-start(f32[32,32,1024]{2,0,1:T(8,128)} %copy.112), calls=%async_computation.9 | async-start | bytes 8388608 | tf_op jit(solution)/shard_map/all_to_all | solution.py:72
  386.8 170.4 %all-to-all-start.1 = ((f32[32,32,2048]{2,0,1:T(8,128)}), f32[32,32,2048]{2,0,1:T(8,128)}, u32[]{:S(2)}, u32[]{:S(2)}) async-start(f32[32,32,2048]{2,0,1:T(8,128)} %copy.92), calls=%async_computation.1 | async-start | bytes 16777216 | tf_op jit(solution)/shard_map/all_to_all | solution.py:71
  557.2 187.4 %all-to-all-start.2 = ((f32[32,32,2048]{2,0,1:T(8,128)}), f32[32,32,2048]{2,0,1:T(8,128)}, u32[]{:S(2)}, u32[]{:S(2)}) async-start(f32[32,32,2048]{2,0,1:T(8,128)} %copy.94), calls=%async_computation.2 | async-start | bytes 16777216 | tf_op jit(solution)/shard_map/all_to_all | solution.py:72
  596.6 4.0 copy-start.1
  642.1 3.3 copy-start
  744.6 27.6 %slice-start.2 = ((s8[8388608]{0:T(1024)(128)(4,1)}), s8[4194304]{0:T(1024)(128)(4,1)S(1)}, s32[]{:S(2)}) async-start(s8[8388608]{0:T(1024)(128)(4,1)} %bitcast.176), calls=%async_computation.17 | async-start | bytes 8388608
  748.7 23.4 %slice-start.3 = ((s8[8388608]{0:T(1024)(128)(4,1)}), s8[4194304]{0:T(1024)(128)(4,1)S(1)}, s32[]{:S(2)}) async-start(s8[8388608]{0:T(1024)(128)(4,1)} %bitcast.176), calls=%async_computation.18 | async-start | bytes 8388608
  748.7 45.6 %slice-start = ((s8[8388608]{0:T(1024)(128)(4,1)}), s8[4194304]{0:T(1024)(128)(4,1)S(1)}, s32[]{:S(2)}) async-start(s8[8388608]{0:T(1024)(128)(4,1)} %bitcast.165), calls=%async_computation.15 | async-start | bytes 8388608
  772.2 22.1 %slice-start.1 = ((s8[8388608]{0:T(1024)(128)(4,1)}), s8[4194304]{0:T(1024)(128)(4,1)S(1)}, s32[]{:S(2)}) async-start(s8[8388608]{0:T(1024)(128)(4,1)} %bitcast.165), calls=%async_computation.16 | async-start | bytes 8388608
  794.3 25.9 %copy-start.2 = (f32[32,16,2,1024]{3,0,1,2:T(8,128)S(1)}, f32[32,16,2,1024]{3,0,1,2:T(8,128)}, u32[]{:S(2)}) copy-start(f32[32,16,2,1024]{3,0,1,2:T(8,128)} %copy-done.1) | copy-start | bytes 12582916
  794.3 25.9 %copy-start.3 = (f32[512,2,1024]{2,0,1:T(8,128)S(1)}, f32[512,2,1024]{2,0,1:T(8,128)}, u32[]{:S(2)}) copy-start(f32[512,2,1024]{2,0,1:T(8,128)} %convolution_add_fusion.2) | copy-start | bytes 12582916
  991.6 114.2 %all-to-all-start.3 = ((f32[2,512,1024]{2,0,1:T(2,128)}), f32[2,512,1024]{2,0,1:T(2,128)}, u32[]{:S(2)}, u32[]{:S(2)}) async-start(f32[2,512,1024]{2,0,1:T(2,128)} %copy.100), calls=%async_computation.3 | async-start | bytes 8388608 | tf_op jit(solution)/shard_map/all_to_all | solution.py:71
  1105.8 97.4 %all-to-all-start.4 = ((f32[2,512,1024]{2,0,1:T(2,128)}), f32[2,512,1024]{2,0,1:T(2,128)}, u32[]{:S(2)}, u32[]{:S(2)}) async-start(f32[2,512,1024]{2,0,1:T(2,128)} %copy.103), calls=%async_computation.4 | async-start | bytes 8388608 | tf_op jit(solution)/shard_map/all_to_all | solution.py:72
  1203.2 97.4 %all-to-all-start.9 = ((f32[2,512,1024]{2,0,1:T(2,128)}), f32[2,512,1024]{2,0,1:T(2,128)}, u32[]{:S(2)}, u32[]{:S(2)}) async-start(f32[2,512,1024]{2,0,1:T(2,128)} %copy.118), calls=%async_computation.10 | async-start | bytes 8388608 | tf_op jit(solution)/shard_map/all_to_all | solution.py:71
  1300.6 97.6 %all-to-all-start.10 = ((f32[2,512,1024]{2,0,1:T(2,128)}), f32[2,512,1024]{2,0,1:T(2,128)}, u32[]{:S(2)}, u32[]{:S(2)}) async-start(f32[2,512,1024]{2,0,1:T(2,128)} %copy.121), calls=%async_computation.11 | async-start | bytes 8388608 | tf_op jit(solution)/shard_map/all_to_all | solution.py:72
  1350.2 4.9 copy-start.4
  1398.2 60.9 %all-to-all-start.5 = ((f32[32,16,1024]{2,0,1:T(8,128)}), f32[32,16,1024]{2,0,1:T(8,128)}, u32[]{:S(2)}, u32[]{:S(2)}) async-start(f32[32,16,1024]{2,0,1:T(8,128)} %copy.106), calls=%async_computation.5 | async-start | bytes 4194304 | tf_op jit(solution)/shard_map/all_to_all | solution.py:66
  1417.9 163.3 %reduce-scatter.2.cloned.1.call-start = ((), (), s32[]{:S(2)}) async-start(), calls=%async_computation.13 | async-start | bytes 6291456 | tf_op jit(solution)/shard_map/reduce_scatter | solution.py:126
  1447.9 4.4 copy-start.5
  1455.1 62.7 %copy-start.9 = (bf16[512,1024]{1,0:T(8,128)(2,1)S(1)}, bf16[512,1024]{1,0:T(8,128)(2,1)}, u32[]{:S(2)}) copy-start(bf16[512,1024]{1,0:T(8,128)(2,1)} %param.7) | copy-start | bytes 3145732
  1455.1 62.7 %copy-start.13 = (f32[1024]{0:T(1024)S(1)}, f32[1024]{0:T(1024)}, u32[]{:S(2)}) copy-start(f32[1024]{0:T(1024)} %param.11) | copy-start | bytes 12292
  1459.0 58.8 %copy-start.7 = (f32[512,1024]{1,0:T(8,128)S(1)}, f32[512,1024]{1,0:T(8,128)}, u32[]{:S(2)}) copy-start(f32[512,1024]{1,0:T(8,128)} %copy-done.6) | copy-start | bytes 6291460
  1459.0 58.8 %copy-start.10 = (bf16[512,1024]{1,0:T(8,128)(2,1)S(1)}, bf16[512,1024]{1,0:T(8,128)(2,1)}, u32[]{:S(2)}) copy-start(bf16[512,1024]{1,0:T(8,128)(2,1)} %param.8) | copy-start | bytes 3145732
  1459.0 58.8 %copy-start.11 = (bf16[512,1024]{1,0:T(8,128)(2,1)S(1)}, bf16[512,1024]{1,0:T(8,128)(2,1)}, u32[]{:S(2)}) copy-start(bf16[512,1024]{1,0:T(8,128)(2,1)} %param.9) | copy-start | bytes 3145732
  1517.8 5.0 copy-start.14
Sparse Core Ops, SparseCore 0:
  9.5 35.8 all-gather.1
  1527.3 53.7 reduce-scatter.1
where the time goes:
time: 1600 us; the launch traced here: 1590 us
  waiting for transfers between devices  757 us (47%)
  matrix products  363 us (23%)
  starting transfers between devices  229 us (14%)
  local copies, waits for them, and re-layouts  158 us (10%)
  blocking collectives  58.8 us (4%)
    all_to_all x4, waiting for transfers between devices, regroup_pair(): lax.all_to_all(real_part, 'seq', split_axis=1, concat_axis=0, tiled=True)  351 us
    all_to_all x4, waiting for transfers between devices, regroup_pair(): lax.all_to_all(imag_part, 'seq', split_axis=1, concat_axis=0, tiled=True)  221 us
    all_to_all x4, starting transfers between devices, regroup_pair(): lax.all_to_all(imag_part, 'seq', split_axis=1, concat_axis=0, tiled=True)  96.2 us
    all_to_all x4, starting transfers between devices, regroup_pair(): lax.all_to_all(real_part, 'seq', split_axis=1, concat_axis=0, tiled=True)  95.6 us
    all_to_all x3, waiting for transfers between devices, regroup_real(): lax.all_to_all(values, 'seq', split_axis=1, concat_axis=0, tiled=True)  92.8 us
    all_to_all x1, blocking collectives, regroup_real(): lax.all_to_all(values, 'seq', split_axis=1, concat_axis=0, tiled=True)  58.8 us
    reduce_scatter x1, waiting for transfers between devices, on_device(): lax.psum_scatter(out_terms, 'ch', scatter_dimension=1, tiled=True)  53.9 us
    dot_general x2, matrix products, forward_spectrum(): jnp.einsum('mn,njc->mjc', sin_long, moved_real, precision=FULL_PRECISION)  43.1 us
  transfers between devices with their start and end apart: 13, of which 13 were waited for; matrix products, arithmetic and copies ran while one was open for 15% of the time, Pallas kernels for 0%

commit v1 on v0

v1 whole, which is shorter than its diff:
```python
import functools
import math

import jax
import jax.numpy as jnp
import ml_dtypes
import numpy as np
from jax import lax
from jax.experimental import pallas as pl
from jax.experimental.pallas import tpu as pltpu
from jax.sharding import PartitionSpec as P

F32 = jnp.float32
BF16 = jnp.bfloat16
LANES = 128
HALF = 64
FULL_PRECISION = lax.Precision.HIGHEST


def split_high_low(table):
    high = table.astype(ml_dtypes.bfloat16)
    low = (table - high.astype(np.float64)).astype(ml_dtypes.bfloat16)
    return high, low


def slow_positions(devices, tokens_each):
    per_half = tokens_each // 2 // LANES
    half, device, piece = np.meshgrid(
        np.arange(2), np.arange(devices), np.arange(per_half), indexing="ij"
    )
    return (device * 2 * per_half + half * per_half + piece).reshape(-1)


def transform_tables(devices, tokens_each):
    length = devices * tokens_each
    rows = length // LANES
    slow = slow_positions(devices, tokens_each)
    k1 = np.arange(rows)
    n2 = np.arange(LANES)
    turns = (4 * k1[None, :, None] + 1) * (LANES * slow[None, None, :] + n2[:, None, None])
    angle = (turns % (4 * length)) * (2.0 * math.pi / (4 * length))
    cosine, sine = np.cos(angle), np.sin(angle)
    enter = np.concatenate([cosine, -sine], axis=1)
    enter_high, enter_low = split_high_low(enter)
    enter_table = np.concatenate([enter_high, enter_low], axis=2)
    pairs = rows // 2
    leave = np.stack([cosine, -sine], axis=1).reshape(LANES, 2, 2, pairs, rows)
    leave = leave.transpose(0, 4, 2, 1, 3).reshape(LANES, rows, 2 * rows) / length
    leave_high, leave_low = split_high_low(leave)
    leave_table = np.concatenate([leave_high, leave_low], axis=2)
    small = (n2[:, None] * n2[None, :] % LANES) * (2.0 * math.pi / LANES)
    c, s = np.cos(small), np.sin(small)
    forth_high, forth_low = split_high_low(np.block([[c, s], [-s, c]]))
    back_high, back_low = split_high_low(np.block([[c, -s], [s, c]]))
    forth_table = np.concatenate([forth_high, forth_low, forth_high], axis=1)
    back_table = np.concatenate([back_high, back_low, back_high], axis=1)
    return enter_table, forth_table, back_table, leave_table


def low_lanes(rows):
    return lax.broadcasted_iota(jnp.int32, (rows, LANES), 1) < HALF


def swap_lanes(values):
    return pltpu.roll(values, HALF, 1)


def split_float(values):
    high = values.astype(BF16)
    return high, (values - high.astype(F32)).astype(BF16)


def mxu(left, right):
    return jnp.dot(left, right, preferred_element_type=F32)


def convolve_kernel(
    adjoint,
    signal_ref,
    taps_ref,
    enter_ref,
    forth_ref,
    back_ref,
    leave_ref,
    out_ref,
    signal_wide,
    taps_wide,
    entered,
    returned,
    out_wide,
):
    steps = signal_ref.shape[0] // LANES
    rows = 2 * steps
    signal_wide[...] = signal_ref[...].astype(F32)
    taps_wide[...] = taps_ref[...].astype(F32)
    low_steps = low_lanes(steps)

    def enter(n2):
        signal = signal_wide[pl.ds(n2, steps, stride=LANES), :]
        taps = taps_wide[pl.ds(n2, steps, stride=LANES), :]
        first = jnp.where(low_steps, signal, swap_lanes(taps))
        second = jnp.where(low_steps, swap_lanes(signal), taps)
        both = jnp.concatenate([first, second], axis=0).astype(BF16)
        place = pl.multiple_of(n2 * 2 * rows, 2 * rows)
        entered[pl.ds(place, 2 * rows), :] = mxu(
            enter_ref[n2], jnp.concatenate([both, both], axis=0)
        )

    def enter_group(group, _):
        for member in range(4):
            enter(group * 4 + member)
        return 0

    lax.fori_loop(0, LANES // 4, enter_group, 0)
    low = low_lanes(LANES)

    def column(k1):
        real = entered[pl.ds(k1, LANES, stride=2 * rows), :]
        imag = entered[pl.ds(rows + k1, LANES, stride=2 * rows), :]
        return jnp.concatenate([real, imag], axis=0)

    def middle(pair):
        data = jnp.concatenate([column(pair), column(pair + steps)], axis=1)
        high, rest = split_float(data)
        spectrum = mxu(forth_ref[...], jnp.concatenate([high, high, rest], axis=0))
        real_a, real_b = spectrum[:LANES, :LANES], spectrum[:LANES, LANES:]
        imag_a, imag_b = spectrum[LANES:, :LANES], spectrum[LANES:, LANES:]
        signal_real = jnp.where(low, real_a, swap_lanes(real_b))
        signal_imag = jnp.where(low, imag_a, swap_lanes(imag_b))
        taps_real = jnp.where(low, swap_lanes(real_a), real_b)
        taps_imag = jnp.where(low, swap_lanes(imag_a), imag_b)
        if adjoint:
            real = taps_real * signal_real + taps_imag * signal_imag
            imag = taps_real * signal_imag - taps_imag * signal_real
        else:
            real = taps_real * signal_real - taps_imag * signal_imag
            imag = taps_real * signal_imag + taps_imag * signal_real
        high, rest = split_float(jnp.concatenate([real, imag], axis=0))
        place = pl.multiple_of(pair * 2 * LANES, 2 * LANES)
        returned[pl.ds(place, 2 * LANES), :] = mxu(
            back_ref[...], jnp.concatenate([high, high, rest], axis=0)
        )

    def middle_group(group, _):
        for member in range(2):
            middle(group * 2 + member)
        return 0

    lax.fori_loop(0, steps // 2, middle_group, 0)
    low_rows = low_lanes(rows)

    def leave(n2):
        real = returned[pl.ds(n2, steps, stride=2 * LANES), :]
        imag = returned[pl.ds(LANES + n2, steps, stride=2 * LANES), :]
        both = jnp.concatenate([real, imag], axis=0)
        turned = swap_lanes(both)
        data = jnp.concatenate(
            [jnp.where(low_rows, both, turned), jnp.where(low_rows, turned, both)], axis=0
        )
        high, rest = split_float(data)
        table = leave_ref[n2]
        result = mxu(table, jnp.concatenate([high, high], axis=0)) + mxu(
            table[:, : 2 * rows], rest
        )
        out_wide[pl.ds(n2, steps, stride=LANES), :] = jnp.where(
            low_steps, result[:steps], result[steps:]
        )

    def leave_group(group, _):
        for member in range(4):
            leave(group * 4 + member)
        return 0

    lax.fori_loop(0, LANES // 4, leave_group, 0)
    out_ref[...] = out_wide[...].astype(BF16)


def convolve(signal, taps, tables, adjoint):
    devices, places, lanes = signal.shape
    count = devices * places
    rows = 2 * (count // LANES)
    vmem = pl.BlockSpec(memory_space=pltpu.VMEM)
    result = pl.pallas_call(
        functools.partial(convolve_kernel, adjoint),
        out_shape=jax.ShapeDtypeStruct((count, lanes), BF16),
        in_specs=[vmem] * 6,
        out_specs=vmem,
        scratch_shapes=[
            pltpu.VMEM((count, lanes), F32),
            pltpu.VMEM((count, lanes), F32),
            pltpu.VMEM((LANES * 2 * rows, lanes), F32),
            pltpu.VMEM((rows * LANES, lanes), F32),
            pltpu.VMEM((count, lanes), F32),
        ],
        compiler_params=pltpu.CompilerParams(vmem_limit_bytes=56 * 1024 * 1024),
        cost_estimate=pl.CostEstimate(
            flops=6 * 2 * 2 * LANES * 2 * LANES * rows * LANES,
            bytes_accessed=12 * 1024 * 1024,
            transcendentals=0,
        ),
        name="convolve_adjoint" if adjoint else "convolve",
    )(signal.reshape(count, lanes), taps.reshape(count, lanes), *tables)
    return result.reshape(devices, places, lanes)


def pack_block(values):
    places = values.shape[0] // 2
    first, second = values[:places], values[places:]
    low = low_lanes(places)
    return (
        jnp.where(low, first, swap_lanes(second)),
        jnp.where(low, swap_lanes(first), second),
    )


def unpack_block(message_ref):
    first, second = message_ref[0].astype(F32), message_ref[1].astype(F32)
    low = low_lanes(first.shape[0])
    return jnp.concatenate(
        [
            jnp.where(low, first, swap_lanes(second)),
            jnp.where(low, swap_lanes(first), second),
        ],
        axis=0,
    )


def pack_into(message_ref, values):
    first, second = pack_block(values)
    message_ref[0] = first.astype(BF16)
    message_ref[1] = second.astype(BF16)


def mix_kernel(key_ref, value_ref, mixed_ref):
    pack_into(mixed_ref, key_ref[...].astype(F32) * value_ref[...].astype(F32))


def taps_kernel(taps_ref, message_ref):
    pack_into(message_ref, taps_ref[...])


def grad_kernel(gated_ref, query_ref, message_ref):
    pack_into(message_ref, gated_ref[...] * query_ref[...].astype(F32))


def gate_kernel(
    message_ref, key_ref, value_ref, query_ref, skip_ref, grad_ref, gated_ref, query_grad_ref
):
    mixed = key_ref[...].astype(F32) * value_ref[...].astype(F32)
    conv_out = unpack_block(message_ref) + skip_ref[...] * mixed
    gated_ref[...] = (query_ref[...].astype(F32) * conv_out).astype(BF16)
    query_grad_ref[...] = (grad_ref[...] * conv_out).astype(BF16)


def input_grad_kernel(
    message_ref, key_ref, value_ref, query_ref, skip_ref, grad_ref, key_grad_ref, value_grad_ref
):
    grad_conv = grad_ref[...] * query_ref[...].astype(F32)
    grad_mixed = unpack_block(message_ref) + skip_ref[...] * grad_conv
    key_grad_ref[...] = (grad_mixed * value_ref[...].astype(F32)).astype(BF16)
    value_grad_ref[...] = (grad_mixed * key_ref[...].astype(F32)).astype(BF16)


def by_blocks(kernel, shape, inputs, out_kinds):
    tokens, channels = shape
    plain = pl.BlockSpec((tokens, LANES), lambda j: (0, j))
    message = pl.BlockSpec((2, tokens // 2, LANES), lambda j: (j, 0, 0))
    vector = pl.BlockSpec((1, LANES), lambda j: (0, j))

    def spec_of(array):
        if len(array.shape) == 3:
            return message
        return vector if array.shape[0] == 1 else plain

    outs = []
    for kind in out_kinds:
        if kind == "message":
            outs.append(
                jax.ShapeDtypeStruct((2 * channels // LANES, tokens // 2, LANES), BF16)
            )
        else:
            outs.append(jax.ShapeDtypeStruct((tokens, channels), BF16))
    moved = sum(a.size * a.dtype.itemsize for a in list(inputs) + outs)
    return pl.pallas_call(
        kernel,
        grid=(channels // LANES,),
        out_shape=outs,
        in_specs=[spec_of(a) for a in inputs],
        out_specs=[spec_of(a) for a in outs],
        cost_estimate=pl.CostEstimate(
            flops=4 * tokens * channels, bytes_accessed=moved, transcendentals=0
        ),
        compiler_params=pltpu.CompilerParams(vmem_limit_bytes=32 * 1024 * 1024),
    )(*inputs)


def exchange(values):
    return lax.all_to_all(values, "seq", split_axis=0, concat_axis=0, tiled=True)


def swap_pair(values):
    return lax.ppermute(values, "ch", [(0, 1), (1, 0)])


def on_device(query_in, key_in, value_in, filter_taps, skip_gain, out_weight, out_grad):
    devices = lax.axis_size("seq")
    shape = key_in.shape
    tokens, channels = shape
    tables = [jnp.asarray(table) for table in transform_tables(devices, tokens)]
    skip_row = skip_gain.reshape(1, channels)
    mine = lax.axis_index("ch")
    weight_blocks = out_weight.reshape(channels, 2, channels)
    weight_mine = lax.dynamic_index_in_dim(weight_blocks, mine, axis=1, keepdims=False)
    weight_other = lax.dynamic_index_in_dim(weight_blocks, 1 - mine, axis=1, keepdims=False)

    (mixed_sent,) = by_blocks(mix_kernel, shape, [key_in, value_in], ["message"])
    mixed_held = exchange(mixed_sent)
    (taps_sent,) = by_blocks(taps_kernel, shape, [filter_taps], ["message"])
    taps_held = exchange(taps_sent)

    grad_other = swap_pair(out_grad)
    weight_crossed = swap_pair(weight_other)
    over_columns = (((1,), (1,)), ((), ()))
    grad_gated = lax.dot_general(
        out_grad, weight_mine, over_columns, preferred_element_type=F32
    ) + lax.dot_general(grad_other, weight_other, over_columns, preferred_element_type=F32)
    (grad_sent,) = by_blocks(grad_kernel, shape, [grad_gated, query_in], ["message"])
    grad_held = exchange(grad_sent)

    conv_held = convolve(mixed_held, taps_held, tables, False)
    conv_back = exchange(conv_held)
    grad_mixed_held = convolve(grad_held, taps_held, tables, True)
    grad_mixed_back = exchange(grad_mixed_held)

    gated_out, query_grad = by_blocks(
        gate_kernel,
        shape,
        [conv_back, key_in, value_in, query_in, skip_row, grad_gated],
        ["plain", "plain"],
    )
    gated_other = swap_pair(gated_out)
    mixed_out = (
        jnp.dot(gated_out, weight_mine, preferred_element_type=F32)
        + jnp.dot(gated_other, weight_crossed, preferred_element_type=F32)
    ).astype(BF16)
    key_grad, value_grad = by_blocks(
        input_grad_kernel,
        shape,
        [grad_mixed_back, key_in, value_in, query_in, skip_row, grad_gated],
        ["plain", "plain"],
    )
    return (mixed_out, query_grad, key_grad, value_grad)


def phases(row_ids, col_ids, modulus):
    angles = (row_ids[:, None] * col_ids[None, :] % modulus).astype(F32) * (
        2.0 * math.pi / modulus
    )
    return jnp.cos(angles), jnp.sin(angles)


def einsum(form, left, right):
    return jnp.einsum(form, left, right, precision=FULL_PRECISION)


def plain_tables(rows):
    k1 = jnp.arange(rows, dtype=jnp.int32)
    n2 = jnp.arange(LANES, dtype=jnp.int32)
    return (
        phases(4 * k1 + 1, k1, 4 * rows),
        phases(4 * k1 + 1, n2, 4 * rows * LANES),
        phases(n2, n2, LANES),
    )


def plain_spectrum(signal, tables):
    (slow_cos, slow_sin), (turn_cos, turn_sin), (fast_cos, fast_sin) = tables
    real = einsum("kn,njc->kjc", slow_cos, signal)
    imag = -einsum("kn,njc->kjc", slow_sin, signal)
    turn_cos, turn_sin = turn_cos[:, :, None], turn_sin[:, :, None]
    real, imag = real * turn_cos + imag * turn_sin, imag * turn_cos - real * turn_sin
    return (
        einsum("mj,kjc->kmc", fast_cos, real) + einsum("mj,kjc->kmc", fast_sin, imag),
        einsum("mj,kjc->kmc", fast_cos, imag) - einsum("mj,kjc->kmc", fast_sin, real),
    )


def plain_signal(spectrum, tables):
    (slow_cos, slow_sin), (turn_cos, turn_sin), (fast_cos, fast_sin) = tables
    real, imag = spectrum
    real, imag = (
        einsum("jm,kmc->kjc", fast_cos, real) - einsum("jm,kmc->kjc", fast_sin, imag),
        einsum("jm,kmc->kjc", fast_cos, imag) + einsum("jm,kmc->kjc", fast_sin, real),
    )
    turn_cos, turn_sin = turn_cos[:, :, None], turn_sin[:, :, None]
    real, imag = real * turn_cos - imag * turn_sin, imag * turn_cos + real * turn_sin
    result = einsum("kn,kjc->njc", slow_cos, real) - einsum("kn,kjc->njc", slow_sin, imag)
    return result * (1.0 / (slow_cos.shape[0] * LANES))


def on_any_device(query_in, key_in, value_in, filter_taps, skip_gain, out_weight, out_grad):
    tokens, channels = key_in.shape
    rows = lax.axis_size("seq") * tokens // LANES
    tables = plain_tables(rows)

    def to_channels(values):
        held = lax.all_to_all(values, "seq", split_axis=1, concat_axis=0, tiled=True)
        return plain_spectrum(held.reshape(rows, LANES, held.shape[1]), tables)

    def to_tokens(spectrum):
        held = plain_signal(spectrum, tables)
        held = held.reshape(rows * LANES, held.shape[2])
        return lax.all_to_all(held, "seq", split_axis=0, concat_axis=1, tiled=True)

    query = query_in.astype(F32)
    mixed = key_in.astype(F32) * value_in.astype(F32)
    mixed_real, mixed_imag = to_channels(mixed)
    taps_real, taps_imag = to_channels(filter_taps)
    conv_out = skip_gain * mixed + to_tokens(
        (
            mixed_real * taps_real - mixed_imag * taps_imag,
            mixed_real * taps_imag + mixed_imag * taps_real,
        )
    )
    gated_out = (query * conv_out).astype(BF16)
    out_terms = jnp.dot(gated_out, out_weight, preferred_element_type=F32)
    mixed_out = lax.psum_scatter(out_terms, "ch", scatter_dimension=1, tiled=True).astype(BF16)
    grad_gated = lax.dot_general(
        lax.all_gather(out_grad, "ch", axis=1, tiled=True),
        out_weight,
        (((1,), (1,)), ((), ())),
        preferred_element_type=F32,
    )
    query_grad = (grad_gated * conv_out).astype(BF16)
    grad_conv = grad_gated * query
    grad_real, grad_imag = to_channels(grad_conv)
    grad_mixed = skip_gain * grad_conv + to_tokens(
        (
            taps_real * grad_real + taps_imag * grad_imag,
            taps_real * grad_imag - taps_imag * grad_real,
        )
    )
    key_grad = (grad_mixed * value_in.astype(F32)).astype(BF16)
    value_grad = (grad_mixed * key_in.astype(F32)).astype(BF16)
    return (mixed_out, query_grad, key_grad, value_grad)


def solution(mesh):
    spread = P("seq", "ch")
    placed = (spread, spread, spread, spread, P("ch"), P("ch", None), spread)

    def body(*arguments):
        tokens, channels = arguments[1].shape
        fits = (
            lax.axis_size("ch") == 2
            and channels == HALF * lax.axis_size("seq")
            and tokens % (2 * LANES) == 0
        )
        return (on_device if fits else on_any_device)(*arguments)

    return jax.shard_map(
        body, mesh=mesh, in_specs=placed, out_specs=(spread,) * 4, check_vma=False
    )
```

time: 1600 us -> 247 us (0.15)
  waiting for transfers between devices: 757 us -> 46.1 us
  matrix products: 363 us -> 11.8 us
  starting transfers between devices: 229 us -> 35.8 us
  local copies, waits for them, and re-layouts: 158 us -> 21.6 us
  Pallas kernels: 0 us -> 130 us
  blocking collectives: 58.8 us -> 0 us
    all_to_all x11 -> x5, waiting for transfers between devices: 665 us -> 29.5 us  [exchange(): lax.all_to_all(values, 'seq', split_axis=0, concat_axis=0, tiled=True)]
    dot_general x26 -> x4, matrix products: 363 us -> 11.8 us  [the longest x1 4.14 us: on_device(): jnp.dot(gated_other, weight_crossed, preferred_element_type=F32)]
    all_to_all x11 -> x5, starting transfers between devices: 229 us -> 32.2 us  [exchange(): lax.all_to_all(values, 'seq', split_axis=0, concat_axis=0, tiled=True)]
    pallas_call x0 -> x7, Pallas kernels: none -> 130 us  [the longest x2 107 us: convolve(): pl.pallas_call(functools.partial(convolve_kernel, adjoint), out_shape=jax...]
    all_to_all x16 -> x0, local copies, waits for them, and re-layouts: 74.3 us -> none  [the longest x8 37.9 us: regroup_pair(): lax.all_to_all(imag_part, 'seq', split_axis=1, concat_axis=0, tiled=True)]
    all_to_all x1 -> x0, blocking collectives: 58.8 us -> none  [regroup_real(): lax.all_to_all(values, 'seq', split_axis=1, concat_axis=0, tiled=True)]
    reduce_scatter x1 -> x0, waiting for transfers between devices: 53.9 us -> none  [on_device(): lax.psum_scatter(out_terms, 'ch', scatter_dimension=1, tiled=True)]
    all_gather x1 -> x0, waiting for transfers between devices: 37.5 us -> none  [on_device(): lax.all_gather(out_grad, 'ch', axis=1, tiled=True)]
  transfers between devices with their start and end apart: 13 -> 8, of which waited for: 13 -> 4; matrix products, arithmetic and copies ran while one was open for 15% -> 8% of each run, Pallas kernels for 0% -> 51%
where the time goes in v1:
time: 247 us; the launch traced here: 246 us
  Pallas kernels  130 us (53%)
  waiting for transfers between devices  46.1 us (19%)
  starting transfers between devices  35.8 us (14%)
  local copies, waits for them, and re-layouts  21.6 us (9%)
  matrix products  11.8 us (5%)
    pallas_call x2, Pallas kernels, convolve(): pl.pallas_call(functools.partial(convolve_kernel, adjoint), out_shape=jax...  107 us
    all_to_all x5, starting transfers between devices, exchange(): lax.all_to_all(values, 'seq', split_axis=0, concat_axis=0, tiled=True)  32.2 us
    all_to_all x5, waiting for transfers between devices, exchange(): lax.all_to_all(values, 'seq', split_axis=0, concat_axis=0, tiled=True)  29.5 us
    pallas_call x5, Pallas kernels, by_blocks(): pl.pallas_call(kernel, grid=(channels // LANES,), out_shape=outs, in_spec...  22.7 us
    ppermute x3, waiting for transfers between devices, swap_pair(): return lax.ppermute(values, 'ch', [(0, 1), (1, 0)])  16.6 us
    unnamed x35, local copies, waits for them, and re-layouts  15.7 us
    dynamic_slice x2, local copies, waits for them, and re-layouts, on_device(): lax.dynamic_index_in_dim(weight_blocks, 1 - mine, axis=1, keepdims=False)  5.87 us
  transfers between devices with their start and end apart: 8, of which 4 were waited for; matrix products, arithmetic and copies ran while one was open for 8% of the time, Pallas kernels for 51%

profile of v1, /device:TPU:0, one launch (start us, length us, event | category | flops | bytes accessed | tf_op | source)
XLA Modules:
  0.0 245.7 jit_solution(2071028755609173839)
XLA Ops:
  0.6 0.0 copy-start
  0.6 1.2 copy-done
  1.9 0.0 copy-start.2
  1.9 1.2 copy-done.2
  3.1 0.0 copy-start.8
  3.1 3.5 %shard_map.138 = bf16[16,256,128]{2,1,0:T(8,128)(2,1)} custom-call(bf16[512,1024]{1,0:T(8,128)(2,1)S(1)} %copy-done, bf16[512,1024]{1,0:T(8,128)(2,1)S(1)} %copy-done.2), custom_call_target="tpu_custom_call" | custom-call | flops 2097152 | bytes 3145728 | tf_op jit(solution)/shard_map/pallas_call | solution.py:284
  6.6 7.4 %all-to-all-start = ((bf16[16,256,128]{2,1,0:T(8,128)(2,1)}), bf16[16,256,128]{2,1,0:T(8,128)(2,1)S(1)}, u32[]{:S(2)}, u32[]{:S(2)}) async-start(bf16[16,256,128]{2,1,0:T(8,128)(2,1)} %shard_map.138), calls=%async_computation | async-start | bytes 2097152 | tf_op jit(solution)/shard_map/all_to_all | solution.py:298
  14.0 0.0 copy-done.8
  14.0 3.4 %shard_map.139 = bf16[16,256,128]{2,1,0:T(8,128)(2,1)} custom-call(f32[512,1024]{1,0:T(8,128)S(1)} %copy-done.8), custom_call_target="tpu_custom_call" | custom-call | flops 2097152 | bytes 3145728 | tf_op jit(solution)/shard_map/pallas_call | solution.py:284
  17.4 19.6 %all-to-all-done = bf16[16,256,128]{2,1,0:T(8,128)(2,1)S(1)} async-done(((bf16[16,256,128]{2,1,0:T(8,128)(2,1)}), bf16[16,256,128]{2,1,0:T(8,128)(2,1)S(1)}, u32[]{:S(2)}, u32[]{:S(2)}) %all-to-all-start) | async-done | bytes 1048608 | tf_op jit(solution)/shard_map/all_to_all | solution.py:298
  36.9 0.0 copy-start.14
  36.9 1.0 copy-done.14
  37.9 6.9 %all-to-all-start.1 = ((bf16[16,256,128]{2,1,0:T(8,128)(2,1)}), bf16[16,256,128]{2,1,0:T(8,128)(2,1)S(1)}, u32[]{:S(2)}, u32[]{:S(2)}) async-start(bf16[16,256,128]{2,1,0:T(8,128)(2,1)} %shard_map.139), calls=%async_computation.1 | async-start | bytes 2097152 | tf_op jit(solution)/shard_map/all_to_all | solution.py:298
  44.8 1.6 collective-permute-start
  46.4 0.0 copy-start.15
  46.4 6.5 %copy.19 = bf16[1024,2048]{0,1:T(8,128)(2,1)} copy(bf16[1024,2048]{1,0:T(8,128)(2,1)} %param.16) | data formatting | bytes 8388608 | tf_op args[5]
  52.8 0.0 copy-start.10
  52.8 1.9 constant_dynamic-slice_fusion
  54.8 0.0 copy-done.15
  54.8 0.9 copy-done.10
  55.7 0.0 copy-start.12
  55.7 1.3 fusion.4
  56.9 0.0 copy-start.5
  56.9 13.6 %collective-permute-done = bf16[512,1024]{1,0:T(8,128)(2,1)} collective-permute-done((bf16[512,1024]{1,0:T(8,128)(2,1)}, bf16[512,1024]{1,0:T(8,128)(2,1)}, u32[]{:S(2)}, u32[]{:S(2)}) %collective-permute-start) | collective-permute-done | bytes 1048608 | tf_op jit(solution)/shard_map/ppermute | solution.py:302
  70.6 0.0 copy-done.12
  70.6 2.5 %add_bitcast_fusion.grad_ref.gated_ref = f32[512,1024]{1,0:T(8,128)S(1)} fusion(f32[1024,512]{0,1:T(8,128)S(1)} %fusion.4, bf16[512,1024]{1,0:T(8,128)(2,1)} %collective-permute-done, bf16[1024,1,1024]{0,2,1:T(8,128)(2,1)S(1)} %constant_dynamic-slice_fusion), kind=kOutput, calls=%fused_computation.7 | convolution fusion | flops 1074266112 | bytes 7340032 | tf_op jit(solution)/shard_map/dot_general | solution.py:326
  73.1 0.0 copy-done.5
  73.1 3.6 %shard_map.141 = bf16[16,256,128]{2,1,0:T(8,128)(2,1)} custom-call(f32[512,1024]{1,0:T(8,128)S(1)} %add_bitcast_fusion.grad_ref.gated_ref, bf16[512,1024]{1,0:T(8,128)(2,1)S(1)} %copy-done.5), custom_call_target="tpu_custom_call" | custom-call | flops 2097152 | bytes 4194304 | tf_op jit(solution)/shard_map/pallas_call | solution.py:284
  76.6 0.0 all-to-all-done.1
  76.6 0.0 copy-start.13
  76.6 5.8 %all-to-all-start.3 = ((bf16[16,256,128]{2,1,0:T(8,128)(2,1)}), bf16[16,256,128]{2,1,0:T(8,128)(2,1)}, u32[]{:S(2)}, u32[]{:S(2)}) async-start(bf16[16,256,128]{2,1,0:T(8,128)(2,1)} %shard_map.141), calls=%async_computation.3 | async-start | bytes 2097152 | tf_op jit(solution)/shard_map/all_to_all | solution.py:298
  82.5 0.0 copy-done.13
  82.5 53.5 %convolve.1 = bf16[4096,128]{1,0:T(8,128)(2,1)} custom-call(bf16[4096,128]{1,0:T(8,128)(2,1)} %bitcast.35, bf16[4096,128]{1,0:T(8,128)(2,1)} %bitcast.33, bf16[128,128,128]{2,1,0:T(8,128)(2,1)} %constant.24.clone.enter_ref, bf16[256,768]{1,0:T(8,128)(2,1)} %constant.25.clone.forth_ref, bf16[256,768]{1,0:T(8,128)(2,1)} %constant.26.clone.back_ref, ...), custom_call_target="tpu_custom_call" | custom-call | flops 6442450944 | bytes 12582912 | tf_op jit(solution)/shard_map/convolve/pallas_call | solution.py:183
  136.0 0.0 all-to-all-done.3
  136.0 6.0 %all-to-all-start.2 = ((bf16[16,256,128]{2,1,0:T(8,128)(2,1)}), bf16[16,256,128]{2,1,0:T(8,128)(2,1)}, u32[]{:S(2)}, u32[]{:S(2)}) async-start(bf16[16,256,128]{2,1,0:T(8,128)(2,1)} %bitcast.37), calls=%async_computation.2 | async-start | bytes 2097152 | tf_op jit(solution)/shard_map/all_to_all | solution.py:298
  142.0 4.0 %copy.21 = bf16[1024,1,1024]{2,0,1:T(8,128)(2,1)} copy(bf16[1024,1,1024]{0,2,1:T(8,128)(2,1)} %copy-done.12) | data formatting | bytes 4194304 | tf_op jit(solution)/shard_map/jit(dynamic_index_in_dim)/dynamic_slice | solution.py:314
  145.9 1.5 collective-permute-start.2
  147.5 53.5 %convolve_adjoint.1 = bf16[4096,128]{1,0:T(8,128)(2,1)} custom-call(bf16[4096,128]{1,0:T(8,128)(2,1)} %bitcast.8.signal_ref, bf16[4096,128]{1,0:T(8,128)(2,1)} %bitcast.34, bf16[128,128,128]{2,1,0:T(8,128)(2,1)} %constant.24.clone.enter_ref, bf16[256,768]{1,0:T(8,128)(2,1)} %constant.25.clone.forth_ref, bf16[256,768]{1,0:T(8,128)(2,1)} %constant.26.clone.back_ref, ...), custom_call_target="tpu_custom_call" | custom-call | flops 6442450944 | bytes 12582912 | tf_op jit(solution)/shard_map/convolve_adjoint/pallas_call | solution.py:183
  201.0 0.0 copy-start.1
  201.0 0.0 copy-start.9
  201.0 0.0 all-to-all-done.2.message_ref
  201.0 6.1 %all-to-all-start.4 = ((bf16[16,256,128]{2,1,0:T(8,128)(2,1)}), bf16[16,256,128]{2,1,0:T(8,128)(2,1)}, u32[]{:S(2)}, u32[]{:S(2)}) async-start(bf16[16,256,128]{2,1,0:T(8,128)(2,1)} %bitcast.36), calls=%async_computation.4 | async-start | bytes 2097152 | tf_op jit(solution)/shard_map/all_to_all | solution.py:298
  207.1 0.0 copy-done.1
  207.1 0.0 copy-done.9
  207.1 0.0 copy-start.3
  207.2 1.2 copy-done.3
  208.4 0.0 copy-start.6
  208.4 1.2 copy-done.6
  209.6 0.0 copy-start.11
  209.6 6.2 %shard_map.140 = (bf16[512,1024]{1,0:T(8,128)(2,1)}, bf16[512,1024]{1,0:T(8,128)(2,1)}) custom-call(bf16[16,256,128]{2,1,0:T(8,128)(2,1)} %all-to-all-done.2.message_ref, bf16[512,1024]{1,0:T(8,128)(2,1)S(1)} %copy-done.1, bf16[512,1024]{1,0:T(8,128)(2,1)S(1)} %copy-done.3, bf16[512,1024]{1,0:T(8,128)(2,1)S(1)} %copy-done.6, f32[1,1024]{1,0:T(1,128)S(1)} %bitcast.27, ...), custom_call_target="tpu_custom_call" | custom-call | flops 2097152 | bytes 8392704 | tf_op jit(solution)/shard_map/pallas_call | solution.py:284
  215.8 0.5 collective-permute-start.1
  216.3 0.0 copy-done.11
  216.3 3.9 %fusion.2 = f32[512,1024]{1,0:T(8,128)} fusion(bf16[512,1024]{1,0:T(8,128)(2,1)} %get-tuple-element.8, bf16[1024,2,1024]{0,2,1:T(8,128)(2,1)S(1)} %bitcast.31, s32[]{:T(128)S(6)} %select_n.7), kind=kOutput, calls=%fused_computation.2 | convolution fusion | flops 1073741824 | bytes 5242884 | tf_op jit(solution)/shard_map/dot_general | solution.py:343
  220.2 9.9 %all-to-all-done.4.message_ref = bf16[16,256,128]{2,1,0:T(8,128)(2,1)} async-done(((bf16[16,256,128]{2,1,0:T(8,128)(2,1)}), bf16[16,256,128]{2,1,0:T(8,128)(2,1)}, u32[]{:S(2)}, u32[]{:S(2)}) %all-to-all-start.4) | async-done | bytes 1048608 | tf_op jit(solution)/shard_map/all_to_all | solution.py:298
  230.1 0.0 copy-start.4
  230.1 1.2 copy-done.4
  231.3 0.0 copy-start.7
  231.3 1.2 copy-done.7
  232.6 0.0 copy-start.16
  232.6 6.0 %shard_map.142 = (bf16[512,1024]{1,0:T(8,128)(2,1)}, bf16[512,1024]{1,0:T(8,128)(2,1)}) custom-call(bf16[16,256,128]{2,1,0:T(8,128)(2,1)} %all-to-all-done.4.message_ref, bf16[512,1024]{1,0:T(8,128)(2,1)S(1)} %copy-done.1, bf16[512,1024]{1,0:T(8,128)(2,1)S(1)} %copy-done.4, bf16[512,1024]{1,0:T(8,128)(2,1)S(1)} %copy-done.7, f32[1,1024]{1,0:T(1,128)S(1)} %bitcast.28, ...), custom_call_target="tpu_custom_call" | custom-call | flops 2097152 | bytes 8392704 | tf_op jit(solution)/shard_map/pallas_call | solution.py:284
  238.6 0.0 collective-permute-done.2
  238.6 3.0 %collective-permute-done.1 = bf16[512,1024]{1,0:T(8,128)(2,1)} collective-permute-done((bf16[512,1024]{1,0:T(8,128)(2,1)}, bf16[512,1024]{1,0:T(8,128)(2,1)}, u32[]{:S(2)}, u32[]{:S(2)}) %collective-permute-start.1) | collective-permute-done | bytes 1048608 | tf_op jit(solution)/shard_map/ppermute | solution.py:302
  241.5 0.0 copy-done.16
  241.5 4.1 %add_convert_fusion = bf16[512,1024]{1,0:T(8,128)(2,1)} fusion(f32[512,1024]{1,0:T(8,128)S(1)} %copy-done.16, bf16[512,1024]{1,0:T(8,128)(2,1)} %collective-permute-done.1, bf16[1024,1024]{1,0:T(8,128)(2,1)} %collective-permute-done.2), kind=kOutput, calls=%fused_computation.6 | convolution fusion | flops 1074790400 | bytes 6291456 | tf_op jit(solution)/shard_map/dot_general | solution.py:344
Async XLA Ops:
  0.6 1.2 copy-start
  1.9 1.2 copy-start.2
  3.1 10.9 %copy-start.8 = (f32[512,1024]{1,0:T(8,128)S(1)}, f32[512,1024]{1,0:T(8,128)}, u32[]{:S(2)}) copy-start(f32[512,1024]{1,0:T(8,128)} %taps_ref.1) | copy-start | bytes 6291460
  6.6 30.3 %all-to-all-start = ((bf16[16,256,128]{2,1,0:T(8,128)(2,1)}), bf16[16,256,128]{2,1,0:T(8,128)(2,1)S(1)}, u32[]{:S(2)}, u32[]{:S(2)}) async-start(bf16[16,256,128]{2,1,0:T(8,128)(2,1)} %shard_map.138), calls=%async_computation | async-start | bytes 2097152 | tf_op jit(solution)/shard_map/all_to_all | solution.py:298
  36.9 1.0 copy-start.14
  37.9 38.7 %all-to-all-start.1 = ((bf16[16,256,128]{2,1,0:T(8,128)(2,1)}), bf16[16,256,128]{2,1,0:T(8,128)(2,1)S(1)}, u32[]{:S(2)}, u32[]{:S(2)}) async-start(bf16[16,256,128]{2,1,0:T(8,128)(2,1)} %shard_map.139), calls=%async_computation.1 | async-start | bytes 2097152 | tf_op jit(solution)/shard_map/all_to_all | solution.py:298
  44.8 25.8 %collective-permute-start = (bf16[512,1024]{1,0:T(8,128)(2,1)}, bf16[512,1024]{1,0:T(8,128)(2,1)}, u32[]{:S(2)}, u32[]{:S(2)}) collective-permute-start(bf16[512,1024]{1,0:T(8,128)(2,1)} %param.17), channel_id=1, source_target_pairs={{0,1},{1,0},{2,3},{3,2},{4,5},{5,4},{6,7},{7,6},{8,9},{9,8},{10,11... | collective-permute-start | bytes 3145736 | tf_op jit(solution)/shard_map/ppermute | solution.py:302
  46.4 8.4 %copy-start.15 = (bf16[512,1024]{1,0:T(8,128)(2,1)S(1)}, bf16[512,1024]{1,0:T(8,128)(2,1)}, u32[]{:S(2)}) copy-start(bf16[512,1024]{1,0:T(8,128)(2,1)} %param.17) | copy-start | bytes 3145732
  52.8 2.8 %copy-start.10 = (bf16[1024,2048]{0,1:T(8,128)(2,1)S(1)}, bf16[1024,2048]{0,1:T(8,128)(2,1)}, u32[]{:S(2)}) copy-start(bf16[1024,2048]{0,1:T(8,128)(2,1)} %copy.19) | copy-start | bytes 12582916
  55.7 14.9 %copy-start.12 = (bf16[1024,1,1024]{0,2,1:T(8,128)(2,1)}, bf16[1024,1,1024]{0,2,1:T(8,128)(2,1)S(1)}, u32[]{:S(2)}) copy-start(bf16[1024,1,1024]{0,2,1:T(8,128)(2,1)S(1)} %constant_dynamic-slice_fusion) | copy-start | bytes 6291460
  56.9 16.2 %copy-start.5 = (bf16[512,1024]{1,0:T(8,128)(2,1)S(1)}, bf16[512,1024]{1,0:T(8,128)(2,1)}, u32[]{:S(2)}) copy-start(bf16[512,1024]{1,0:T(8,128)(2,1)} %query_ref.5) | copy-start | bytes 3145732
  76.6 5.8 %copy-start.13 = (bf16[16,256,128]{2,1,0:T(8,128)(2,1)}, bf16[16,256,128]{2,1,0:T(8,128)(2,1)S(1)}, u32[]{:S(2)}) copy-start(bf16[16,256,128]{2,1,0:T(8,128)(2,1)S(1)} %all-to-all-done.1) | copy-start | bytes 3145732
  76.6 59.3 %all-to-all-start.3 = ((bf16[16,256,128]{2,1,0:T(8,128)(2,1)}), bf16[16,256,128]{2,1,0:T(8,128)(2,1)}, u32[]{:S(2)}, u32[]{:S(2)}) async-start(bf16[16,256,128]{2,1,0:T(8,128)(2,1)} %shard_map.141), calls=%async_computation.3 | async-start | bytes 2097152 | tf_op jit(solution)/shard_map/all_to_all | solution.py:298
  136.0 65.0 %all-to-all-start.2 = ((bf16[16,256,128]{2,1,0:T(8,128)(2,1)}), bf16[16,256,128]{2,1,0:T(8,128)(2,1)}, u32[]{:S(2)}, u32[]{:S(2)}) async-start(bf16[16,256,128]{2,1,0:T(8,128)(2,1)} %bitcast.37), calls=%async_computation.2 | async-start | bytes 2097152 | tf_op jit(solution)/shard_map/all_to_all | solution.py:298
  145.9 92.6 %collective-permute-start.2 = (bf16[1024,1024]{1,0:T(8,128)(2,1)}, bf16[1024,1024]{1,0:T(8,128)(2,1)}, u32[]{:S(2)}, u32[]{:S(2)}) collective-permute-start(bf16[1024,1024]{1,0:T(8,128)(2,1)} %bitcast.32), channel_id=1, source_target_pairs={{0,1},{1,0},{2,3},{3,2},{4,5},{5,4},{6,7},{7,6},{8,9},{9,8},{10,11... | collective-permute-start | bytes 6291464 | tf_op jit(solution)/shard_map/ppermute | solution.py:302
  201.0 6.2 %copy-start.1 = (bf16[512,1024]{1,0:T(8,128)(2,1)S(1)}, bf16[512,1024]{1,0:T(8,128)(2,1)}, u32[]{:S(2)}) copy-start(bf16[512,1024]{1,0:T(8,128)(2,1)} %key_ref.5) | copy-start | bytes 3145732
  201.0 6.2 %copy-start.9 = (f32[1024]{0:T(1024)S(1)}, f32[1024]{0:T(1024)}, u32[]{:S(2)}) copy-start(f32[1024]{0:T(1024)} %param.15) | copy-start | bytes 12292
  201.0 29.2 %all-to-all-start.4 = ((bf16[16,256,128]{2,1,0:T(8,128)(2,1)}), bf16[16,256,128]{2,1,0:T(8,128)(2,1)}, u32[]{:S(2)}, u32[]{:S(2)}) async-start(bf16[16,256,128]{2,1,0:T(8,128)(2,1)} %bitcast.36), calls=%async_computation.4 | async-start | bytes 2097152 | tf_op jit(solution)/shard_map/all_to_all | solution.py:298
  207.1 1.2 copy-start.3
  208.4 1.2 copy-start.6
  209.6 6.7 %copy-start.11 = (bf16[1024,2048]{0,1:T(8,128)(2,1)S(1)}, bf16[1024,2048]{0,1:T(8,128)(2,1)}, u32[]{:S(2)}) copy-start(bf16[1024,2048]{0,1:T(8,128)(2,1)} %copy.19) | copy-start | bytes 12582916
  215.8 25.7 %collective-permute-start.1 = (bf16[512,1024]{1,0:T(8,128)(2,1)}, bf16[512,1024]{1,0:T(8,128)(2,1)}, u32[]{:S(2)}, u32[]{:S(2)}) collective-permute-start(bf16[512,1024]{1,0:T(8,128)(2,1)} %get-tuple-element.8), channel_id=1, source_target_pairs={{0,1},{1,0},{2,3},{3,2},{4,5},{5,4},{6,7},{7,6},{8,9},{9,8},{10,11... | collective-permute-start | bytes 3145736 | tf_op jit(solution)/shard_map/ppermute | solution.py:302
  230.1 1.2 copy-start.4
  231.3 1.2 copy-start.7
  232.6 9.0 %copy-start.16 = (f32[512,1024]{1,0:T(8,128)S(1)}, f32[512,1024]{1,0:T(8,128)}, u32[]{:S(2)}) copy-start(f32[512,1024]{1,0:T(8,128)} %fusion.2) | copy-start | bytes 6291460

commit v2 on v0

v2 whole, which is shorter than its diff:
```python
import functools
import math

import jax
import jax.numpy as jnp
import ml_dtypes
import numpy as np
from jax import lax
from jax.experimental import pallas as pl
from jax.experimental.pallas import tpu as pltpu
from jax.sharding import PartitionSpec as P

F32 = jnp.float32
BF16 = jnp.bfloat16
LANES = 128


def split_table(table):
    high = table.astype(ml_dtypes.bfloat16)
    low = (table - high.astype(np.float64)).astype(ml_dtypes.bfloat16)
    return high, low


def transform_tables(devices, tokens_each):
    length = devices * tokens_each
    rows = length // LANES
    pieces = tokens_each // LANES
    row = np.arange(rows)
    n1 = (row % devices) * pieces + row // devices
    k1 = np.arange(rows)
    n2 = np.arange(LANES)

    def waves(turns, modulus):
        angle = (turns % modulus) * (2.0 * math.pi / modulus)
        return np.cos(angle), np.sin(angle)

    c, s = waves((4 * k1 + 1)[:, None] * n1[None, :], 4 * rows)
    high, low = split_table(np.concatenate([c, -s], axis=0))
    enter = np.concatenate([high, low], axis=1)
    high, low = split_table(np.concatenate([c.T, -s.T], axis=1) / length)
    leave = np.concatenate([high, low, high], axis=1)
    c, s = waves(n2[:, None] * n2[None, :], LANES)
    high, low = split_table(np.block([[c, -s], [s, c]]))
    forth = np.concatenate([high, low, high], axis=0)
    high, low = split_table(np.block([[c, s], [-s, c]]))
    back = np.concatenate([high, low, high], axis=0)
    c, s = waves((4 * k1 + 1)[:, None] * n2[None, :], 4 * length)
    turn = np.concatenate([c, s], axis=1).astype(np.float32)
    return enter, turn, np.concatenate([forth, back], axis=0), leave


def split_float(values):
    high = values.astype(BF16)
    return high, (values - high.astype(F32)).astype(BF16)


def mxu(left, right):
    return jnp.dot(left, right, preferred_element_type=F32)


def widen(held_ref, wide):
    for piece in range(wide.shape[0]):
        wide[piece] = held_ref[:, piece * LANES : (piece + 1) * LANES].astype(F32)


def narrow(wide, out_ref):
    for piece in range(wide.shape[0]):
        out_ref[:, piece * LANES : (piece + 1) * LANES] = wide[piece].astype(BF16)


def load_channels(wide, first, stride, devices, group):
    columns = []
    for member in range(group):
        place = pl.ds(first + member, devices, stride=stride)
        columns.append(
            jnp.concatenate([wide[piece, place, :] for piece in range(wide.shape[0])], axis=0)
        )
    return jnp.concatenate(columns, axis=1).astype(BF16)


def to_spectrum(data, group, enter_ref, turn_ref, waves_ref):
    rows = data.shape[0]
    entered = mxu(enter_ref[...], jnp.concatenate([data, data], axis=0))
    cosine, sine = turn_ref[:, :LANES], turn_ref[:, LANES:]
    turned = []
    for member in range(group):
        at = member * LANES
        real, imag = entered[:rows, at : at + LANES], entered[rows:, at : at + LANES]
        turned.append(
            jnp.concatenate([real * cosine + imag * sine, imag * cosine - real * sine], axis=1)
        )
    high, low = split_float(jnp.concatenate(turned, axis=0))
    return mxu(jnp.concatenate([high, high, low], axis=1), waves_ref[: 6 * LANES, :])


def from_spectrum(real, imag, group, turn_ref, waves_ref, leave_ref):
    high, low = split_float(jnp.concatenate([real, imag], axis=1))
    returned = mxu(jnp.concatenate([high, high, low], axis=1), waves_ref[6 * LANES :, :])
    rows = returned.shape[0] // group
    cosine, sine = turn_ref[:, :LANES], turn_ref[:, LANES:]
    turned = []
    for member in range(group):
        at = member * rows
        real, imag = returned[at : at + rows, :LANES], returned[at : at + rows, LANES:]
        turned.append(
            jnp.concatenate([real * cosine - imag * sine, real * sine + imag * cosine], axis=0)
        )
    high, low = split_float(jnp.concatenate(turned, axis=1))
    return mxu(leave_ref[...], jnp.concatenate([high, high, low], axis=0))


def store_channels(wide, first, stride, devices, group, result):
    for member in range(group):
        at = member * LANES
        place = pl.ds(first + member, devices, stride=stride)
        for piece in range(wide.shape[0]):
            row = piece * devices
            wide[piece, place, :] = result[row : row + devices, at : at + LANES]


def forward_kernel(
    devices,
    group,
    held_ref,
    enter_ref,
    turn_ref,
    waves_ref,
    leave_ref,
    out_ref,
    spectrum_ref,
    held_wide,
    out_wide,
):
    step = pl.program_id(0)
    channels = out_ref.shape[0] // devices

    @pl.when(step == 0)
    def _():
        widen(held_ref, held_wide)

    first = step * group
    data = load_channels(held_wide, first, 2 * channels, devices, group)
    taps = load_channels(held_wide, channels + first, 2 * channels, devices, group)
    into = (enter_ref, turn_ref, waves_ref)
    data = to_spectrum(data, group, *into)
    taps = to_spectrum(taps, group, *into)
    spectrum_ref[...] = taps
    data_real, data_imag = data[:, :LANES], data[:, LANES:]
    taps_real, taps_imag = taps[:, :LANES], taps[:, LANES:]
    result = from_spectrum(
        taps_real * data_real - taps_imag * data_imag,
        taps_real * data_imag + taps_imag * data_real,
        group,
        turn_ref,
        waves_ref,
        leave_ref,
    )
    store_channels(out_wide, first, channels, devices, group, result)

    @pl.when(step == pl.num_programs(0) - 1)
    def _():
        narrow(out_wide, out_ref)


def adjoint_kernel(
    devices,
    group,
    held_ref,
    enter_ref,
    turn_ref,
    waves_ref,
    leave_ref,
    spectrum_ref,
    out_ref,
    held_wide,
    out_wide,
):
    step = pl.program_id(0)
    channels = out_ref.shape[0] // devices

    @pl.when(step == 0)
    def _():
        widen(held_ref, held_wide)

    first = step * group
    data = load_channels(held_wide, first, channels, devices, group)
    data = to_spectrum(data, group, enter_ref, turn_ref, waves_ref)
    data_real, data_imag = data[:, :LANES], data[:, LANES:]
    taps_real, taps_imag = spectrum_ref[:, :LANES], spectrum_ref[:, LANES:]
    result = from_spectrum(
        taps_real * data_real + taps_imag * data_imag,
        taps_real * data_imag - taps_imag * data_real,
        group,
        turn_ref,
        waves_ref,
        leave_ref,
    )
    store_channels(out_wide, first, channels, devices, group, result)

    @pl.when(step == pl.num_programs(0) - 1)
    def _():
        narrow(out_wide, out_ref)


GROUP = 16
WIDTH = 512
VMEM_LIMIT = 60 * 1024 * 1024


def whole_block(array):
    return pl.BlockSpec(array.shape, lambda i: (0,) * len(array.shape))


def convolve(held, tables, devices, spectrum=None):
    width, tokens = held.shape
    channels = width // devices // (2 if spectrum is None else 1)
    rows = devices * tokens // LANES
    group = math.gcd(GROUP, channels)
    out = jax.ShapeDtypeStruct((devices * channels, tokens), BF16)
    taps = jax.ShapeDtypeStruct((channels * rows, 2 * LANES), F32)
    taps_block = pl.BlockSpec((group * rows, 2 * LANES), lambda i: (i, 0))
    forward = spectrum is None
    transforms = 3 if forward else 2
    return pl.pallas_call(
        functools.partial(forward_kernel if forward else adjoint_kernel, devices, group),
        grid=(channels // group,),
        out_shape=(out, taps) if forward else out,
        in_specs=[whole_block(held)]
        + [whole_block(table) for table in tables]
        + ([] if forward else [taps_block]),
        out_specs=(whole_block(out), taps_block) if forward else whole_block(out),
        scratch_shapes=[
            pltpu.VMEM((tokens // LANES, width, LANES), F32),
            pltpu.VMEM((tokens // LANES, devices * channels, LANES), F32),
        ],
        compiler_params=pltpu.CompilerParams(vmem_limit_bytes=VMEM_LIMIT),
        cost_estimate=pl.CostEstimate(
            flops=transforms * 8 * 2 * 2 * LANES * 2 * LANES * rows * channels,
            bytes_accessed=8 * 1024 * 1024,
            transcendentals=0,
        ),
        name="convolve" if forward else "correlate",
    )(held, *tables, *([] if forward else [spectrum]))


def rows_of(block, which, channels):
    return block[which * channels : (which + 1) * channels, :]


def mix_kernel(key_ref, value_ref, taps_ref, message_ref):
    targets, both, _ = message_ref.shape
    channels = both // 2
    mixed = (key_ref[...].astype(F32) * value_ref[...].astype(F32)).astype(BF16).T
    taps = taps_ref[...].astype(BF16).T
    for target in range(targets):
        message_ref[target, :channels, :] = rows_of(mixed, target, channels)
        message_ref[target, channels:, :] = rows_of(taps, target, channels)


def grad_kernel(gated_ref, query_ref, message_ref):
    targets, channels, _ = message_ref.shape
    grad = (gated_ref[...] * query_ref[...].astype(F32)).astype(BF16).T
    for target in range(targets):
        message_ref[target] = rows_of(grad, target, channels)


def tokens_first(message_ref):
    targets, channels, tokens = message_ref.shape
    return message_ref[...].reshape(targets * channels, tokens).T.astype(F32)


def gate_kernel(
    message_ref, key_ref, value_ref, query_ref, skip_ref, grad_ref, gated_ref, query_grad_ref
):
    mixed = key_ref[...].astype(F32) * value_ref[...].astype(F32)
    conv_out = tokens_first(message_ref) + skip_ref[...] * mixed
    gated_ref[...] = (query_ref[...].astype(F32) * conv_out).astype(BF16)
    query_grad_ref[...] = (grad_ref[...] * conv_out).astype(BF16)


def input_grad_kernel(
    message_ref, key_ref, value_ref, query_ref, skip_ref, grad_ref, key_grad_ref, value_grad_ref
):
    grad_conv = grad_ref[...] * query_ref[...].astype(F32)
    grad_mixed = tokens_first(message_ref) + skip_ref[...] * grad_conv
    key_grad_ref[...] = (grad_mixed * value_ref[...].astype(F32)).astype(BF16)
    value_grad_ref[...] = (grad_mixed * key_ref[...].astype(F32)).astype(BF16)


def by_blocks(kernel, shape, inputs, outs):
    tokens, channels = shape
    steps = channels // math.gcd(channels, WIDTH)

    def spec_of(array):
        if len(array.shape) == 3:
            targets, rows, _ = array.shape
            return pl.BlockSpec((targets // steps, rows, tokens), lambda j: (j, 0, 0))
        return pl.BlockSpec((array.shape[0], channels // steps), lambda j: (0, j))

    moved = sum(a.size * a.dtype.itemsize for a in list(inputs) + list(outs))
    return pl.pallas_call(
        kernel,
        grid=(steps,),
        out_shape=outs,
        in_specs=[spec_of(a) for a in inputs],
        out_specs=[spec_of(a) for a in outs],
        cost_estimate=pl.CostEstimate(
            flops=4 * tokens * channels, bytes_accessed=moved, transcendentals=0
        ),
        compiler_params=pltpu.CompilerParams(vmem_limit_bytes=VMEM_LIMIT),
    )(*inputs)


def exchange(values):
    return lax.all_to_all(values, "seq", split_axis=0, concat_axis=0, tiled=True)


def swap_pair(values):
    return lax.ppermute(values, "ch", [(0, 1), (1, 0)])


def on_device(query_in, key_in, value_in, filter_taps, skip_gain, out_weight, out_grad):
    devices = lax.axis_size("seq")
    in_pairs = lax.axis_size("ch") == 2
    shape = key_in.shape
    tokens, channels = shape
    each = channels // devices
    tables = [jnp.asarray(table) for table in transform_tables(devices, tokens)]
    skip_row = skip_gain.reshape(1, channels)
    plain = jax.ShapeDtypeStruct(shape, BF16)
    message = jax.ShapeDtypeStruct((devices, each, tokens), BF16)
    double = jax.ShapeDtypeStruct((devices, 2 * each, tokens), BF16)
    over_columns = (((1,), (1,)), ((), ()))

    def project_back(grad, weight):
        return lax.dot_general(grad, weight, over_columns, preferred_element_type=F32)

    if in_pairs:
        grad_other = swap_pair(out_grad)
    (sent,) = by_blocks(mix_kernel, shape, [key_in, value_in, filter_taps], [double])
    held = exchange(sent)

    if in_pairs:
        mine = lax.axis_index("ch") * channels
        other = channels - mine
        weight_mine = lax.dynamic_slice_in_dim(out_weight, mine, channels, axis=1)
        weight_other = lax.dynamic_slice_in_dim(out_weight, other, channels, axis=1)
        grad_other, weight_sent = lax.optimization_barrier((grad_other, weight_other))
        weight_crossed = swap_pair(weight_sent)
        grad_gated = project_back(out_grad, weight_mine) + project_back(grad_other, weight_other)
    else:
        grad_gated = project_back(
            lax.all_gather(out_grad, "ch", axis=1, tiled=True), out_weight
        )
    (grad_sent,) = by_blocks(grad_kernel, shape, [grad_gated, query_in], [message])
    grad_held = exchange(grad_sent)

    conv_held, spectrum = convolve(held.reshape(-1, tokens), tables, devices)
    if in_pairs:
        conv_held, weight_crossed = lax.optimization_barrier((conv_held, weight_crossed))
    conv_back = exchange(conv_held.reshape(message.shape))
    mixed_grad_held = convolve(grad_held.reshape(-1, tokens), tables, devices, spectrum)
    mixed_grad_back = exchange(mixed_grad_held.reshape(message.shape))

    gated_out, query_grad = by_blocks(
        gate_kernel,
        shape,
        [conv_back, key_in, value_in, query_in, skip_row, grad_gated],
        [plain, plain],
    )
    if in_pairs:
        gated_other = swap_pair(gated_out)
        mixed_out = (
            jnp.dot(gated_out, weight_mine, preferred_element_type=F32)
            + jnp.dot(gated_other, weight_crossed, preferred_element_type=F32)
        ).astype(BF16)
    else:
        out_terms = jnp.dot(gated_out, out_weight, preferred_element_type=F32)
        mixed_out = lax.psum_scatter(out_terms, "ch", scatter_dimension=1, tiled=True)
        mixed_out = mixed_out.astype(BF16)
    key_grad, value_grad = by_blocks(
        input_grad_kernel,
        shape,
        [mixed_grad_back, key_in, value_in, query_in, skip_row, grad_gated],
        [plain, plain],
    )
    return (mixed_out, query_grad, key_grad, value_grad)


def solution(mesh):
    spread = P("seq", "ch")
    placed = (spread, spread, spread, spread, P("ch"), P("ch", None), spread)
    return jax.shard_map(
        on_device, mesh=mesh, in_specs=placed, out_specs=(spread,) * 4, check_vma=False
    )
```

time: 1600 us -> 160 us (0.10)
  waiting for transfers between devices: 757 us -> 60.9 us
  matrix products: 363 us -> 12.5 us
  starting transfers between devices: 229 us -> 37.1 us
  local copies, waits for them, and re-layouts: 158 us -> 4.32 us
  blocking collectives: 58.8 us -> 0 us
  Pallas kernels: 0 us -> 42.8 us
    all_to_all x11 -> x4, waiting for transfers between devices: 665 us -> 36.3 us  [exchange(): lax.all_to_all(values, 'seq', split_axis=0, concat_axis=0, tiled=True)]
    dot_general x26 -> x4, matrix products: 363 us -> 12.5 us  [the longest x2 5.86 us: project_back(): lax.dot_general(grad, weight, over_columns, preferred_element_type=F32)]
    all_to_all x11 -> x4, starting transfers between devices: 229 us -> 32.4 us  [exchange(): lax.all_to_all(values, 'seq', split_axis=0, concat_axis=0, tiled=True)]
    all_to_all x16 -> x0, local copies, waits for them, and re-layouts: 74.3 us -> none  [the longest x8 37.9 us: regroup_pair(): lax.all_to_all(imag_part, 'seq', split_axis=1, concat_axis=0, tiled=True)]
    all_to_all x1 -> x0, blocking collectives: 58.8 us -> none  [regroup_real(): lax.all_to_all(values, 'seq', split_axis=1, concat_axis=0, tiled=True)]
    reduce_scatter x1 -> x0, waiting for transfers between devices: 53.9 us -> none  [on_device(): lax.psum_scatter(out_terms, 'ch', scatter_dimension=1, tiled=True)]
    pallas_call x0 -> x6, Pallas kernels: none -> 42.8 us  [the longest x2 28.1 us: convolve(): pl.pallas_call(functools.partial(forward_kernel if forward else adjoint_k...]
    all_gather x1 -> x0, waiting for transfers between devices: 37.5 us -> none  [on_device(): lax.all_gather(out_grad, 'ch', axis=1, tiled=True)]
  transfers between devices with their start and end apart: 13 -> 7, of which waited for: 13 -> 6; matrix products, arithmetic and copies ran while one was open for 15% -> 8% of each run, Pallas kernels for 0% -> 25%
where the time goes in v2:
time: 160 us; the launch traced here: 158 us
  waiting for transfers between devices  60.9 us (38%)
  Pallas kernels  42.8 us (27%)
  starting transfers between devices  37.1 us (23%)
  matrix products  12.5 us (8%)
  local copies, waits for them, and re-layouts  4.32 us (3%)
    all_to_all x4, waiting for transfers between devices, exchange(): lax.all_to_all(values, 'seq', split_axis=0, concat_axis=0, tiled=True)  36.3 us
    all_to_all x4, starting transfers between devices, exchange(): lax.all_to_all(values, 'seq', split_axis=0, concat_axis=0, tiled=True)  32.4 us
    pallas_call x2, Pallas kernels, convolve(): pl.pallas_call(functools.partial(forward_kernel if forward else adjoint_k...  28.1 us
    ppermute x3, waiting for transfers between devices, swap_pair(): return lax.ppermute(values, 'ch', [(0, 1), (1, 0)])  24.5 us
    pallas_call x4, Pallas kernels, by_blocks(): pl.pallas_call(kernel, grid=(steps,), out_shape=outs, in_specs=[spec_of(a...  14.7 us
    dot_general x2, matrix products, project_back(): lax.dot_general(grad, weight, over_columns, preferred_element_type=F32)  5.86 us
    ppermute x3, starting transfers between devices, swap_pair(): return lax.ppermute(values, 'ch', [(0, 1), (1, 0)])  4.68 us
    dot_general x1, matrix products, on_device(): jnp.dot(gated_other, weight_crossed, preferred_element_type=F32)  3.83 us
  transfers between devices with their start and end apart: 7, of which 6 were waited for; matrix products, arithmetic and copies ran while one was open for 8% of the time, Pallas kernels for 25%

profile of v2, /device:TPU:0, one launch (start us, length us, event | category | flops | bytes accessed | tf_op | source)
XLA Modules:
  0.0 158.4 jit_solution(4713088541044971037)
XLA Ops:
  0.6 3.5 %shard_map.138 = bf16[16,128,512]{2,1,0:T(8,128)(2,1)} custom-call(bf16[512,1024]{1,0:T(8,128)(2,1)} %key_ref.5, bf16[512,1024]{1,0:T(8,128)(2,1)} %value_ref.5, f32[512,1024]{1,0:T(8,128)} %taps_ref.1), custom_call_target="tpu_custom_call" | custom-call | flops 2097152 | bytes 6291456 | tf_op jit(solution)/shard_map/pallas_call | solution.py:301
  4.1 0.0 copy-start.5
  4.1 7.5 %all-to-all-start = ((bf16[16,128,512]{2,1,0:T(8,128)(2,1)}), bf16[16,128,512]{2,1,0:T(8,128)(2,1)S(1)}, u32[]{:S(2)}, u32[]{:S(2)}) async-start(bf16[16,128,512]{2,1,0:T(8,128)(2,1)} %shard_map.138), calls=%async_computation | async-start | bytes 4194304 | tf_op jit(solution)/shard_map/all_to_all | solution.py:315
  11.6 0.0 copy-done.5
  11.6 1.6 %collective-permute-start = (bf16[512,1024]{1,0:T(8,128)(2,1)S(1)}, bf16[512,1024]{1,0:T(8,128)(2,1)}, u32[]{:S(2)}, u32[]{:S(2)}) collective-permute-start(bf16[512,1024]{1,0:T(8,128)(2,1)S(1)} %copy-done.5), channel_id=1, source_target_pairs={{0,1},{1,0},{2,3},{3,2},{4,5},{5,4},{6,7},{7,6},{8,9},{9,8},{10,11... | collective-permute-start | bytes 3145736 | tf_op jit(solution)/shard_map/ppermute | solution.py:319
  13.2 0.0 copy-start.3
  13.2 3.3 %constant_dynamic-slice_fusion = bf16[1024,1024]{1,0:T(8,128)(2,1)} fusion(bf16[1024,2048]{1,0:T(8,128)(2,1)} %param.16, s32[]{:T(128)S(6)} %select_n.6), kind=kLoop, calls=%fused_computation.8 | loop fusion | bytes 4194308 | tf_op jit(solution)/shard_map/dynamic_slice | solution.py:347
  16.5 0.0 copy-done.3
  16.5 1.3 fusion.2
  17.8 19.5 %collective-permute-done = bf16[512,1024]{1,0:T(8,128)(2,1)} collective-permute-done((bf16[512,1024]{1,0:T(8,128)(2,1)S(1)}, bf16[512,1024]{1,0:T(8,128)(2,1)}, u32[]{:S(2)}, u32[]{:S(2)}) %collective-permute-start) | collective-permute-done | bytes 1048608 | tf_op jit(solution)/shard_map/ppermute | solution.py:319
  37.3 1.5 collective-permute-start.1
  38.8 4.6 %bitcast_add_fusion.grad_ref.gated_ref = f32[512,1024]{1,0:T(8,128)} fusion(f32[1024,512]{0,1:T(8,128)S(1)} %fusion.2, bf16[512,1024]{1,0:T(8,128)(2,1)} %collective-permute-done, bf16[1024,1024]{1,0:T(8,128)(2,1)} %constant_dynamic-slice_fusion), kind=kOutput, calls=%fused_computation | convolution fusion | flops 1074266112 | bytes 7340032 | tf_op jit(solution)/shard_map/dot_general | solution.py:336
  43.4 2.8 %shard_map.140 = bf16[16,64,512]{2,1,0:T(8,128)(2,1)} custom-call(f32[512,1024]{1,0:T(8,128)} %bitcast_add_fusion.grad_ref.gated_ref, bf16[512,1024]{1,0:T(8,128)(2,1)} %query_ref.5), custom_call_target="tpu_custom_call" | custom-call | flops 2097152 | bytes 4194304 | tf_op jit(solution)/shard_map/pallas_call | solution.py:301
  46.2 6.5 %all-to-all-done = bf16[16,128,512]{2,1,0:T(8,128)(2,1)S(1)} async-done(((bf16[16,128,512]{2,1,0:T(8,128)(2,1)}), bf16[16,128,512]{2,1,0:T(8,128)(2,1)S(1)}, u32[]{:S(2)}, u32[]{:S(2)}) %all-to-all-start) | async-done | bytes 2097184 | tf_op jit(solution)/shard_map/all_to_all | solution.py:315
  52.7 0.0 copy-start.2
  52.7 11.2 %all-to-all-start.2 = ((bf16[16,64,512]{2,1,0:T(8,128)(2,1)}), bf16[16,64,512]{2,1,0:T(8,128)(2,1)S(1)}, u32[]{:S(2)}, u32[]{:S(2)}) async-start(bf16[16,64,512]{2,1,0:T(8,128)(2,1)} %shard_map.140), calls=%async_computation.2 | async-start | bytes 2097152 | tf_op jit(solution)/shard_map/all_to_all | solution.py:315
  64.0 0.0 copy-done.2
  64.0 15.8 %convolve.1 = (bf16[1024,512]{1,0:T(8,128)(2,1)}, f32[4096,256]{1,0:T(8,128)}) custom-call(bf16[2048,512]{1,0:T(8,128)(2,1)} %bitcast.13, bf16[128,128]{1,0:T(8,128)(2,1)} %constant.20.clone.enter_ref, f32[64,256]{1,0:T(8,128)} %constant.21.clone.turn_ref, bf16[1536,256]{1,0:T(8,128)(2,1)} %constant.22.clone.waves_ref, bf16[64,384]{1,0:T(8,128)(2,1)} %constant.23.clone.leave_ref), custom_call_target="tpu_custom_call" | custom-call | flops 12884901888 | bytes 8388608 | tf_op jit(solution)/shard_map/convolve/pallas_call | solution.py:224
  79.7 5.1 %collective-permute-done.1 = bf16[1024,1024]{1,0:T(8,128)(2,1)} collective-permute-done((bf16[1024,1024]{1,0:T(8,128)(2,1)}, bf16[1024,1024]{1,0:T(8,128)(2,1)}, u32[]{:S(2)}, u32[]{:S(2)}) %collective-permute-start.1) | collective-permute-done | bytes 2097184 | tf_op jit(solution)/shard_map/ppermute | solution.py:319
  84.8 2.1 %all-to-all-done.2 = bf16[16,64,512]{2,1,0:T(8,128)(2,1)S(1)} async-done(((bf16[16,64,512]{2,1,0:T(8,128)(2,1)}), bf16[16,64,512]{2,1,0:T(8,128)(2,1)S(1)}, u32[]{:S(2)}, u32[]{:S(2)}) %all-to-all-start.2) | async-done | bytes 1048608 | tf_op jit(solution)/shard_map/all_to_all | solution.py:315
  86.9 0.0 copy-start.4
  86.9 6.9 %all-to-all-start.1 = ((bf16[16,64,512]{2,1,0:T(8,128)(2,1)}), bf16[16,64,512]{2,1,0:T(8,128)(2,1)S(1)}, u32[]{:S(2)}, u32[]{:S(2)}) async-start(bf16[16,64,512]{2,1,0:T(8,128)(2,1)} %bitcast.16), calls=%async_computation.1 | async-start | bytes 2097152 | tf_op jit(solution)/shard_map/all_to_all | solution.py:315
  93.8 0.0 copy-done.4
  93.8 12.3 %correlate.1 = bf16[1024,512]{1,0:T(8,128)(2,1)} custom-call(bf16[1024,512]{1,0:T(8,128)(2,1)} %bitcast.14, bf16[128,128]{1,0:T(8,128)(2,1)} %constant.20.clone.enter_ref, f32[64,256]{1,0:T(8,128)} %constant.21.clone.turn_ref, bf16[1536,256]{1,0:T(8,128)(2,1)} %constant.22.clone.waves_ref, bf16[64,384]{1,0:T(8,128)(2,1)} %constant.23.clone.leave_ref, ...), custom_call_target="tpu_custom_call" | custom-call | flops 8589934592 | bytes 8388608 | tf_op jit(solution)/shard_map/correlate/pallas_call | solution.py:224
  106.1 10.6 %all-to-all-done.1.message_ref = bf16[16,64,512]{2,1,0:T(8,128)(2,1)S(1)} async-done(((bf16[16,64,512]{2,1,0:T(8,128)(2,1)}), bf16[16,64,512]{2,1,0:T(8,128)(2,1)S(1)}, u32[]{:S(2)}, u32[]{:S(2)}) %all-to-all-start.1) | async-done | bytes 1048608 | tf_op jit(solution)/shard_map/all_to_all | solution.py:315
  116.7 0.0 copy-start
  116.7 6.9 %all-to-all-start.3 = ((bf16[16,64,512]{2,1,0:T(8,128)(2,1)}), bf16[16,64,512]{2,1,0:T(8,128)(2,1)S(1)}, u32[]{:S(2)}, u32[]{:S(2)}) async-start(bf16[16,64,512]{2,1,0:T(8,128)(2,1)} %bitcast.15), calls=%async_computation.3 | async-start | bytes 2097152 | tf_op jit(solution)/shard_map/all_to_all | solution.py:315
  123.6 0.0 copy-done
  123.6 4.2 %shard_map.139 = (bf16[512,1024]{1,0:T(8,128)(2,1)}, bf16[512,1024]{1,0:T(8,128)(2,1)}) custom-call(bf16[16,64,512]{2,1,0:T(8,128)(2,1)} %copy-done, bf16[512,1024]{1,0:T(8,128)(2,1)} %key_ref.5, bf16[512,1024]{1,0:T(8,128)(2,1)} %value_ref.5, bf16[512,1024]{1,0:T(8,128)(2,1)} %query_ref.5, f32[1,1024]{1,0:T(1,128)} %bitcast.17, ...), custom_call_target="tpu_custom_call" | custom-call | flops 2097152 | bytes 8392704 | tf_op jit(solution)/shard_map/pallas_call | solution.py:301
  127.8 0.0 copy-start.6
  127.8 1.6 collective-permute-start.2
  129.4 17.1 %all-to-all-done.3.message_ref = bf16[16,64,512]{2,1,0:T(8,128)(2,1)S(1)} async-done(((bf16[16,64,512]{2,1,0:T(8,128)(2,1)}), bf16[16,64,512]{2,1,0:T(8,128)(2,1)S(1)}, u32[]{:S(2)}, u32[]{:S(2)}) %all-to-all-start.3) | async-done | bytes 1048608 | tf_op jit(solution)/shard_map/all_to_all | solution.py:315
  146.5 0.0 copy-start.1
  146.5 1.0 copy-done.1
  147.5 4.2 %shard_map.141 = (bf16[512,1024]{1,0:T(8,128)(2,1)}, bf16[512,1024]{1,0:T(8,128)(2,1)}) custom-call(bf16[16,64,512]{2,1,0:T(8,128)(2,1)} %copy-done.1, bf16[512,1024]{1,0:T(8,128)(2,1)} %key_ref.5, bf16[512,1024]{1,0:T(8,128)(2,1)} %value_ref.5, bf16[512,1024]{1,0:T(8,128)(2,1)} %query_ref.5, f32[1,1024]{1,0:T(1,128)} %bitcast.18, ...), custom_call_target="tpu_custom_call" | custom-call | flops 2097152 | bytes 8392704 | tf_op jit(solution)/shard_map/pallas_call | solution.py:301
  151.7 0.0 copy-done.6
  151.7 2.8 %fusion = f32[512,1024]{1,0:T(8,128)S(1)} fusion(bf16[512,1024]{1,0:T(8,128)(2,1)S(1)} %copy-done.6, bf16[1024,2048]{1,0:T(8,128)(2,1)} %param.16, s32[]{:T(128)S(6)} %select_n.7), kind=kOutput, calls=%fused_computation.2 | convolution fusion | flops 1073741824 | bytes 5242884 | tf_op jit(solution)/shard_map/dot_general | solution.py:374
  154.6 0.0 collective-permute-done.2
  154.6 3.8 %add_convert_fusion = bf16[512,1024]{1,0:T(8,128)(2,1)} fusion(f32[512,1024]{1,0:T(8,128)S(1)} %fusion, bf16[512,1024]{1,0:T(8,128)(2,1)S(1)} %collective-permute-done.2, bf16[1024,1024]{1,0:T(8,128)(2,1)} %collective-permute-done.1), kind=kOutput, calls=%fused_computation.1 | convolution fusion | flops 1074790400 | bytes 6291456 | tf_op jit(solution)/shard_map/dot_general | solution.py:375
Async XLA Ops:
  4.1 7.5 %copy-start.5 = (bf16[512,1024]{1,0:T(8,128)(2,1)S(1)}, bf16[512,1024]{1,0:T(8,128)(2,1)}, u32[]{:S(2)}) copy-start(bf16[512,1024]{1,0:T(8,128)(2,1)} %param.17) | copy-start | bytes 3145732
  4.1 48.6 %all-to-all-start = ((bf16[16,128,512]{2,1,0:T(8,128)(2,1)}), bf16[16,128,512]{2,1,0:T(8,128)(2,1)S(1)}, u32[]{:S(2)}, u32[]{:S(2)}) async-start(bf16[16,128,512]{2,1,0:T(8,128)(2,1)} %shard_map.138), calls=%async_computation | async-start | bytes 4194304 | tf_op jit(solution)/shard_map/all_to_all | solution.py:315
  11.6 25.7 %collective-permute-start = (bf16[512,1024]{1,0:T(8,128)(2,1)S(1)}, bf16[512,1024]{1,0:T(8,128)(2,1)}, u32[]{:S(2)}, u32[]{:S(2)}) collective-permute-start(bf16[512,1024]{1,0:T(8,128)(2,1)S(1)} %copy-done.5), channel_id=1, source_target_pairs={{0,1},{1,0},{2,3},{3,2},{4,5},{5,4},{6,7},{7,6},{8,9},{9,8},{10,11... | collective-permute-start | bytes 3145736 | tf_op jit(solution)/shard_map/ppermute | solution.py:319
  13.2 3.3 %copy-start.3 = (bf16[1024,2048]{1,0:T(8,128)(2,1)S(1)}, bf16[1024,2048]{1,0:T(8,128)(2,1)}, u32[]{:S(2)}) copy-start(bf16[1024,2048]{1,0:T(8,128)(2,1)} %param.16) | copy-start | bytes 12582916
  37.3 47.5 %collective-permute-start.1 = (bf16[1024,1024]{1,0:T(8,128)(2,1)}, bf16[1024,1024]{1,0:T(8,128)(2,1)}, u32[]{:S(2)}, u32[]{:S(2)}) collective-permute-start(bf16[1024,1024]{1,0:T(8,128)(2,1)} %constant_dynamic-slice_fusion), channel_id=1, source_target_pairs={{0,1},{1,0},{2,3},{3,2},{4,5},{5,4},{6,7},{7,6},{8,9},{9,8},{10,11... | collective-permute-start | bytes 6291464 | tf_op jit(solution)/shard_map/ppermute | solution.py:319
  52.7 11.2 %copy-start.2 = (bf16[16,128,512]{2,1,0:T(8,128)(2,1)}, bf16[16,128,512]{2,1,0:T(8,128)(2,1)S(1)}, u32[]{:S(2)}) copy-start(bf16[16,128,512]{2,1,0:T(8,128)(2,1)S(1)} %all-to-all-done) | copy-start | bytes 6291460
  52.7 34.2 %all-to-all-start.2 = ((bf16[16,64,512]{2,1,0:T(8,128)(2,1)}), bf16[16,64,512]{2,1,0:T(8,128)(2,1)S(1)}, u32[]{:S(2)}, u32[]{:S(2)}) async-start(bf16[16,64,512]{2,1,0:T(8,128)(2,1)} %shard_map.140), calls=%async_computation.2 | async-start | bytes 2097152 | tf_op jit(solution)/shard_map/all_to_all | solution.py:315
  86.9 6.9 %copy-start.4 = (bf16[16,64,512]{2,1,0:T(8,128)(2,1)}, bf16[16,64,512]{2,1,0:T(8,128)(2,1)S(1)}, u32[]{:S(2)}) copy-start(bf16[16,64,512]{2,1,0:T(8,128)(2,1)S(1)} %all-to-all-done.2) | copy-start | bytes 3145732
  86.9 29.8 %all-to-all-start.1 = ((bf16[16,64,512]{2,1,0:T(8,128)(2,1)}), bf16[16,64,512]{2,1,0:T(8,128)(2,1)S(1)}, u32[]{:S(2)}, u32[]{:S(2)}) async-start(bf16[16,64,512]{2,1,0:T(8,128)(2,1)} %bitcast.16), calls=%async_computation.1 | async-start | bytes 2097152 | tf_op jit(solution)/shard_map/all_to_all | solution.py:315
  116.7 6.9 %copy-start = (bf16[16,64,512]{2,1,0:T(8,128)(2,1)}, bf16[16,64,512]{2,1,0:T(8,128)(2,1)S(1)}, u32[]{:S(2)}) copy-start(bf16[16,64,512]{2,1,0:T(8,128)(2,1)S(1)} %all-to-all-done.1.message_ref) | copy-start | bytes 3145732
  116.7 29.8 %all-to-all-start.3 = ((bf16[16,64,512]{2,1,0:T(8,128)(2,1)}), bf16[16,64,512]{2,1,0:T(8,128)(2,1)S(1)}, u32[]{:S(2)}, u32[]{:S(2)}) async-start(bf16[16,64,512]{2,1,0:T(8,128)(2,1)} %bitcast.15), calls=%async_computation.3 | async-start | bytes 2097152 | tf_op jit(solution)/shard_map/all_to_all | solution.py:315
  127.8 23.9 %copy-start.6 = (bf16[512,1024]{1,0:T(8,128)(2,1)S(1)}, bf16[512,1024]{1,0:T(8,128)(2,1)}, u32[]{:S(2)}) copy-start(bf16[512,1024]{1,0:T(8,128)(2,1)} %get-tuple-element.18) | copy-start | bytes 3145732
  127.8 26.8 %collective-permute-start.2 = (bf16[512,1024]{1,0:T(8,128)(2,1)}, bf16[512,1024]{1,0:T(8,128)(2,1)S(1)}, u32[]{:S(2)}, u32[]{:S(2)}) collective-permute-start(bf16[512,1024]{1,0:T(8,128)(2,1)} %get-tuple-element.18), channel_id=1, source_target_pairs={{0,1},{1,0},{2,3},{3,2},{4,5},{5,4},{6,7},{7,6},{8,9},{9,8},{10,11... | collective-permute-start | bytes 3145736 | tf_op jit(solution)/shard_map/ppermute | solution.py:319
  146.5 1.0 copy-start.1

commit v3 on v2

--- a/solution.py
+++ b/solution.py
@@ -269,12 +269,15 @@
     return message_ref[...].reshape(targets * channels, tokens).T.astype(F32)
 
 
-def gate_kernel(
-    message_ref, key_ref, value_ref, query_ref, skip_ref, grad_ref, gated_ref, query_grad_ref
-):
+def gate_kernel(message_ref, key_ref, value_ref, query_ref, skip_ref, gated_ref):
     mixed = key_ref[...].astype(F32) * value_ref[...].astype(F32)
     conv_out = tokens_first(message_ref) + skip_ref[...] * mixed
     gated_ref[...] = (query_ref[...].astype(F32) * conv_out).astype(BF16)
+
+
+def query_grad_kernel(message_ref, key_ref, value_ref, skip_ref, grad_ref, query_grad_ref):
+    mixed = key_ref[...].astype(F32) * value_ref[...].astype(F32)
+    conv_out = tokens_first(message_ref) + skip_ref[...] * mixed
     query_grad_ref[...] = (grad_ref[...] * conv_out).astype(BF16)
 
 
@@ -360,31 +363,33 @@
         conv_held, weight_crossed = lax.optimization_barrier((conv_held, weight_crossed))
     conv_back = exchange(conv_held.reshape(message.shape))
     mixed_grad_held = convolve(grad_held.reshape(-1, tokens), tables, devices, spectrum)
+    (gated_out,) = by_blocks(
+        gate_kernel, shape, [conv_back, key_in, value_in, query_in, skip_row], [plain]
+    )
     mixed_grad_back = exchange(mixed_grad_held.reshape(message.shape))
-
-    gated_out, query_grad = by_blocks(
-        gate_kernel,
-        shape,
-        [conv_back, key_in, value_in, query_in, skip_row, grad_gated],
-        [plain, plain],
+    (query_grad,) = by_blocks(
+        query_grad_kernel, shape, [conv_back, key_in, value_in, skip_row, grad_gated], [plain]
+    )
+    own_terms = jnp.dot(
+        gated_out, weight_mine if in_pairs else out_weight, preferred_element_type=F32
     )
     if in_pairs:
         gated_other = swap_pair(gated_out)
-        mixed_out = (
-            jnp.dot(gated_out, weight_mine, preferred_element_type=F32)
-            + jnp.dot(gated_other, weight_crossed, preferred_element_type=F32)
-        ).astype(BF16)
+        own_terms, query_grad, mixed_grad_back = lax.optimization_barrier(
+            (own_terms, query_grad, mixed_grad_back)
+        )
+        mixed_out = own_terms + jnp.dot(
+            gated_other, weight_crossed, preferred_element_type=F32
+        )
     else:
-        out_terms = jnp.dot(gated_out, out_weight, preferred_element_type=F32)
-        mixed_out = lax.psum_scatter(out_terms, "ch", scatter_dimension=1, tiled=True)
-        mixed_out = mixed_out.astype(BF16)
+        mixed_out = lax.psum_scatter(own_terms, "ch", scatter_dimension=1, tiled=True)
     key_grad, value_grad = by_blocks(
         input_grad_kernel,
         shape,
         [mixed_grad_back, key_in, value_in, query_in, skip_row, grad_gated],
         [plain, plain],
     )
-    return (mixed_out, query_grad, key_grad, value_grad)
+    return (mixed_out.astype(BF16), query_grad, key_grad, value_grad)
 
 
 def solution(mesh):

time: 160 us -> 158 us (0.988)
  waiting for transfers between devices: 60.9 us -> 55 us
  Pallas kernels: 42.8 us -> 45.5 us
  matrix products: 12.5 us -> 14.5 us
    all_to_all x4, waiting for transfers between devices: 36.3 us -> 29.5 us  [exchange(): lax.all_to_all(values, 'seq', split_axis=0, concat_axis=0, tiled=True)]
    pallas_call x4 -> x5, Pallas kernels: 14.7 us -> 17.5 us  [by_blocks(): pl.pallas_call(kernel, grid=(steps,), out_shape=outs, in_specs=[spec_of(a...]
  transfers between devices with their start and end apart: 7 -> 7, of which waited for: 6 -> 7; matrix products, arithmetic and copies ran while one was open for 8% -> 9% of each run, Pallas kernels for 25% -> 27%
where the time goes in v3:
time: 158 us; the launch traced here: 157 us
  waiting for transfers between devices  55 us (35%)
  Pallas kernels  45.5 us (29%)
  starting transfers between devices  37.1 us (23%)
  matrix products  14.5 us (9%)
  local copies, waits for them, and re-layouts  4.29 us (3%)
    all_to_all x4, starting transfers between devices, exchange(): lax.all_to_all(values, 'seq', split_axis=0, concat_axis=0, tiled=True)  32.4 us
    all_to_all x4, waiting for transfers between devices, exchange(): lax.all_to_all(values, 'seq', split_axis=0, concat_axis=0, tiled=True)  29.5 us
    pallas_call x2, Pallas kernels, convolve(): pl.pallas_call(functools.partial(forward_kernel if forward else adjoint_k...  28.1 us
    ppermute x3, waiting for transfers between devices, swap_pair(): return lax.ppermute(values, 'ch', [(0, 1), (1, 0)])  25.5 us
    pallas_call x5, Pallas kernels, by_blocks(): pl.pallas_call(kernel, grid=(steps,), out_shape=outs, in_specs=[spec_of(a...  17.5 us
    dot_general x2, matrix products, project_back(): lax.dot_general(grad, weight, over_columns, preferred_element_type=F32)  5.86 us
    ppermute x3, starting transfers between devices, swap_pair(): return lax.ppermute(values, 'ch', [(0, 1), (1, 0)])  4.62 us
    dot_general x1, matrix products, on_device(): jnp.dot(gated_other, weight_crossed, preferred_element_type=F32)  4.45 us
  transfers between devices with their start and end apart: 7, of which 7 were waited for; matrix products, arithmetic and copies ran while one was open for 9% of the time, Pallas kernels for 27%

profile of v3, /device:TPU:0, one launch (start us, length us, event | category | flops | bytes accessed | tf_op | source)
XLA Modules:
  0.0 157.1 jit_solution(1168974709669789879)
XLA Ops:
  0.6 3.5 %shard_map.138 = bf16[16,128,512]{2,1,0:T(8,128)(2,1)} custom-call(bf16[512,1024]{1,0:T(8,128)(2,1)} %key_ref.7, bf16[512,1024]{1,0:T(8,128)(2,1)} %value_ref.7, f32[512,1024]{1,0:T(8,128)} %taps_ref.1), custom_call_target="tpu_custom_call" | custom-call | flops 2097152 | bytes 6291456 | tf_op jit(solution)/shard_map/pallas_call | solution.py:304
  4.1 0.0 copy-start.6
  4.1 7.5 %all-to-all-start = ((bf16[16,128,512]{2,1,0:T(8,128)(2,1)}), bf16[16,128,512]{2,1,0:T(8,128)(2,1)S(1)}, u32[]{:S(2)}, u32[]{:S(2)}) async-start(bf16[16,128,512]{2,1,0:T(8,128)(2,1)} %shard_map.138), calls=%async_computation | async-start | bytes 4194304 | tf_op jit(solution)/shard_map/all_to_all | solution.py:318
  11.6 0.0 copy-done.6
  11.7 1.6 %collective-permute-start = (bf16[512,1024]{1,0:T(8,128)(2,1)S(1)}, bf16[512,1024]{1,0:T(8,128)(2,1)}, u32[]{:S(2)}, u32[]{:S(2)}) collective-permute-start(bf16[512,1024]{1,0:T(8,128)(2,1)S(1)} %copy-done.6), channel_id=1, source_target_pairs={{0,1},{1,0},{2,3},{3,2},{4,5},{5,4},{6,7},{7,6},{8,9},{9,8},{10,11... | collective-permute-start | bytes 3145736 | tf_op jit(solution)/shard_map/ppermute | solution.py:322
  13.2 0.0 copy-start.3
  13.2 3.3 %constant_dynamic-slice_fusion = bf16[1024,1024]{1,0:T(8,128)(2,1)} fusion(bf16[1024,2048]{1,0:T(8,128)(2,1)} %param.16, s32[]{:T(128)S(6)} %select_n.6), kind=kLoop, calls=%fused_computation.8 | loop fusion | bytes 4194308 | tf_op jit(solution)/shard_map/dynamic_slice | solution.py:350
  16.5 0.0 copy-done.3
  16.6 1.3 fusion
  17.8 19.5 %collective-permute-done = bf16[512,1024]{1,0:T(8,128)(2,1)} collective-permute-done((bf16[512,1024]{1,0:T(8,128)(2,1)S(1)}, bf16[512,1024]{1,0:T(8,128)(2,1)}, u32[]{:S(2)}, u32[]{:S(2)}) %collective-permute-start) | collective-permute-done | bytes 1048608 | tf_op jit(solution)/shard_map/ppermute | solution.py:322
  37.3 1.5 collective-permute-start.1
  38.8 4.6 %bitcast_add_fusion.grad_ref.gated_ref = f32[512,1024]{1,0:T(8,128)} fusion(f32[1024,512]{0,1:T(8,128)S(1)} %fusion, bf16[512,1024]{1,0:T(8,128)(2,1)} %collective-permute-done, bf16[1024,1024]{1,0:T(8,128)(2,1)} %constant_dynamic-slice_fusion), kind=kOutput, calls=%fused_computation | convolution fusion | flops 1074266112 | bytes 7340032 | tf_op jit(solution)/shard_map/dot_general | solution.py:339
  43.4 2.8 %shard_map.141 = bf16[16,64,512]{2,1,0:T(8,128)(2,1)} custom-call(f32[512,1024]{1,0:T(8,128)} %bitcast_add_fusion.grad_ref.gated_ref, bf16[512,1024]{1,0:T(8,128)(2,1)} %query_ref.5), custom_call_target="tpu_custom_call" | custom-call | flops 2097152 | bytes 4194304 | tf_op jit(solution)/shard_map/pallas_call | solution.py:304
  46.2 6.5 %all-to-all-done = bf16[16,128,512]{2,1,0:T(8,128)(2,1)S(1)} async-done(((bf16[16,128,512]{2,1,0:T(8,128)(2,1)}), bf16[16,128,512]{2,1,0:T(8,128)(2,1)S(1)}, u32[]{:S(2)}, u32[]{:S(2)}) %all-to-all-start) | async-done | bytes 2097184 | tf_op jit(solution)/shard_map/all_to_all | solution.py:318
  52.8 0.0 copy-start.2
  52.8 11.2 %all-to-all-start.2 = ((bf16[16,64,512]{2,1,0:T(8,128)(2,1)}), bf16[16,64,512]{2,1,0:T(8,128)(2,1)S(1)}, u32[]{:S(2)}, u32[]{:S(2)}) async-start(bf16[16,64,512]{2,1,0:T(8,128)(2,1)} %shard_map.141), calls=%async_computation.2 | async-start | bytes 2097152 | tf_op jit(solution)/shard_map/all_to_all | solution.py:318
  64.0 0.0 copy-done.2
  64.0 15.8 %convolve.1 = (bf16[1024,512]{1,0:T(8,128)(2,1)}, f32[4096,256]{1,0:T(8,128)}) custom-call(bf16[2048,512]{1,0:T(8,128)(2,1)} %bitcast.13, bf16[128,128]{1,0:T(8,128)(2,1)} %constant.20.clone.enter_ref, f32[64,256]{1,0:T(8,128)} %constant.21.clone.turn_ref, bf16[1536,256]{1,0:T(8,128)(2,1)} %constant.22.clone.waves_ref, bf16[64,384]{1,0:T(8,128)(2,1)} %constant.23.clone.leave_ref), custom_call_target="tpu_custom_call" | custom-call | flops 12884901888 | bytes 8388608 | tf_op jit(solution)/shard_map/convolve/pallas_call | solution.py:224
  79.7 5.1 %collective-permute-done.1 = bf16[1024,1024]{1,0:T(8,128)(2,1)} collective-permute-done((bf16[1024,1024]{1,0:T(8,128)(2,1)}, bf16[1024,1024]{1,0:T(8,128)(2,1)}, u32[]{:S(2)}, u32[]{:S(2)}) %collective-permute-start.1) | collective-permute-done | bytes 2097184 | tf_op jit(solution)/shard_map/ppermute | solution.py:322
  84.8 2.1 %all-to-all-done.2 = bf16[16,64,512]{2,1,0:T(8,128)(2,1)S(1)} async-done(((bf16[16,64,512]{2,1,0:T(8,128)(2,1)}), bf16[16,64,512]{2,1,0:T(8,128)(2,1)S(1)}, u32[]{:S(2)}, u32[]{:S(2)}) %all-to-all-start.2) | async-done | bytes 1048608 | tf_op jit(solution)/shard_map/all_to_all | solution.py:318
  86.9 0.0 copy-start.4
  86.9 6.9 %all-to-all-start.1 = ((bf16[16,64,512]{2,1,0:T(8,128)(2,1)}), bf16[16,64,512]{2,1,0:T(8,128)(2,1)S(1)}, u32[]{:S(2)}, u32[]{:S(2)}) async-start(bf16[16,64,512]{2,1,0:T(8,128)(2,1)} %bitcast.16), calls=%async_computation.1 | async-start | bytes 2097152 | tf_op jit(solution)/shard_map/all_to_all | solution.py:318
  93.8 0.0 copy-done.4
  93.8 12.3 %correlate.1 = bf16[1024,512]{1,0:T(8,128)(2,1)} custom-call(bf16[1024,512]{1,0:T(8,128)(2,1)} %bitcast.14, bf16[128,128]{1,0:T(8,128)(2,1)} %constant.20.clone.enter_ref, f32[64,256]{1,0:T(8,128)} %constant.21.clone.turn_ref, bf16[1536,256]{1,0:T(8,128)(2,1)} %constant.22.clone.waves_ref, bf16[64,384]{1,0:T(8,128)(2,1)} %constant.23.clone.leave_ref, ...), custom_call_target="tpu_custom_call" | custom-call | flops 8589934592 | bytes 8388608 | tf_op jit(solution)/shard_map/correlate/pallas_call | solution.py:224
  106.1 10.6 %all-to-all-done.1.message_ref = bf16[16,64,512]{2,1,0:T(8,128)(2,1)S(1)} async-done(((bf16[16,64,512]{2,1,0:T(8,128)(2,1)}), bf16[16,64,512]{2,1,0:T(8,128)(2,1)S(1)}, u32[]{:S(2)}, u32[]{:S(2)}) %all-to-all-start.1) | async-done | bytes 1048608 | tf_op jit(solution)/shard_map/all_to_all | solution.py:318
  116.7 0.0 copy-start
  116.7 6.9 %all-to-all-start.3 = ((bf16[16,64,512]{2,1,0:T(8,128)(2,1)}), bf16[16,64,512]{2,1,0:T(8,128)(2,1)S(1)}, u32[]{:S(2)}, u32[]{:S(2)}) async-start(bf16[16,64,512]{2,1,0:T(8,128)(2,1)} %bitcast.15), calls=%async_computation.3 | async-start | bytes 2097152 | tf_op jit(solution)/shard_map/all_to_all | solution.py:318
  123.6 0.0 copy-done
  123.6 3.3 %shard_map.139 = bf16[512,1024]{1,0:T(8,128)(2,1)} custom-call(bf16[16,64,512]{2,1,0:T(8,128)(2,1)} %copy-done, bf16[512,1024]{1,0:T(8,128)(2,1)} %key_ref.7, bf16[512,1024]{1,0:T(8,128)(2,1)} %value_ref.7, bf16[512,1024]{1,0:T(8,128)(2,1)} %query_ref.5, f32[1,1024]{1,0:T(1,128)} %bitcast.17), custom_call_target="tpu_custom_call" | custom-call | flops 2097152 | bytes 5246976 | tf_op jit(solution)/shard_map/pallas_call | solution.py:304
  126.9 0.0 copy-start.5
  126.9 1.5 collective-permute-start.2
  128.5 3.6 %shard_map.140 = bf16[512,1024]{1,0:T(8,128)(2,1)} custom-call(bf16[16,64,512]{2,1,0:T(8,128)(2,1)} %copy-done, bf16[512,1024]{1,0:T(8,128)(2,1)} %key_ref.7, bf16[512,1024]{1,0:T(8,128)(2,1)} %value_ref.7, f32[1,1024]{1,0:T(1,128)} %bitcast.18, f32[512,1024]{1,0:T(8,128)} %bitcast_add_fusion.grad_ref.gated_ref), custom_call_target="tpu_custom_call" | custom-call | flops 2097152 | bytes 6295552 | tf_op jit(solution)/shard_map/pallas_call | solution.py:304
  132.1 0.0 copy-done.5
  132.1 4.2 %fusion.2 = f32[512,1024]{1,0:T(8,128)} fusion(bf16[512,1024]{1,0:T(8,128)(2,1)S(1)} %copy-done.5, bf16[1024,2048]{1,0:T(8,128)(2,1)} %param.16, s32[]{:T(128)S(6)} %select_n.7), kind=kOutput, calls=%fused_computation.4 | convolution fusion | flops 1073741824 | bytes 5242884 | tf_op jit(solution)/shard_map/dot_general | solution.py:373
  136.3 10.3 %all-to-all-done.3.message_ref = bf16[16,64,512]{2,1,0:T(8,128)(2,1)S(1)} async-done(((bf16[16,64,512]{2,1,0:T(8,128)(2,1)}), bf16[16,64,512]{2,1,0:T(8,128)(2,1)S(1)}, u32[]{:S(2)}, u32[]{:S(2)}) %all-to-all-start.3) | async-done | bytes 1048608 | tf_op jit(solution)/shard_map/all_to_all | solution.py:318
  146.6 0.0 copy-start.1
  146.6 1.0 copy-done.1
  147.5 4.2 %shard_map.142 = (bf16[512,1024]{1,0:T(8,128)(2,1)}, bf16[512,1024]{1,0:T(8,128)(2,1)}) custom-call(bf16[16,64,512]{2,1,0:T(8,128)(2,1)} %copy-done.1, bf16[512,1024]{1,0:T(8,128)(2,1)} %key_ref.7, bf16[512,1024]{1,0:T(8,128)(2,1)} %value_ref.7, bf16[512,1024]{1,0:T(8,128)(2,1)} %query_ref.5, f32[1,1024]{1,0:T(1,128)} %bitcast.19, ...), custom_call_target="tpu_custom_call" | custom-call | flops 2097152 | bytes 8392704 | tf_op jit(solution)/shard_map/pallas_call | solution.py:304
  151.7 0.9 collective-permute-done.2
  152.6 4.4 %add_convert_fusion = bf16[512,1024]{1,0:T(8,128)(2,1)} fusion(f32[512,1024]{1,0:T(8,128)} %fusion.2, bf16[512,1024]{1,0:T(8,128)(2,1)S(1)} %collective-permute-done.2, bf16[1024,1024]{1,0:T(8,128)(2,1)} %collective-permute-done.1), kind=kOutput, calls=%fused_computation.1 | convolution fusion | flops 1074790400 | bytes 6291456 | tf_op jit(solution)/shard_map/dot_general | solution.py:381
Async XLA Ops:
  4.1 7.5 %copy-start.6 = (bf16[512,1024]{1,0:T(8,128)(2,1)S(1)}, bf16[512,1024]{1,0:T(8,128)(2,1)}, u32[]{:S(2)}) copy-start(bf16[512,1024]{1,0:T(8,128)(2,1)} %param.17) | copy-start | bytes 3145732
  4.1 48.6 %all-to-all-start = ((bf16[16,128,512]{2,1,0:T(8,128)(2,1)}), bf16[16,128,512]{2,1,0:T(8,128)(2,1)S(1)}, u32[]{:S(2)}, u32[]{:S(2)}) async-start(bf16[16,128,512]{2,1,0:T(8,128)(2,1)} %shard_map.138), calls=%async_computation | async-start | bytes 4194304 | tf_op jit(solution)/shard_map/all_to_all | solution.py:318
  11.7 25.7 %collective-permute-start = (bf16[512,1024]{1,0:T(8,128)(2,1)S(1)}, bf16[512,1024]{1,0:T(8,128)(2,1)}, u32[]{:S(2)}, u32[]{:S(2)}) collective-permute-start(bf16[512,1024]{1,0:T(8,128)(2,1)S(1)} %copy-done.6), channel_id=1, source_target_pairs={{0,1},{1,0},{2,3},{3,2},{4,5},{5,4},{6,7},{7,6},{8,9},{9,8},{10,11... | collective-permute-start | bytes 3145736 | tf_op jit(solution)/shard_map/ppermute | solution.py:322
  13.2 3.3 %copy-start.3 = (bf16[1024,2048]{1,0:T(8,128)(2,1)S(1)}, bf16[1024,2048]{1,0:T(8,128)(2,1)}, u32[]{:S(2)}) copy-start(bf16[1024,2048]{1,0:T(8,128)(2,1)} %param.16) | copy-start | bytes 12582916
  37.3 47.5 %collective-permute-start.1 = (bf16[1024,1024]{1,0:T(8,128)(2,1)}, bf16[1024,1024]{1,0:T(8,128)(2,1)}, u32[]{:S(2)}, u32[]{:S(2)}) collective-permute-start(bf16[1024,1024]{1,0:T(8,128)(2,1)} %constant_dynamic-slice_fusion), channel_id=1, source_target_pairs={{0,1},{1,0},{2,3},{3,2},{4,5},{5,4},{6,7},{7,6},{8,9},{9,8},{10,11... | collective-permute-start | bytes 6291464 | tf_op jit(solution)/shard_map/ppermute | solution.py:322
  52.8 11.2 %copy-start.2 = (bf16[16,128,512]{2,1,0:T(8,128)(2,1)}, bf16[16,128,512]{2,1,0:T(8,128)(2,1)S(1)}, u32[]{:S(2)}) copy-start(bf16[16,128,512]{2,1,0:T(8,128)(2,1)S(1)} %all-to-all-done) | copy-start | bytes 6291460
  52.8 34.2 %all-to-all-start.2 = ((bf16[16,64,512]{2,1,0:T(8,128)(2,1)}), bf16[16,64,512]{2,1,0:T(8,128)(2,1)S(1)}, u32[]{:S(2)}, u32[]{:S(2)}) async-start(bf16[16,64,512]{2,1,0:T(8,128)(2,1)} %shard_map.141), calls=%async_computation.2 | async-start | bytes 2097152 | tf_op jit(solution)/shard_map/all_to_all | solution.py:318
  86.9 6.9 %copy-start.4 = (bf16[16,64,512]{2,1,0:T(8,128)(2,1)}, bf16[16,64,512]{2,1,0:T(8,128)(2,1)S(1)}, u32[]{:S(2)}) copy-start(bf16[16,64,512]{2,1,0:T(8,128)(2,1)S(1)} %all-to-all-done.2) | copy-start | bytes 3145732
  86.9 29.8 %all-to-all-start.1 = ((bf16[16,64,512]{2,1,0:T(8,128)(2,1)}), bf16[16,64,512]{2,1,0:T(8,128)(2,1)S(1)}, u32[]{:S(2)}, u32[]{:S(2)}) async-start(bf16[16,64,512]{2,1,0:T(8,128)(2,1)} %bitcast.16), calls=%async_computation.1 | async-start | bytes 2097152 | tf_op jit(solution)/shard_map/all_to_all | solution.py:318
  116.7 6.9 %copy-start = (bf16[16,64,512]{2,1,0:T(8,128)(2,1)}, bf16[16,64,512]{2,1,0:T(8,128)(2,1)S(1)}, u32[]{:S(2)}) copy-start(bf16[16,64,512]{2,1,0:T(8,128)(2,1)S(1)} %all-to-all-done.1.message_ref) | copy-start | bytes 3145732
  116.7 29.8 %all-to-all-start.3 = ((bf16[16,64,512]{2,1,0:T(8,128)(2,1)}), bf16[16,64,512]{2,1,0:T(8,128)(2,1)S(1)}, u32[]{:S(2)}, u32[]{:S(2)}) async-start(bf16[16,64,512]{2,1,0:T(8,128)(2,1)} %bitcast.15), calls=%async_computation.3 | async-start | bytes 2097152 | tf_op jit(solution)/shard_map/all_to_all | solution.py:318
  126.9 5.1 %copy-start.5 = (bf16[512,1024]{1,0:T(8,128)(2,1)S(1)}, bf16[512,1024]{1,0:T(8,128)(2,1)}, u32[]{:S(2)}) copy-start(bf16[512,1024]{1,0:T(8,128)(2,1)} %shard_map.139) | copy-start | bytes 3145732
  126.9 25.7 %collective-permute-start.2 = (bf16[512,1024]{1,0:T(8,128)(2,1)}, bf16[512,1024]{1,0:T(8,128)(2,1)S(1)}, u32[]{:S(2)}, u32[]{:S(2)}) collective-permute-start(bf16[512,1024]{1,0:T(8,128)(2,1)} %shard_map.139), channel_id=1, source_target_pairs={{0,1},{1,0},{2,3},{3,2},{4,5},{5,4},{6,7},{7,6},{8,9},{9,8},{10,11... | collective-permute-start | bytes 3145736 | tf_op jit(solution)/shard_map/ppermute | solution.py:322
  146.6 1.0 copy-start.1

commit v4 on v3

--- a/solution.py
+++ b/solution.py
@@ -205,6 +205,7 @@
 GROUP = 16
 WIDTH = 512
 VMEM_LIMIT = 60 * 1024 * 1024
+LAST_LIMIT = 48 * 1024 * 1024
 
 
 def whole_block(array):
@@ -275,42 +276,86 @@
     gated_ref[...] = (query_ref[...].astype(F32) * conv_out).astype(BF16)
 
 
-def query_grad_kernel(message_ref, key_ref, value_ref, skip_ref, grad_ref, query_grad_ref):
+def query_grad_kernel(
+    message_ref, key_ref, value_ref, query_ref, skip_ref, grad_ref, query_grad_ref, near_ref
+):
+    width = key_ref.shape[1]
+    for at, ref in enumerate((key_ref, value_ref, query_ref)):
+        near_ref[:, at * width : (at + 1) * width] = ref[...]
     mixed = key_ref[...].astype(F32) * value_ref[...].astype(F32)
     conv_out = tokens_first(message_ref) + skip_ref[...] * mixed
     query_grad_ref[...] = (grad_ref[...] * conv_out).astype(BF16)
 
 
 def input_grad_kernel(
-    message_ref, key_ref, value_ref, query_ref, skip_ref, grad_ref, key_grad_ref, value_grad_ref
+    message_ref, near_ref, skip_ref, grad_ref, key_grad_ref, value_grad_ref
 ):
-    grad_conv = grad_ref[...] * query_ref[...].astype(F32)
-    grad_mixed = tokens_first(message_ref) + skip_ref[...] * grad_conv
-    key_grad_ref[...] = (grad_mixed * value_ref[...].astype(F32)).astype(BF16)
-    value_grad_ref[...] = (grad_mixed * key_ref[...].astype(F32)).astype(BF16)
-
-
-def by_blocks(kernel, shape, inputs, outs):
+    width = grad_ref.shape[1]
+    key, value, query = (
+        near_ref[:, at * width : (at + 1) * width].astype(F32) for at in range(3)
+    )
+    grad_mixed = tokens_first(message_ref) + skip_ref[...] * (grad_ref[...] * query)
+    key_grad_ref[...] = (grad_mixed * value).astype(BF16)
+    value_grad_ref[...] = (grad_mixed * key).astype(BF16)
+
+
+def project_kernel(terms_ref, gated_ref, weight_ref, out_ref):
+    total = terms_ref[...] + mxu(gated_ref[...], weight_ref[...])
+    out_ref[...] = total.astype(out_ref.dtype)
+
+
+def project(terms, gated, weight, at, kind):
+    tokens, depth = gated.shape
+    width = math.gcd(terms.shape[1], WIDTH)
+    block = pl.BlockSpec((tokens, width), lambda j: (0, j))
+    return pl.pallas_call(
+        project_kernel,
+        grid=(terms.shape[1] // width,),
+        out_shape=jax.ShapeDtypeStruct(terms.shape, kind),
+        in_specs=[
+            block,
+            pl.BlockSpec((tokens, depth), lambda j: (0, 0)),
+            pl.BlockSpec((depth, width), lambda j: (at, j)),
+        ],
+        out_specs=block,
+        cost_estimate=pl.CostEstimate(
+            flops=2 * tokens * depth * terms.shape[1],
+            bytes_accessed=6 * terms.size,
+            transcendentals=0,
+        ),
+        compiler_params=pltpu.CompilerParams(vmem_limit_bytes=VMEM_LIMIT),
+        name="project",
+    )(terms, gated, weight)
+
+
+def by_blocks(kernel, shape, inputs, outs, only=None, vmem_limit=None):
     tokens, channels = shape
     steps = channels // math.gcd(channels, WIDTH)
+    width = channels // steps
 
     def spec_of(array):
+        def at(j):
+            return j if only is None or array.shape[-1] == width else only
+
         if len(array.shape) == 3:
             targets, rows, _ = array.shape
-            return pl.BlockSpec((targets // steps, rows, tokens), lambda j: (j, 0, 0))
-        return pl.BlockSpec((array.shape[0], channels // steps), lambda j: (0, j))
+            return pl.BlockSpec(
+                (targets // steps, rows, tokens), lambda j: (j if only is None else only, 0, 0)
+            )
+        size = width if only is not None else array.shape[1] // steps
+        return pl.BlockSpec((array.shape[0], size), lambda j: (0, at(j)))
 
     moved = sum(a.size * a.dtype.itemsize for a in list(inputs) + list(outs))
     return pl.pallas_call(
         kernel,
-        grid=(steps,),
+        grid=(steps if only is None else 1,),
         out_shape=outs,
         in_specs=[spec_of(a) for a in inputs],
         out_specs=[spec_of(a) for a in outs],
         cost_estimate=pl.CostEstimate(
             flops=4 * tokens * channels, bytes_accessed=moved, transcendentals=0
         ),
-        compiler_params=pltpu.CompilerParams(vmem_limit_bytes=VMEM_LIMIT),
+        compiler_params=pltpu.CompilerParams(vmem_limit_bytes=vmem_limit or VMEM_LIMIT),
     )(*inputs)
 
 
@@ -363,32 +408,43 @@
         conv_held, weight_crossed = lax.optimization_barrier((conv_held, weight_crossed))
     conv_back = exchange(conv_held.reshape(message.shape))
     mixed_grad_held = convolve(grad_held.reshape(-1, tokens), tables, devices, spectrum)
-    (gated_out,) = by_blocks(
-        gate_kernel, shape, [conv_back, key_in, value_in, query_in, skip_row], [plain]
-    )
+    triple = jax.ShapeDtypeStruct((tokens, 3 * channels), BF16)
+    gate_inputs = [conv_back, key_in, value_in, query_in, skip_row]
+    if in_pairs:
+        half = math.gcd(channels, WIDTH)
+        gated = []
+        for at in range(channels // half):
+            block = jax.ShapeDtypeStruct((tokens, half), BF16)
+            gated += by_blocks(gate_kernel, shape, gate_inputs, [block], only=at)
+        crossed = [swap_pair(block) for block in gated]
+        gated_out = jnp.concatenate(gated, axis=1)
+    else:
+        (gated_out,) = by_blocks(gate_kernel, shape, gate_inputs, [plain])
     mixed_grad_back = exchange(mixed_grad_held.reshape(message.shape))
-    (query_grad,) = by_blocks(
-        query_grad_kernel, shape, [conv_back, key_in, value_in, skip_row, grad_gated], [plain]
-    )
-    own_terms = jnp.dot(
-        gated_out, weight_mine if in_pairs else out_weight, preferred_element_type=F32
-    )
-    if in_pairs:
-        gated_other = swap_pair(gated_out)
-        own_terms, query_grad, mixed_grad_back = lax.optimization_barrier(
-            (own_terms, query_grad, mixed_grad_back)
+    query_grad, near = by_blocks(
+        query_grad_kernel, shape, gate_inputs + [grad_gated], [plain, triple], vmem_limit=LAST_LIMIT
+    )
+    if in_pairs:
+        terms = jnp.dot(gated_out, weight_mine, preferred_element_type=F32)
+        for at, block in enumerate(crossed[:-1]):
+            rows = weight_crossed[at * half : (at + 1) * half, :]
+            terms += jnp.dot(block, rows, preferred_element_type=F32)
+        terms, query_grad, mixed_grad_back = lax.optimization_barrier(
+            (terms, query_grad, mixed_grad_back)
         )
-        mixed_out = own_terms + jnp.dot(
-            gated_other, weight_crossed, preferred_element_type=F32
-        )
-    else:
-        mixed_out = lax.psum_scatter(own_terms, "ch", scatter_dimension=1, tiled=True)
     key_grad, value_grad = by_blocks(
         input_grad_kernel,
         shape,
-        [mixed_grad_back, key_in, value_in, query_in, skip_row, grad_gated],
+        [mixed_grad_back, near, skip_row, grad_gated],
         [plain, plain],
-    )
+        vmem_limit=LAST_LIMIT,
+    )
+    if in_pairs:
+        terms, key_grad, value_grad = lax.optimization_barrier((terms, key_grad, value_grad))
+        mixed_out = project(terms, crossed[-1], weight_crossed, len(crossed) - 1, BF16)
+    else:
+        own_terms = jnp.dot(gated_out, out_weight, preferred_element_type=F32)
+        mixed_out = lax.psum_scatter(own_terms, "ch", scatter_dimension=1, tiled=True)
     return (mixed_out.astype(BF16), query_grad, key_grad, value_grad)
 
 

time: 158 us -> 156 us (0.987)
  matrix products: 14.5 us -> 8.97 us
  Pallas kernels: 45.5 us -> 50.2 us
  waiting for transfers between devices: 55 us -> 52.9 us
    all_to_all x4, waiting for transfers between devices: 29.5 us -> 23.3 us  [exchange(): lax.all_to_all(values, 'seq', split_axis=0, concat_axis=0, tiled=True)]
    dot_general x2, matrix products: 8.63 us -> 3.39 us  [the longest x1 2.13 us: on_device(): terms += jnp.dot(block, rows, preferred_element_type=F32)]
    pallas_call x5 -> x7, Pallas kernels: 17.5 us -> 22.3 us  [the longest x6 19 us: by_blocks(): pl.pallas_call(kernel, grid=(steps if only is None else 1,), out_shape=ou...]
    ppermute x3 -> x4, waiting for transfers between devices: 25.5 us -> 29.6 us  [swap_pair(): return lax.ppermute(values, 'ch', [(0, 1), (1, 0)])]
    ppermute x3 -> x4, starting transfers between devices: 4.62 us -> 5.48 us  [swap_pair(): return lax.ppermute(values, 'ch', [(0, 1), (1, 0)])]
  transfers between devices with their start and end apart: 7 -> 8, of which waited for: 7 -> 8; matrix products, arithmetic and copies ran while one was open for 9% -> 8% of each run, Pallas kernels for 27% -> 28%
where the time goes in v4:
time: 156 us; the launch traced here: 155 us
  waiting for transfers between devices  52.9 us (34%)
  Pallas kernels  50.2 us (32%)
  starting transfers between devices  38 us (24%)
  matrix products  8.97 us (6%)
  local copies, waits for them, and re-layouts  4.56 us (3%)
    all_to_all x4, starting transfers between devices, exchange(): lax.all_to_all(values, 'seq', split_axis=0, concat_axis=0, tiled=True)  32.5 us
    ppermute x4, waiting for transfers between devices, swap_pair(): return lax.ppermute(values, 'ch', [(0, 1), (1, 0)])  29.6 us
    pallas_call x2, Pallas kernels, convolve(): pl.pallas_call(functools.partial(forward_kernel if forward else adjoint_k...  27.9 us
    all_to_all x4, waiting for transfers between devices, exchange(): lax.all_to_all(values, 'seq', split_axis=0, concat_axis=0, tiled=True)  23.3 us
    pallas_call x6, Pallas kernels, by_blocks(): pl.pallas_call(kernel, grid=(steps if only is None else 1,), out_shape=ou...  19 us
    dot_general x2, matrix products, project_back(): lax.dot_general(grad, weight, over_columns, preferred_element_type=F32)  5.58 us
    ppermute x4, starting transfers between devices, swap_pair(): return lax.ppermute(values, 'ch', [(0, 1), (1, 0)])  5.48 us
    dynamic_slice x1, local copies, waits for them, and re-layouts, on_device(): weight_other = lax.dynamic_slice_in_dim(out_weight, other, channels, axis=1)  3.29 us
  transfers between devices with their start and end apart: 8, of which 8 were waited for; matrix products, arithmetic and copies ran while one was open for 8% of the time, Pallas kernels for 28%

profile of v4, /device:TPU:0, one launch (start us, length us, event | category | flops | bytes accessed | tf_op | source)
XLA Modules:
  0.0 155.4 jit_solution(5964099244269286685)
XLA Ops:
  0.6 3.5 %shard_map.138 = bf16[16,128,512]{2,1,0:T(8,128)(2,1)} custom-call(bf16[512,1024]{1,0:T(8,128)(2,1)} %key_ref.7, bf16[512,1024]{1,0:T(8,128)(2,1)} %value_ref.7, f32[512,1024]{1,0:T(8,128)} %taps_ref.1), custom_call_target="tpu_custom_call" | custom-call | flops 2097152 | bytes 6291456 | tf_op jit(solution)/shard_map/pallas_call | solution.py:349
  4.1 0.0 copy-start.14
  4.1 7.5 %all-to-all-start = ((bf16[16,128,512]{2,1,0:T(8,128)(2,1)}), bf16[16,128,512]{2,1,0:T(8,128)(2,1)}, u32[]{:S(2)}, u32[]{:S(2)}) async-start(bf16[16,128,512]{2,1,0:T(8,128)(2,1)} %shard_map.138), calls=%async_computation | async-start | bytes 4194304 | tf_op jit(solution)/shard_map/all_to_all | solution.py:363
  11.7 0.0 copy-done.14
  11.7 1.6 %collective-permute-start = (bf16[512,1024]{1,0:T(8,128)(2,1)S(1)}, bf16[512,1024]{1,0:T(8,128)(2,1)S(1)}, u32[]{:S(2)}, u32[]{:S(2)}) collective-permute-start(bf16[512,1024]{1,0:T(8,128)(2,1)S(1)} %copy-done.14), channel_id=1, source_target_pairs={{0,1},{1,0},{2,3},{3,2},{4,5},{5,4},{6,7},{7,6},{8,9},{9,8},{10,11... | collective-permute-start | bytes 3145736 | tf_op jit(solution)/shard_map/ppermute | solution.py:367
  13.3 0.0 copy-start.9
  13.3 3.3 %constant_dynamic-slice_fusion = bf16[1024,1024]{1,0:T(8,128)(2,1)} fusion(bf16[1024,2048]{1,0:T(8,128)(2,1)} %param.16, s32[]{:T(128)S(6)} %select_n.6), kind=kLoop, calls=%fused_computation.12 | loop fusion | bytes 4194308 | tf_op jit(solution)/shard_map/dynamic_slice | solution.py:395
  16.6 0.0 copy-done.9
  16.6 1.3 fusion
  17.9 19.3 %collective-permute-done = bf16[512,1024]{1,0:T(8,128)(2,1)S(1)} collective-permute-done((bf16[512,1024]{1,0:T(8,128)(2,1)S(1)}, bf16[512,1024]{1,0:T(8,128)(2,1)S(1)}, u32[]{:S(2)}, u32[]{:S(2)}) %collective-permute-start) | collective-permute-done | bytes 1048608 | tf_op jit(solution)/shard_map/ppermute | solution.py:367
  37.2 1.5 collective-permute-start.1
  38.7 4.3 %bitcast_add_fusion.grad_ref.gated_ref = f32[512,1024]{1,0:T(8,128)} fusion(f32[1024,512]{0,1:T(8,128)S(1)} %fusion, bf16[512,1024]{1,0:T(8,128)(2,1)S(1)} %collective-permute-done, bf16[1024,1024]{1,0:T(8,128)(2,1)} %constant_dynamic-slice_fusion), kind=kOutput, calls=%fused_computation | convolution fusion | flops 1074266112 | bytes 7340032 | tf_op jit(solution)/shard_map/dot_general | solution.py:384
  43.0 2.8 %shard_map.142 = bf16[16,64,512]{2,1,0:T(8,128)(2,1)} custom-call(f32[512,1024]{1,0:T(8,128)} %bitcast_add_fusion.grad_ref.gated_ref, bf16[512,1024]{1,0:T(8,128)(2,1)} %query_ref.7), custom_call_target="tpu_custom_call" | custom-call | flops 2097152 | bytes 4194304 | tf_op jit(solution)/shard_map/pallas_call | solution.py:349
  45.8 7.0 %all-to-all-done = bf16[16,128,512]{2,1,0:T(8,128)(2,1)} async-done(((bf16[16,128,512]{2,1,0:T(8,128)(2,1)}), bf16[16,128,512]{2,1,0:T(8,128)(2,1)}, u32[]{:S(2)}, u32[]{:S(2)}) %all-to-all-start) | async-done | bytes 2097184 | tf_op jit(solution)/shard_map/all_to_all | solution.py:363
  52.8 11.2 %all-to-all-start.2 = ((bf16[16,64,512]{2,1,0:T(8,128)(2,1)}), bf16[16,64,512]{2,1,0:T(8,128)(2,1)S(1)}, u32[]{:S(2)}, u32[]{:S(2)}) async-start(bf16[16,64,512]{2,1,0:T(8,128)(2,1)} %shard_map.142), calls=%async_computation.2 | async-start | bytes 2097152 | tf_op jit(solution)/shard_map/all_to_all | solution.py:363
  64.0 15.7 %convolve.1 = (bf16[1024,512]{1,0:T(8,128)(2,1)}, f32[4096,256]{1,0:T(8,128)}) custom-call(bf16[2048,512]{1,0:T(8,128)(2,1)} %bitcast.held_ref, bf16[128,128]{1,0:T(8,128)(2,1)} %constant.20.clone.enter_ref, f32[64,256]{1,0:T(8,128)} %constant.21.clone.turn_ref, bf16[1536,256]{1,0:T(8,128)(2,1)} %constant.22.clone.waves_ref, ...), custom_call_target="tpu_custom_call" | custom-call | flops 12884901888 | bytes 8388608 | tf_op jit(solution)/shard_map/convolve/pallas_call | solution.py:225
  79.8 4.8 %collective-permute-done.1.weight_ref = bf16[1024,1024]{1,0:T(8,128)(2,1)S(1)} collective-permute-done((bf16[1024,1024]{1,0:T(8,128)(2,1)}, bf16[1024,1024]{1,0:T(8,128)(2,1)S(1)}, u32[]{:S(2)}, u32[]{:S(2)}) %collective-permute-start.1) | collective-permute-done | bytes 2097184 | tf_op jit(solution)/shard_map/ppermute | solution.py:367
  84.6 0.0 copy-start.7
  84.6 2.4 %all-to-all-done.2 = bf16[16,64,512]{2,1,0:T(8,128)(2,1)S(1)} async-done(((bf16[16,64,512]{2,1,0:T(8,128)(2,1)}), bf16[16,64,512]{2,1,0:T(8,128)(2,1)S(1)}, u32[]{:S(2)}, u32[]{:S(2)}) %all-to-all-start.2) | async-done | bytes 1048608 | tf_op jit(solution)/shard_map/all_to_all | solution.py:363
  87.0 0.0 copy-start.11
  87.0 0.0 copy-done.7
  87.0 6.9 %all-to-all-start.1 = ((bf16[16,64,512]{2,1,0:T(8,128)(2,1)}), bf16[16,64,512]{2,1,0:T(8,128)(2,1)S(1)}, u32[]{:S(2)}, u32[]{:S(2)}) async-start(bf16[16,64,512]{2,1,0:T(8,128)(2,1)} %bitcast.17), calls=%async_computation.1 | async-start | bytes 2097152 | tf_op jit(solution)/shard_map/all_to_all | solution.py:363
  93.9 0.0 copy-done.11
  93.9 12.2 %correlate.1 = bf16[1024,512]{1,0:T(8,128)(2,1)} custom-call(bf16[1024,512]{1,0:T(8,128)(2,1)} %bitcast.16, bf16[128,128]{1,0:T(8,128)(2,1)} %constant.20.clone.enter_ref, f32[64,256]{1,0:T(8,128)} %constant.21.clone.turn_ref, bf16[1536,256]{1,0:T(8,128)(2,1)} %constant.22.clone.waves_ref, bf16[64,384]{1,0:T(8,128)(2,1)} %constant.23.clone.leave_ref, ...), custom_call_target="tpu_custom_call" | custom-call | flops 8589934592 | bytes 8388608 | tf_op jit(solution)/shard_map/correlate/pallas_call | solution.py:225
  106.1 10.7 %all-to-all-done.1.message_ref = bf16[16,64,512]{2,1,0:T(8,128)(2,1)S(1)} async-done(((bf16[16,64,512]{2,1,0:T(8,128)(2,1)}), bf16[16,64,512]{2,1,0:T(8,128)(2,1)S(1)}, u32[]{:S(2)}, u32[]{:S(2)}) %all-to-all-start.1) | async-done | bytes 1048608 | tf_op jit(solution)/shard_map/all_to_all | solution.py:363
  116.8 0.0 copy-start.1
  116.8 6.9 %all-to-all-start.3 = ((bf16[16,64,512]{2,1,0:T(8,128)(2,1)}), bf16[16,64,512]{2,1,0:T(8,128)(2,1)}, u32[]{:S(2)}, u32[]{:S(2)}) async-start(bf16[16,64,512]{2,1,0:T(8,128)(2,1)} %bitcast.15), calls=%async_computation.3 | async-start | bytes 2097152 | tf_op jit(solution)/shard_map/all_to_all | solution.py:363
  123.7 0.0 copy-done.1
  123.8 2.6 %shard_map.139 = bf16[512,512]{1,0:T(8,128)(2,1)} custom-call(bf16[16,64,512]{2,1,0:T(8,128)(2,1)} %copy-done.1, bf16[512,1024]{1,0:T(8,128)(2,1)} %key_ref.7, bf16[512,1024]{1,0:T(8,128)(2,1)} %value_ref.7, bf16[512,1024]{1,0:T(8,128)(2,1)} %query_ref.7, f32[1,1024]{1,0:T(1,128)} %bitcast.11), custom_call_target="tpu_custom_call" | custom-call | flops 2097152 | bytes 4722688 | tf_op jit(solution)/shard_map/pallas_call | solution.py:349
  126.4 0.0 copy-start.2
  126.4 0.0 copy-start.3
  126.4 0.0 copy-start.4
  126.4 0.0 copy-start.6
  126.4 1.6 %collective-permute-start.2 = (bf16[512,512]{1,0:T(8,128)(2,1)}, bf16[512,512]{1,0:T(8,128)(2,1)S(1)}, u32[]{:S(2)}, u32[]{:S(2)}) collective-permute-start(bf16[512,512]{1,0:T(8,128)(2,1)} %shard_map.139), channel_id=1, source_target_pairs={{0,1},{1,0},{2,3},{3,2},{4,5},{5,4},{6,7},{7,6},{8,9},{9,8},{10,11... | collective-permute-start | bytes 1572872 | tf_op jit(solution)/shard_map/ppermute | solution.py:367
  128.0 2.6 %shard_map.140 = bf16[512,512]{1,0:T(8,128)(2,1)} custom-call(bf16[16,64,512]{2,1,0:T(8,128)(2,1)} %copy-done.1, bf16[512,1024]{1,0:T(8,128)(2,1)} %key_ref.7, bf16[512,1024]{1,0:T(8,128)(2,1)} %value_ref.7, bf16[512,1024]{1,0:T(8,128)(2,1)} %query_ref.7, f32[1,1024]{1,0:T(1,128)} %bitcast.12), custom_call_target="tpu_custom_call" | custom-call | flops 2097152 | bytes 4722688 | tf_op jit(solution)/shard_map/pallas_call | solution.py:349
  130.6 0.8 collective-permute-start.3
  131.4 0.0 copy-done.2
  131.4 0.0 copy-done.3
  131.4 0.0 copy-done.4
  131.4 0.0 copy-done.6
  131.4 0.0 copy-start.5
  131.4 1.2 copy-done.5
  132.6 0.0 copy-start.10
  132.6 0.0 copy-start.12
  132.7 0.0 copy-start.13
  132.7 3.9 %shard_map.141 = (bf16[512,1024]{1,0:T(8,128)(2,1)}, bf16[512,3072]{1,0:T(8,128)(2,1)}) custom-call(bf16[16,64,512]{2,1,0:T(8,128)(2,1)S(1)} %copy-done.2, bf16[512,1024]{1,0:T(8,128)(2,1)S(1)} %copy-done.3, bf16[512,1024]{1,0:T(8,128)(2,1)S(1)} %copy-done.4, bf16[512,1024]{1,0:T(8,128)(2,1)S(1)} %copy-done.5, f32[1,1024]{1,0:T(1,128)S(1)} %bitcast.13, ...), custom_call_target="tpu_custom_call" | custom-call | flops 2097152 | bytes 10489856 | tf_op jit(solution)/shard_map/pallas_call | solution.py:349
  136.5 0.0 copy-done.10
  136.5 0.0 copy-done.12
  136.5 0.0 copy-done.13
  136.6 0.0 copy-start.8
  136.6 1.3 fusion.2
  137.8 0.0 copy-start
  137.8 3.6 %collective-permute-done.2 = bf16[512,512]{1,0:T(8,128)(2,1)S(1)} collective-permute-done((bf16[512,512]{1,0:T(8,128)(2,1)}, bf16[512,512]{1,0:T(8,128)(2,1)S(1)}, u32[]{:S(2)}, u32[]{:S(2)}) %collective-permute-start.2) | collective-permute-done | bytes 524320 | tf_op jit(solution)/shard_map/ppermute | solution.py:367
  141.4 0.0 copy-done.8
  141.4 2.1 %convolution_add_fusion.terms_ref = f32[512,1024]{1,0:T(8,128)} fusion(f32[512,1024]{1,0:T(8,128)S(1)} %fusion.2, bf16[512,512]{1,0:T(8,128)(2,1)S(1)} %collective-permute-done.2, bf16[1024,1024]{1,0:T(8,128)(2,1)S(1)} %copy-done.8), kind=kOutput, calls=%fused_computation.5 | convolution fusion | flops 537395200 | bytes 5767168 | tf_op jit(solution)/shard_map/dot_general | solution.py:431
  143.6 3.2 %all-to-all-done.3.message_ref = bf16[16,64,512]{2,1,0:T(8,128)(2,1)} async-done(((bf16[16,64,512]{2,1,0:T(8,128)(2,1)}), bf16[16,64,512]{2,1,0:T(8,128)(2,1)}, u32[]{:S(2)}, u32[]{:S(2)}) %all-to-all-start.3) | async-done | bytes 1048608 | tf_op jit(solution)/shard_map/all_to_all | solution.py:363
  146.7 0.0 copy-done
  146.7 3.6 %shard_map.143 = (bf16[512,1024]{1,0:T(8,128)(2,1)}, bf16[512,1024]{1,0:T(8,128)(2,1)}) custom-call(bf16[16,64,512]{2,1,0:T(8,128)(2,1)} %all-to-all-done.3.message_ref, bf16[512,3072]{1,0:T(8,128)(2,1)} %get-tuple-element.29.near_ref, f32[1,1024]{1,0:T(1,128)S(1)} %bitcast.14, f32[512,1024]{1,0:T(8,128)S(1)} %copy-done), custom_call_target="tpu_custom_call" | custom-call | flops 2097152 | bytes 8392704 | tf_op jit(solution)/shard_map/pallas_call | solution.py:349
  150.3 1.9 %collective-permute-done.3.gated_ref = bf16[512,512]{1,0:T(8,128)(2,1)} collective-permute-done((bf16[512,512]{1,0:T(8,128)(2,1)}, bf16[512,512]{1,0:T(8,128)(2,1)}, u32[]{:S(2)}, u32[]{:S(2)}) %collective-permute-start.3) | collective-permute-done | bytes 524320 | tf_op jit(solution)/shard_map/ppermute | solution.py:367
  152.2 3.2 %project.1 = bf16[512,1024]{1,0:T(8,128)(2,1)} custom-call(f32[512,1024]{1,0:T(8,128)} %convolution_add_fusion.terms_ref, bf16[512,512]{1,0:T(8,128)(2,1)} %collective-permute-done.3.gated_ref, bf16[1024,1024]{1,0:T(8,128)(2,1)} %copy-done.7), custom_call_target="tpu_custom_call" | custom-call | flops 536870912 | bytes 3145728 | tf_op jit(solution)/shard_map/project/pallas_call | solution.py:311
Async XLA Ops:
  4.1 7.6 %copy-start.14 = (bf16[512,1024]{1,0:T(8,128)(2,1)S(1)}, bf16[512,1024]{1,0:T(8,128)(2,1)}, u32[]{:S(2)}) copy-start(bf16[512,1024]{1,0:T(8,128)(2,1)} %param.17) | copy-start | bytes 3145732
  4.1 48.7 %all-to-all-start = ((bf16[16,128,512]{2,1,0:T(8,128)(2,1)}), bf16[16,128,512]{2,1,0:T(8,128)(2,1)}, u32[]{:S(2)}, u32[]{:S(2)}) async-start(bf16[16,128,512]{2,1,0:T(8,128)(2,1)} %shard_map.138), calls=%async_computation | async-start | bytes 4194304 | tf_op jit(solution)/shard_map/all_to_all | solution.py:363
  11.7 25.5 %collective-permute-start = (bf16[512,1024]{1,0:T(8,128)(2,1)S(1)}, bf16[512,1024]{1,0:T(8,128)(2,1)S(1)}, u32[]{:S(2)}, u32[]{:S(2)}) collective-permute-start(bf16[512,1024]{1,0:T(8,128)(2,1)S(1)} %copy-done.14), channel_id=1, source_target_pairs={{0,1},{1,0},{2,3},{3,2},{4,5},{5,4},{6,7},{7,6},{8,9},{9,8},{10,11... | collective-permute-start | bytes 3145736 | tf_op jit(solution)/shard_map/ppermute | solution.py:367
  13.3 3.3 %copy-start.9 = (bf16[1024,2048]{1,0:T(8,128)(2,1)S(1)}, bf16[1024,2048]{1,0:T(8,128)(2,1)}, u32[]{:S(2)}) copy-start(bf16[1024,2048]{1,0:T(8,128)(2,1)} %param.16) | copy-start | bytes 12582916
  37.2 47.4 %collective-permute-start.1 = (bf16[1024,1024]{1,0:T(8,128)(2,1)}, bf16[1024,1024]{1,0:T(8,128)(2,1)S(1)}, u32[]{:S(2)}, u32[]{:S(2)}) collective-permute-start(bf16[1024,1024]{1,0:T(8,128)(2,1)} %constant_dynamic-slice_fusion), channel_id=1, source_target_pairs={{0,1},{1,0},{2,3},{3,2},{4,5},{5,4},{6,7},{7,6},{8,9},{9,8},{10,11... | collective-permute-start | bytes 6291464 | tf_op jit(solution)/shard_map/ppermute | solution.py:367
  52.8 34.2 %all-to-all-start.2 = ((bf16[16,64,512]{2,1,0:T(8,128)(2,1)}), bf16[16,64,512]{2,1,0:T(8,128)(2,1)S(1)}, u32[]{:S(2)}, u32[]{:S(2)}) async-start(bf16[16,64,512]{2,1,0:T(8,128)(2,1)} %shard_map.142), calls=%async_computation.2 | async-start | bytes 2097152 | tf_op jit(solution)/shard_map/all_to_all | solution.py:363
  84.6 2.4 %copy-start.7 = (bf16[1024,1024]{1,0:T(8,128)(2,1)}, bf16[1024,1024]{1,0:T(8,128)(2,1)S(1)}, u32[]{:S(2)}) copy-start(bf16[1024,1024]{1,0:T(8,128)(2,1)S(1)} %collective-permute-done.1.weight_ref) | copy-start | bytes 6291460
  87.0 6.9 %copy-start.11 = (bf16[16,64,512]{2,1,0:T(8,128)(2,1)}, bf16[16,64,512]{2,1,0:T(8,128)(2,1)S(1)}, u32[]{:S(2)}) copy-start(bf16[16,64,512]{2,1,0:T(8,128)(2,1)S(1)} %all-to-all-done.2) | copy-start | bytes 3145732
  87.0 29.8 %all-to-all-start.1 = ((bf16[16,64,512]{2,1,0:T(8,128)(2,1)}), bf16[16,64,512]{2,1,0:T(8,128)(2,1)S(1)}, u32[]{:S(2)}, u32[]{:S(2)}) async-start(bf16[16,64,512]{2,1,0:T(8,128)(2,1)} %bitcast.17), calls=%async_computation.1 | async-start | bytes 2097152 | tf_op jit(solution)/shard_map/all_to_all | solution.py:363
  116.8 6.9 %copy-start.1 = (bf16[16,64,512]{2,1,0:T(8,128)(2,1)}, bf16[16,64,512]{2,1,0:T(8,128)(2,1)S(1)}, u32[]{:S(2)}) copy-start(bf16[16,64,512]{2,1,0:T(8,128)(2,1)S(1)} %all-to-all-done.1.message_ref) | copy-start | bytes 3145732
  116.8 29.9 %all-to-all-start.3 = ((bf16[16,64,512]{2,1,0:T(8,128)(2,1)}), bf16[16,64,512]{2,1,0:T(8,128)(2,1)}, u32[]{:S(2)}, u32[]{:S(2)}) async-start(bf16[16,64,512]{2,1,0:T(8,128)(2,1)} %bitcast.15), calls=%async_computation.3 | async-start | bytes 2097152 | tf_op jit(solution)/shard_map/all_to_all | solution.py:363
  126.4 5.0 %copy-start.2 = (bf16[16,64,512]{2,1,0:T(8,128)(2,1)S(1)}, bf16[16,64,512]{2,1,0:T(8,128)(2,1)}, u32[]{:S(2)}) copy-start(bf16[16,64,512]{2,1,0:T(8,128)(2,1)} %copy-done.1) | copy-start | bytes 3145732
  126.4 5.0 %copy-start.3 = (bf16[512,1024]{1,0:T(8,128)(2,1)S(1)}, bf16[512,1024]{1,0:T(8,128)(2,1)}, u32[]{:S(2)}) copy-start(bf16[512,1024]{1,0:T(8,128)(2,1)} %key_ref.7) | copy-start | bytes 3145732
  126.4 5.0 %copy-start.4 = (bf16[512,1024]{1,0:T(8,128)(2,1)S(1)}, bf16[512,1024]{1,0:T(8,128)(2,1)}, u32[]{:S(2)}) copy-start(bf16[512,1024]{1,0:T(8,128)(2,1)} %value_ref.7) | copy-start | bytes 3145732
  126.4 5.0 %copy-start.6 = (f32[1024]{0:T(1024)S(1)}, f32[1024]{0:T(1024)}, u32[]{:S(2)}) copy-start(f32[1024]{0:T(1024)} %param.15) | copy-start | bytes 12292
  126.4 15.0 %collective-permute-start.2 = (bf16[512,512]{1,0:T(8,128)(2,1)}, bf16[512,512]{1,0:T(8,128)(2,1)S(1)}, u32[]{:S(2)}, u32[]{:S(2)}) collective-permute-start(bf16[512,512]{1,0:T(8,128)(2,1)} %shard_map.139), channel_id=1, source_target_pairs={{0,1},{1,0},{2,3},{3,2},{4,5},{5,4},{6,7},{7,6},{8,9},{9,8},{10,11... | collective-permute-start | bytes 1572872 | tf_op jit(solution)/shard_map/ppermute | solution.py:367
  130.6 21.6 %collective-permute-start.3 = (bf16[512,512]{1,0:T(8,128)(2,1)}, bf16[512,512]{1,0:T(8,128)(2,1)}, u32[]{:S(2)}, u32[]{:S(2)}) collective-permute-start(bf16[512,512]{1,0:T(8,128)(2,1)} %shard_map.140), channel_id=1, source_target_pairs={{0,1},{1,0},{2,3},{3,2},{4,5},{5,4},{6,7},{7,6},{8,9},{9,8},{10,11... | collective-permute-start | bytes 1572872 | tf_op jit(solution)/shard_map/ppermute | solution.py:367
  131.4 1.2 copy-start.5
  132.6 3.9 %copy-start.10 = (bf16[1024,2048]{1,0:T(8,128)(2,1)S(1)}, bf16[1024,2048]{1,0:T(8,128)(2,1)}, u32[]{:S(2)}) copy-start(bf16[1024,2048]{1,0:T(8,128)(2,1)} %param.16) | copy-start | bytes 12582916
  132.6 3.9 %copy-start.12 = (bf16[512,512]{1,0:T(8,128)(2,1)S(1)}, bf16[512,512]{1,0:T(8,128)(2,1)}, u32[]{:S(2)}) copy-start(bf16[512,512]{1,0:T(8,128)(2,1)} %shard_map.140) | copy-start | bytes 1572868
  132.7 3.9 %copy-start.13 = (bf16[512,512]{1,0:T(8,128)(2,1)S(1)}, bf16[512,512]{1,0:T(8,128)(2,1)}, u32[]{:S(2)}) copy-start(bf16[512,512]{1,0:T(8,128)(2,1)} %shard_map.139) | copy-start | bytes 1572868
  136.6 4.9 %copy-start.8 = (bf16[1024,1024]{1,0:T(8,128)(2,1)S(1)}, bf16[1024,1024]{1,0:T(8,128)(2,1)}, u32[]{:S(2)}) copy-start(bf16[1024,1024]{1,0:T(8,128)(2,1)} %copy-done.7) | copy-start | bytes 6291460
  137.8 8.9 %copy-start = (f32[512,1024]{1,0:T(8,128)S(1)}, f32[512,1024]{1,0:T(8,128)}, u32[]{:S(2)}) copy-start(f32[512,1024]{1,0:T(8,128)} %bitcast_add_fusion.grad_ref.gated_ref) | copy-start | bytes 6291460

commit v5 on v4

--- a/solution.py
+++ b/solution.py
@@ -323,7 +323,7 @@
             bytes_accessed=6 * terms.size,
             transcendentals=0,
         ),
-        compiler_params=pltpu.CompilerParams(vmem_limit_bytes=VMEM_LIMIT),
+        compiler_params=pltpu.CompilerParams(vmem_limit_bytes=LAST_LIMIT),
         name="project",
     )(terms, gated, weight)
 

time: 156 us -> 155 us (level)
  transfers between devices with their start and end apart: 8 -> 8, of which waited for: 8 -> 8; matrix products, arithmetic and copies ran while one was open for 8% -> 9% of each run, Pallas kernels for 28% -> 28%
where the time goes in v5:
time: 155 us; the launch traced here: 154 us
  waiting for transfers between devices  51.6 us (33%)
  Pallas kernels  49 us (32%)
  starting transfers between devices  38 us (25%)
  matrix products  10 us (6%)
  local copies, waits for them, and re-layouts  4.59 us (3%)
    all_to_all x4, starting transfers between devices, exchange(): lax.all_to_all(values, 'seq', split_axis=0, concat_axis=0, tiled=True)  32.5 us
    ppermute x4, waiting for transfers between devices, swap_pair(): return lax.ppermute(values, 'ch', [(0, 1), (1, 0)])  29.4 us
    pallas_call x2, Pallas kernels, convolve(): pl.pallas_call(functools.partial(forward_kernel if forward else adjoint_k...  28 us
    all_to_all x4, waiting for transfers between devices, exchange(): lax.all_to_all(values, 'seq', split_axis=0, concat_axis=0, tiled=True)  22.2 us
    pallas_call x6, Pallas kernels, by_blocks(): pl.pallas_call(kernel, grid=(steps if only is None else 1,), out_shape=ou...  19.2 us
    dot_general x2, matrix products, project_back(): lax.dot_general(grad, weight, over_columns, preferred_element_type=F32)  5.6 us
    ppermute x4, starting transfers between devices, swap_pair(): return lax.ppermute(values, 'ch', [(0, 1), (1, 0)])  5.48 us
    dynamic_slice x1, local copies, waits for them, and re-layouts, on_device(): weight_other = lax.dynamic_slice_in_dim(out_weight, other, channels, axis=1)  3.29 us
  transfers between devices with their start and end apart: 8, of which 8 were waited for; matrix products, arithmetic and copies ran while one was open for 9% of the time, Pallas kernels for 28%

profile of v5, /device:TPU:0, one launch (start us, length us, event | category | flops | bytes accessed | tf_op | source)
XLA Modules:
  0.0 154.0 jit_solution(4062498423868633260)
XLA Ops:
  0.6 3.5 %shard_map.138 = bf16[16,128,512]{2,1,0:T(8,128)(2,1)} custom-call(bf16[512,1024]{1,0:T(8,128)(2,1)} %key_ref.7, bf16[512,1024]{1,0:T(8,128)(2,1)} %value_ref.7, f32[512,1024]{1,0:T(8,128)} %taps_ref.1), custom_call_target="tpu_custom_call" | custom-call | flops 2097152 | bytes 6291456 | tf_op jit(solution)/shard_map/pallas_call | solution.py:349
  4.1 0.0 copy-start.16
  4.1 7.5 %all-to-all-start = ((bf16[16,128,512]{2,1,0:T(8,128)(2,1)}), bf16[16,128,512]{2,1,0:T(8,128)(2,1)}, u32[]{:S(2)}, u32[]{:S(2)}) async-start(bf16[16,128,512]{2,1,0:T(8,128)(2,1)} %shard_map.138), calls=%async_computation | async-start | bytes 4194304 | tf_op jit(solution)/shard_map/all_to_all | solution.py:363
  11.7 0.0 copy-done.16
  11.7 1.6 %collective-permute-start = (bf16[512,1024]{1,0:T(8,128)(2,1)S(1)}, bf16[512,1024]{1,0:T(8,128)(2,1)S(1)}, u32[]{:S(2)}, u32[]{:S(2)}) collective-permute-start(bf16[512,1024]{1,0:T(8,128)(2,1)S(1)} %copy-done.16), channel_id=1, source_target_pairs={{0,1},{1,0},{2,3},{3,2},{4,5},{5,4},{6,7},{7,6},{8,9},{9,8},{10,11... | collective-permute-start | bytes 3145736 | tf_op jit(solution)/shard_map/ppermute | solution.py:367
  13.3 0.0 copy-start.11
  13.3 3.3 %constant_dynamic-slice_fusion = bf16[1024,1024]{1,0:T(8,128)(2,1)} fusion(bf16[1024,2048]{1,0:T(8,128)(2,1)} %param.16, s32[]{:T(128)S(6)} %select_n.6), kind=kLoop, calls=%fused_computation.12 | loop fusion | bytes 4194308 | tf_op jit(solution)/shard_map/dynamic_slice | solution.py:395
  16.6 0.0 copy-done.11
  16.6 1.3 fusion
  17.9 19.3 %collective-permute-done = bf16[512,1024]{1,0:T(8,128)(2,1)S(1)} collective-permute-done((bf16[512,1024]{1,0:T(8,128)(2,1)S(1)}, bf16[512,1024]{1,0:T(8,128)(2,1)S(1)}, u32[]{:S(2)}, u32[]{:S(2)}) %collective-permute-start) | collective-permute-done | bytes 1048608 | tf_op jit(solution)/shard_map/ppermute | solution.py:367
  37.2 1.5 collective-permute-start.1
  38.7 4.3 %bitcast_add_fusion.grad_ref.gated_ref = f32[512,1024]{1,0:T(8,128)} fusion(f32[1024,512]{0,1:T(8,128)S(1)} %fusion, bf16[512,1024]{1,0:T(8,128)(2,1)S(1)} %collective-permute-done, bf16[1024,1024]{1,0:T(8,128)(2,1)} %constant_dynamic-slice_fusion), kind=kOutput, calls=%fused_computation | convolution fusion | flops 1074266112 | bytes 7340032 | tf_op jit(solution)/shard_map/dot_general | solution.py:384
  43.0 2.8 %shard_map.142 = bf16[16,64,512]{2,1,0:T(8,128)(2,1)} custom-call(f32[512,1024]{1,0:T(8,128)} %bitcast_add_fusion.grad_ref.gated_ref, bf16[512,1024]{1,0:T(8,128)(2,1)} %query_ref.7), custom_call_target="tpu_custom_call" | custom-call | flops 2097152 | bytes 4194304 | tf_op jit(solution)/shard_map/pallas_call | solution.py:349
  45.8 7.0 %all-to-all-done = bf16[16,128,512]{2,1,0:T(8,128)(2,1)} async-done(((bf16[16,128,512]{2,1,0:T(8,128)(2,1)}), bf16[16,128,512]{2,1,0:T(8,128)(2,1)}, u32[]{:S(2)}, u32[]{:S(2)}) %all-to-all-start) | async-done | bytes 2097184 | tf_op jit(solution)/shard_map/all_to_all | solution.py:363
  52.8 11.2 %all-to-all-start.2 = ((bf16[16,64,512]{2,1,0:T(8,128)(2,1)}), bf16[16,64,512]{2,1,0:T(8,128)(2,1)S(1)}, u32[]{:S(2)}, u32[]{:S(2)}) async-start(bf16[16,64,512]{2,1,0:T(8,128)(2,1)} %shard_map.142), calls=%async_computation.2 | async-start | bytes 2097152 | tf_op jit(solution)/shard_map/all_to_all | solution.py:363
  64.1 15.7 %convolve.1 = (bf16[1024,512]{1,0:T(8,128)(2,1)}, f32[4096,256]{1,0:T(8,128)}) custom-call(bf16[2048,512]{1,0:T(8,128)(2,1)} %bitcast.held_ref, bf16[128,128]{1,0:T(8,128)(2,1)} %constant.20.clone.enter_ref, f32[64,256]{1,0:T(8,128)} %constant.21.clone.turn_ref, bf16[1536,256]{1,0:T(8,128)(2,1)} %constant.22.clone.waves_ref, ...), custom_call_target="tpu_custom_call" | custom-call | flops 12884901888 | bytes 8388608 | tf_op jit(solution)/shard_map/convolve/pallas_call | solution.py:225
  79.8 4.8 %collective-permute-done.1.weight_ref = bf16[1024,1024]{1,0:T(8,128)(2,1)S(1)} collective-permute-done((bf16[1024,1024]{1,0:T(8,128)(2,1)}, bf16[1024,1024]{1,0:T(8,128)(2,1)S(1)}, u32[]{:S(2)}, u32[]{:S(2)}) %collective-permute-start.1) | collective-permute-done | bytes 2097184 | tf_op jit(solution)/shard_map/ppermute | solution.py:367
  84.6 0.0 copy-start.7
  84.6 2.4 %all-to-all-done.2 = bf16[16,64,512]{2,1,0:T(8,128)(2,1)S(1)} async-done(((bf16[16,64,512]{2,1,0:T(8,128)(2,1)}), bf16[16,64,512]{2,1,0:T(8,128)(2,1)S(1)}, u32[]{:S(2)}, u32[]{:S(2)}) %all-to-all-start.2) | async-done | bytes 1048608 | tf_op jit(solution)/shard_map/all_to_all | solution.py:363
  87.0 0.0 copy-start.13
  87.0 0.0 copy-done.7
  87.0 6.9 %all-to-all-start.1 = ((bf16[16,64,512]{2,1,0:T(8,128)(2,1)}), bf16[16,64,512]{2,1,0:T(8,128)(2,1)S(1)}, u32[]{:S(2)}, u32[]{:S(2)}) async-start(bf16[16,64,512]{2,1,0:T(8,128)(2,1)} %bitcast.17), calls=%async_computation.1 | async-start | bytes 2097152 | tf_op jit(solution)/shard_map/all_to_all | solution.py:363
  93.9 0.0 copy-done.13
  93.9 12.2 %correlate.1 = bf16[1024,512]{1,0:T(8,128)(2,1)} custom-call(bf16[1024,512]{1,0:T(8,128)(2,1)} %bitcast.16, bf16[128,128]{1,0:T(8,128)(2,1)} %constant.20.clone.enter_ref, f32[64,256]{1,0:T(8,128)} %constant.21.clone.turn_ref, bf16[1536,256]{1,0:T(8,128)(2,1)} %constant.22.clone.waves_ref, bf16[64,384]{1,0:T(8,128)(2,1)} %constant.23.clone.leave_ref, ...), custom_call_target="tpu_custom_call" | custom-call | flops 8589934592 | bytes 8388608 | tf_op jit(solution)/shard_map/correlate/pallas_call | solution.py:225
  106.1 10.7 %all-to-all-done.1.message_ref = bf16[16,64,512]{2,1,0:T(8,128)(2,1)S(1)} async-done(((bf16[16,64,512]{2,1,0:T(8,128)(2,1)}), bf16[16,64,512]{2,1,0:T(8,128)(2,1)S(1)}, u32[]{:S(2)}, u32[]{:S(2)}) %all-to-all-start.1) | async-done | bytes 1048608 | tf_op jit(solution)/shard_map/all_to_all | solution.py:363
  116.8 0.0 copy-start.1
  116.8 6.9 %all-to-all-start.3 = ((bf16[16,64,512]{2,1,0:T(8,128)(2,1)}), bf16[16,64,512]{2,1,0:T(8,128)(2,1)}, u32[]{:S(2)}, u32[]{:S(2)}) async-start(bf16[16,64,512]{2,1,0:T(8,128)(2,1)} %bitcast.15), calls=%async_computation.3 | async-start | bytes 2097152 | tf_op jit(solution)/shard_map/all_to_all | solution.py:363
  123.8 0.0 copy-done.1
  123.8 2.6 %shard_map.139 = bf16[512,512]{1,0:T(8,128)(2,1)} custom-call(bf16[16,64,512]{2,1,0:T(8,128)(2,1)} %copy-done.1, bf16[512,1024]{1,0:T(8,128)(2,1)} %key_ref.7, bf16[512,1024]{1,0:T(8,128)(2,1)} %value_ref.7, bf16[512,1024]{1,0:T(8,128)(2,1)} %query_ref.7, f32[1,1024]{1,0:T(1,128)} %bitcast.11), custom_call_target="tpu_custom_call" | custom-call | flops 2097152 | bytes 4722688 | tf_op jit(solution)/shard_map/pallas_call | solution.py:349
  126.4 0.0 copy-start.2
  126.4 0.0 copy-start.3
  126.4 0.0 copy-start.4
  126.4 0.0 copy-start.10
  126.4 1.6 %collective-permute-start.2 = (bf16[512,512]{1,0:T(8,128)(2,1)}, bf16[512,512]{1,0:T(8,128)(2,1)}, u32[]{:S(2)}, u32[]{:S(2)}) collective-permute-start(bf16[512,512]{1,0:T(8,128)(2,1)} %shard_map.139), channel_id=1, source_target_pairs={{0,1},{1,0},{2,3},{3,2},{4,5},{5,4},{6,7},{7,6},{8,9},{9,8},{10,11... | collective-permute-start | bytes 1572872 | tf_op jit(solution)/shard_map/ppermute | solution.py:367
  128.0 2.6 %shard_map.140 = bf16[512,512]{1,0:T(8,128)(2,1)} custom-call(bf16[16,64,512]{2,1,0:T(8,128)(2,1)} %copy-done.1, bf16[512,1024]{1,0:T(8,128)(2,1)} %key_ref.7, bf16[512,1024]{1,0:T(8,128)(2,1)} %value_ref.7, bf16[512,1024]{1,0:T(8,128)(2,1)} %query_ref.7, f32[1,1024]{1,0:T(1,128)} %bitcast.12), custom_call_target="tpu_custom_call" | custom-call | flops 2097152 | bytes 4722688 | tf_op jit(solution)/shard_map/pallas_call | solution.py:349
  130.6 0.8 collective-permute-start.3
  131.4 0.0 copy-done.2
  131.4 0.0 copy-done.3
  131.4 0.0 copy-done.4
  131.4 0.0 copy-done.10
  131.5 0.0 copy-start.5
  131.5 1.2 copy-done.5
  132.7 0.0 copy-start.12
  132.7 0.0 copy-start.14
  132.7 0.0 copy-start.15
  132.7 3.9 %shard_map.141 = (bf16[512,1024]{1,0:T(8,128)(2,1)}, bf16[512,3072]{1,0:T(8,128)(2,1)}) custom-call(bf16[16,64,512]{2,1,0:T(8,128)(2,1)S(1)} %copy-done.2, bf16[512,1024]{1,0:T(8,128)(2,1)S(1)} %copy-done.3, bf16[512,1024]{1,0:T(8,128)(2,1)S(1)} %copy-done.4, bf16[512,1024]{1,0:T(8,128)(2,1)S(1)} %copy-done.5, f32[1,1024]{1,0:T(1,128)S(1)} %bitcast.13, ...), custom_call_target="tpu_custom_call" | custom-call | flops 2097152 | bytes 10489856 | tf_op jit(solution)/shard_map/pallas_call | solution.py:349
  136.5 0.0 copy-done.12
  136.5 0.0 copy-done.14
  136.6 0.0 copy-done.15
  136.6 0.0 copy-start.8
  136.6 1.3 fusion.2
  137.8 0.0 copy-start
  137.8 3.7 %collective-permute-done.2 = bf16[512,512]{1,0:T(8,128)(2,1)} collective-permute-done((bf16[512,512]{1,0:T(8,128)(2,1)}, bf16[512,512]{1,0:T(8,128)(2,1)}, u32[]{:S(2)}, u32[]{:S(2)}) %collective-permute-start.2) | collective-permute-done | bytes 524320 | tf_op jit(solution)/shard_map/ppermute | solution.py:367
  141.5 0.0 copy-done.8
  141.5 3.2 %convolution_add_fusion.terms_ref = f32[512,1024]{1,0:T(8,128)} fusion(f32[512,1024]{1,0:T(8,128)S(1)} %fusion.2, bf16[512,512]{1,0:T(8,128)(2,1)} %collective-permute-done.2, bf16[1024,1024]{1,0:T(8,128)(2,1)S(1)} %copy-done.8), kind=kOutput, calls=%fused_computation.5 | convolution fusion | flops 537395200 | bytes 5767168 | tf_op jit(solution)/shard_map/dot_general | solution.py:431
  144.7 2.0 %all-to-all-done.3.message_ref = bf16[16,64,512]{2,1,0:T(8,128)(2,1)} async-done(((bf16[16,64,512]{2,1,0:T(8,128)(2,1)}), bf16[16,64,512]{2,1,0:T(8,128)(2,1)}, u32[]{:S(2)}, u32[]{:S(2)}) %all-to-all-start.3) | async-done | bytes 1048608 | tf_op jit(solution)/shard_map/all_to_all | solution.py:363
  146.7 0.0 copy-done
  146.7 0.0 copy-start.6
  146.7 0.0 copy-start.9
  146.7 3.7 %shard_map.143 = (bf16[512,1024]{1,0:T(8,128)(2,1)}, bf16[512,1024]{1,0:T(8,128)(2,1)}) custom-call(bf16[16,64,512]{2,1,0:T(8,128)(2,1)} %all-to-all-done.3.message_ref, bf16[512,3072]{1,0:T(8,128)(2,1)} %get-tuple-element.29.near_ref, f32[1,1024]{1,0:T(1,128)S(1)} %bitcast.14, f32[512,1024]{1,0:T(8,128)S(1)} %copy-done), custom_call_target="tpu_custom_call" | custom-call | flops 2097152 | bytes 8392704 | tf_op jit(solution)/shard_map/pallas_call | solution.py:349
  150.5 1.6 %collective-permute-done.3.gated_ref = bf16[512,512]{1,0:T(8,128)(2,1)S(1)} collective-permute-done((bf16[512,512]{1,0:T(8,128)(2,1)}, bf16[512,512]{1,0:T(8,128)(2,1)S(1)}, u32[]{:S(2)}, u32[]{:S(2)}) %collective-permute-start.3) | collective-permute-done | bytes 524320 | tf_op jit(solution)/shard_map/ppermute | solution.py:367
  152.1 0.0 copy-done.6
  152.1 0.0 copy-done.9
  152.1 1.9 %project.1 = bf16[512,1024]{1,0:T(8,128)(2,1)} custom-call(f32[512,1024]{1,0:T(8,128)S(1)} %copy-done.6, bf16[512,512]{1,0:T(8,128)(2,1)S(1)} %collective-permute-done.3.gated_ref, bf16[1024,1024]{1,0:T(8,128)(2,1)S(1)} %copy-done.9), custom_call_target="tpu_custom_call" | custom-call | flops 536870912 | bytes 3145728 | tf_op jit(solution)/shard_map/project/pallas_call | solution.py:311
Async XLA Ops:
  4.1 7.6 %copy-start.16 = (bf16[512,1024]{1,0:T(8,128)(2,1)S(1)}, bf16[512,1024]{1,0:T(8,128)(2,1)}, u32[]{:S(2)}) copy-start(bf16[512,1024]{1,0:T(8,128)(2,1)} %param.17) | copy-start | bytes 3145732
  4.1 48.7 %all-to-all-start = ((bf16[16,128,512]{2,1,0:T(8,128)(2,1)}), bf16[16,128,512]{2,1,0:T(8,128)(2,1)}, u32[]{:S(2)}, u32[]{:S(2)}) async-start(bf16[16,128,512]{2,1,0:T(8,128)(2,1)} %shard_map.138), calls=%async_computation | async-start | bytes 4194304 | tf_op jit(solution)/shard_map/all_to_all | solution.py:363
  11.7 25.5 %collective-permute-start = (bf16[512,1024]{1,0:T(8,128)(2,1)S(1)}, bf16[512,1024]{1,0:T(8,128)(2,1)S(1)}, u32[]{:S(2)}, u32[]{:S(2)}) collective-permute-start(bf16[512,1024]{1,0:T(8,128)(2,1)S(1)} %copy-done.16), channel_id=1, source_target_pairs={{0,1},{1,0},{2,3},{3,2},{4,5},{5,4},{6,7},{7,6},{8,9},{9,8},{10,11... | collective-permute-start | bytes 3145736 | tf_op jit(solution)/shard_map/ppermute | solution.py:367
  13.3 3.3 %copy-start.11 = (bf16[1024,2048]{1,0:T(8,128)(2,1)S(1)}, bf16[1024,2048]{1,0:T(8,128)(2,1)}, u32[]{:S(2)}) copy-start(bf16[1024,2048]{1,0:T(8,128)(2,1)} %param.16) | copy-start | bytes 12582916
  37.2 47.4 %collective-permute-start.1 = (bf16[1024,1024]{1,0:T(8,128)(2,1)}, bf16[1024,1024]{1,0:T(8,128)(2,1)S(1)}, u32[]{:S(2)}, u32[]{:S(2)}) collective-permute-start(bf16[1024,1024]{1,0:T(8,128)(2,1)} %constant_dynamic-slice_fusion), channel_id=1, source_target_pairs={{0,1},{1,0},{2,3},{3,2},{4,5},{5,4},{6,7},{7,6},{8,9},{9,8},{10,11... | collective-permute-start | bytes 6291464 | tf_op jit(solution)/shard_map/ppermute | solution.py:367
  52.8 34.2 %all-to-all-start.2 = ((bf16[16,64,512]{2,1,0:T(8,128)(2,1)}), bf16[16,64,512]{2,1,0:T(8,128)(2,1)S(1)}, u32[]{:S(2)}, u32[]{:S(2)}) async-start(bf16[16,64,512]{2,1,0:T(8,128)(2,1)} %shard_map.142), calls=%async_computation.2 | async-start | bytes 2097152 | tf_op jit(solution)/shard_map/all_to_all | solution.py:363
  84.6 2.4 %copy-start.7 = (bf16[1024,1024]{1,0:T(8,128)(2,1)}, bf16[1024,1024]{1,0:T(8,128)(2,1)S(1)}, u32[]{:S(2)}) copy-start(bf16[1024,1024]{1,0:T(8,128)(2,1)S(1)} %collective-permute-done.1.weight_ref) | copy-start | bytes 6291460
  87.0 6.9 %copy-start.13 = (bf16[16,64,512]{2,1,0:T(8,128)(2,1)}, bf16[16,64,512]{2,1,0:T(8,128)(2,1)S(1)}, u32[]{:S(2)}) copy-start(bf16[16,64,512]{2,1,0:T(8,128)(2,1)S(1)} %all-to-all-done.2) | copy-start | bytes 3145732
  87.0 29.8 %all-to-all-start.1 = ((bf16[16,64,512]{2,1,0:T(8,128)(2,1)}), bf16[16,64,512]{2,1,0:T(8,128)(2,1)S(1)}, u32[]{:S(2)}, u32[]{:S(2)}) async-start(bf16[16,64,512]{2,1,0:T(8,128)(2,1)} %bitcast.17), calls=%async_computation.1 | async-start | bytes 2097152 | tf_op jit(solution)/shard_map/all_to_all | solution.py:363
  116.8 6.9 %copy-start.1 = (bf16[16,64,512]{2,1,0:T(8,128)(2,1)}, bf16[16,64,512]{2,1,0:T(8,128)(2,1)S(1)}, u32[]{:S(2)}) copy-start(bf16[16,64,512]{2,1,0:T(8,128)(2,1)S(1)} %all-to-all-done.1.message_ref) | copy-start | bytes 3145732
  116.8 29.9 %all-to-all-start.3 = ((bf16[16,64,512]{2,1,0:T(8,128)(2,1)}), bf16[16,64,512]{2,1,0:T(8,128)(2,1)}, u32[]{:S(2)}, u32[]{:S(2)}) async-start(bf16[16,64,512]{2,1,0:T(8,128)(2,1)} %bitcast.15), calls=%async_computation.3 | async-start | bytes 2097152 | tf_op jit(solution)/shard_map/all_to_all | solution.py:363
  126.4 5.0 %copy-start.2 = (bf16[16,64,512]{2,1,0:T(8,128)(2,1)S(1)}, bf16[16,64,512]{2,1,0:T(8,128)(2,1)}, u32[]{:S(2)}) copy-start(bf16[16,64,512]{2,1,0:T(8,128)(2,1)} %copy-done.1) | copy-start | bytes 3145732
  126.4 5.0 %copy-start.3 = (bf16[512,1024]{1,0:T(8,128)(2,1)S(1)}, bf16[512,1024]{1,0:T(8,128)(2,1)}, u32[]{:S(2)}) copy-start(bf16[512,1024]{1,0:T(8,128)(2,1)} %key_ref.7) | copy-start | bytes 3145732
  126.4 5.0 %copy-start.4 = (bf16[512,1024]{1,0:T(8,128)(2,1)S(1)}, bf16[512,1024]{1,0:T(8,128)(2,1)}, u32[]{:S(2)}) copy-start(bf16[512,1024]{1,0:T(8,128)(2,1)} %value_ref.7) | copy-start | bytes 3145732
  126.4 5.0 %copy-start.10 = (f32[1024]{0:T(1024)S(1)}, f32[1024]{0:T(1024)}, u32[]{:S(2)}) copy-start(f32[1024]{0:T(1024)} %param.15) | copy-start | bytes 12292
  126.4 15.1 %collective-permute-start.2 = (bf16[512,512]{1,0:T(8,128)(2,1)}, bf16[512,512]{1,0:T(8,128)(2,1)}, u32[]{:S(2)}, u32[]{:S(2)}) collective-permute-start(bf16[512,512]{1,0:T(8,128)(2,1)} %shard_map.139), channel_id=1, source_target_pairs={{0,1},{1,0},{2,3},{3,2},{4,5},{5,4},{6,7},{7,6},{8,9},{9,8},{10,11... | collective-permute-start | bytes 1572872 | tf_op jit(solution)/shard_map/ppermute | solution.py:367
  130.6 21.4 %collective-permute-start.3 = (bf16[512,512]{1,0:T(8,128)(2,1)}, bf16[512,512]{1,0:T(8,128)(2,1)S(1)}, u32[]{:S(2)}, u32[]{:S(2)}) collective-permute-start(bf16[512,512]{1,0:T(8,128)(2,1)} %shard_map.140), channel_id=1, source_target_pairs={{0,1},{1,0},{2,3},{3,2},{4,5},{5,4},{6,7},{7,6},{8,9},{9,8},{10,11... | collective-permute-start | bytes 1572872 | tf_op jit(solution)/shard_map/ppermute | solution.py:367
  131.5 1.2 copy-start.5
  132.7 3.9 %copy-start.12 = (bf16[1024,2048]{1,0:T(8,128)(2,1)S(1)}, bf16[1024,2048]{1,0:T(8,128)(2,1)}, u32[]{:S(2)}) copy-start(bf16[1024,2048]{1,0:T(8,128)(2,1)} %param.16) | copy-start | bytes 12582916
  132.7 3.9 %copy-start.14 = (bf16[512,512]{1,0:T(8,128)(2,1)S(1)}, bf16[512,512]{1,0:T(8,128)(2,1)}, u32[]{:S(2)}) copy-start(bf16[512,512]{1,0:T(8,128)(2,1)} %shard_map.140) | copy-start | bytes 1572868
  132.7 3.9 %copy-start.15 = (bf16[512,512]{1,0:T(8,128)(2,1)S(1)}, bf16[512,512]{1,0:T(8,128)(2,1)}, u32[]{:S(2)}) copy-start(bf16[512,512]{1,0:T(8,128)(2,1)} %shard_map.139) | copy-start | bytes 1572868
  136.6 5.0 %copy-start.8 = (bf16[1024,1024]{1,0:T(8,128)(2,1)S(1)}, bf16[1024,1024]{1,0:T(8,128)(2,1)}, u32[]{:S(2)}) copy-start(bf16[1024,1024]{1,0:T(8,128)(2,1)} %copy-done.7) | copy-start | bytes 6291460
  137.8 8.9 %copy-start = (f32[512,1024]{1,0:T(8,128)S(1)}, f32[512,1024]{1,0:T(8,128)}, u32[]{:S(2)}) copy-start(f32[512,1024]{1,0:T(8,128)} %bitcast_add_fusion.grad_ref.gated_ref) | copy-start | bytes 6291460
  146.7 5.4 %copy-start.6 = (f32[512,1024]{1,0:T(8,128)S(1)}, f32[512,1024]{1,0:T(8,128)}, u32[]{:S(2)}) copy-start(f32[512,1024]{1,0:T(8,128)} %convolution_add_fusion.terms_ref) | copy-start | bytes 6291460
  146.7 5.4 %copy-start.9 = (bf16[1024,1024]{1,0:T(8,128)(2,1)S(1)}, bf16[1024,1024]{1,0:T(8,128)(2,1)}, u32[]{:S(2)}) copy-start(bf16[1024,1024]{1,0:T(8,128)(2,1)} %copy-done.7) | copy-start | bytes 6291460

commit v6 on v5

--- a/solution.py
+++ b/solution.py
@@ -60,12 +60,14 @@
 
 def widen(held_ref, wide):
     for piece in range(wide.shape[0]):
-        wide[piece] = held_ref[:, piece * LANES : (piece + 1) * LANES].astype(F32)
+        block = held_ref[:, piece * LANES : (piece + 1) * LANES].astype(F32)
+        wide[piece, : block.shape[0], :] = block
 
 
 def narrow(wide, out_ref):
     for piece in range(wide.shape[0]):
-        out_ref[:, piece * LANES : (piece + 1) * LANES] = wide[piece].astype(BF16)
+        block = wide[piece, : out_ref.shape[0], :]
+        out_ref[:, piece * LANES : (piece + 1) * LANES] = block.astype(BF16)
 
 
 def load_channels(wide, first, stride, devices, group):
@@ -231,8 +233,8 @@
         + ([] if forward else [taps_block]),
         out_specs=(whole_block(out), taps_block) if forward else whole_block(out),
         scratch_shapes=[
-            pltpu.VMEM((tokens // LANES, width, LANES), F32),
-            pltpu.VMEM((tokens // LANES, devices * channels, LANES), F32),
+            pltpu.VMEM((tokens // LANES, width + width // devices, LANES), F32),
+            pltpu.VMEM((tokens // LANES, (devices + 1) * channels, LANES), F32),
         ],
         compiler_params=pltpu.CompilerParams(vmem_limit_bytes=VMEM_LIMIT),
         cost_estimate=pl.CostEstimate(

time: 155 us -> 155 us (level)
  no operation moved by 1% of the time
where the time goes in v6:
time: 155 us; the launch traced here: 154 us
  waiting for transfers between devices  51.6 us (33%)
  Pallas kernels  49 us (32%)
  starting transfers between devices  38 us (25%)
  matrix products  10 us (6%)
  local copies, waits for them, and re-layouts  4.59 us (3%)
    all_to_all x4, starting transfers between devices, exchange(): lax.all_to_all(values, 'seq', split_axis=0, concat_axis=0, tiled=True)  32.5 us
    ppermute x4, waiting for transfers between devices, swap_pair(): return lax.ppermute(values, 'ch', [(0, 1), (1, 0)])  29.4 us
    pallas_call x2, Pallas kernels, convolve(): pl.pallas_call(functools.partial(forward_kernel if forward else adjoint_k...  28 us
    all_to_all x4, waiting for transfers between devices, exchange(): lax.all_to_all(values, 'seq', split_axis=0, concat_axis=0, tiled=True)  22.2 us
    pallas_call x6, Pallas kernels, by_blocks(): pl.pallas_call(kernel, grid=(steps if only is None else 1,), out_shape=ou...  19.2 us
    dot_general x2, matrix products, project_back(): lax.dot_general(grad, weight, over_columns, preferred_element_type=F32)  5.6 us
    ppermute x4, starting transfers between devices, swap_pair(): return lax.ppermute(values, 'ch', [(0, 1), (1, 0)])  5.48 us
    dynamic_slice x1, local copies, waits for them, and re-layouts, on_device(): weight_other = lax.dynamic_slice_in_dim(out_weight, other, channels, axis=1)  3.29 us
  transfers between devices with their start and end apart: 8, of which 8 were waited for; matrix products, arithmetic and copies ran while one was open for 9% of the time, Pallas kernels for 28%

profile of v6, /device:TPU:0, one launch (start us, length us, event | category | flops | bytes accessed | tf_op | source)
XLA Modules:
  0.0 154.0 jit_solution(1530859062607542976)
XLA Ops:
  0.6 3.5 %shard_map.138 = bf16[16,128,512]{2,1,0:T(8,128)(2,1)} custom-call(bf16[512,1024]{1,0:T(8,128)(2,1)} %key_ref.7, bf16[512,1024]{1,0:T(8,128)(2,1)} %value_ref.7, f32[512,1024]{1,0:T(8,128)} %taps_ref.1), custom_call_target="tpu_custom_call" | custom-call | flops 2097152 | bytes 6291456 | tf_op jit(solution)/shard_map/pallas_call | solution.py:351
  4.1 0.0 copy-start.16
  4.1 7.5 %all-to-all-start = ((bf16[16,128,512]{2,1,0:T(8,128)(2,1)}), bf16[16,128,512]{2,1,0:T(8,128)(2,1)}, u32[]{:S(2)}, u32[]{:S(2)}) async-start(bf16[16,128,512]{2,1,0:T(8,128)(2,1)} %shard_map.138), calls=%async_computation | async-start | bytes 4194304 | tf_op jit(solution)/shard_map/all_to_all | solution.py:365
  11.7 0.0 copy-done.16
  11.7 1.6 %collective-permute-start = (bf16[512,1024]{1,0:T(8,128)(2,1)S(1)}, bf16[512,1024]{1,0:T(8,128)(2,1)S(1)}, u32[]{:S(2)}, u32[]{:S(2)}) collective-permute-start(bf16[512,1024]{1,0:T(8,128)(2,1)S(1)} %copy-done.16), channel_id=1, source_target_pairs={{0,1},{1,0},{2,3},{3,2},{4,5},{5,4},{6,7},{7,6},{8,9},{9,8},{10,11... | collective-permute-start | bytes 3145736 | tf_op jit(solution)/shard_map/ppermute | solution.py:369
  13.3 0.0 copy-start.11
  13.3 3.3 %constant_dynamic-slice_fusion = bf16[1024,1024]{1,0:T(8,128)(2,1)} fusion(bf16[1024,2048]{1,0:T(8,128)(2,1)} %param.16, s32[]{:T(128)S(6)} %select_n.6), kind=kLoop, calls=%fused_computation.12 | loop fusion | bytes 4194308 | tf_op jit(solution)/shard_map/dynamic_slice | solution.py:397
  16.6 0.0 copy-done.11
  16.6 1.3 fusion
  17.9 19.3 %collective-permute-done = bf16[512,1024]{1,0:T(8,128)(2,1)S(1)} collective-permute-done((bf16[512,1024]{1,0:T(8,128)(2,1)S(1)}, bf16[512,1024]{1,0:T(8,128)(2,1)S(1)}, u32[]{:S(2)}, u32[]{:S(2)}) %collective-permute-start) | collective-permute-done | bytes 1048608 | tf_op jit(solution)/shard_map/ppermute | solution.py:369
  37.2 1.5 collective-permute-start.1
  38.7 4.3 %bitcast_add_fusion.grad_ref.gated_ref = f32[512,1024]{1,0:T(8,128)} fusion(f32[1024,512]{0,1:T(8,128)S(1)} %fusion, bf16[512,1024]{1,0:T(8,128)(2,1)S(1)} %collective-permute-done, bf16[1024,1024]{1,0:T(8,128)(2,1)} %constant_dynamic-slice_fusion), kind=kOutput, calls=%fused_computation | convolution fusion | flops 1074266112 | bytes 7340032 | tf_op jit(solution)/shard_map/dot_general | solution.py:386
  43.0 2.8 %shard_map.142 = bf16[16,64,512]{2,1,0:T(8,128)(2,1)} custom-call(f32[512,1024]{1,0:T(8,128)} %bitcast_add_fusion.grad_ref.gated_ref, bf16[512,1024]{1,0:T(8,128)(2,1)} %query_ref.7), custom_call_target="tpu_custom_call" | custom-call | flops 2097152 | bytes 4194304 | tf_op jit(solution)/shard_map/pallas_call | solution.py:351
  45.8 7.0 %all-to-all-done = bf16[16,128,512]{2,1,0:T(8,128)(2,1)} async-done(((bf16[16,128,512]{2,1,0:T(8,128)(2,1)}), bf16[16,128,512]{2,1,0:T(8,128)(2,1)}, u32[]{:S(2)}, u32[]{:S(2)}) %all-to-all-start) | async-done | bytes 2097184 | tf_op jit(solution)/shard_map/all_to_all | solution.py:365
  52.8 11.2 %all-to-all-start.2 = ((bf16[16,64,512]{2,1,0:T(8,128)(2,1)}), bf16[16,64,512]{2,1,0:T(8,128)(2,1)S(1)}, u32[]{:S(2)}, u32[]{:S(2)}) async-start(bf16[16,64,512]{2,1,0:T(8,128)(2,1)} %shard_map.142), calls=%async_computation.2 | async-start | bytes 2097152 | tf_op jit(solution)/shard_map/all_to_all | solution.py:365
  64.1 15.7 %convolve.1 = (bf16[1024,512]{1,0:T(8,128)(2,1)}, f32[4096,256]{1,0:T(8,128)}) custom-call(bf16[2048,512]{1,0:T(8,128)(2,1)} %bitcast.held_ref, bf16[128,128]{1,0:T(8,128)(2,1)} %constant.20.clone.enter_ref, f32[64,256]{1,0:T(8,128)} %constant.21.clone.turn_ref, bf16[1536,256]{1,0:T(8,128)(2,1)} %constant.22.clone.waves_ref, ...), custom_call_target="tpu_custom_call" | custom-call | flops 12884901888 | bytes 8388608 | tf_op jit(solution)/shard_map/convolve/pallas_call | solution.py:227
  79.8 4.8 %collective-permute-done.1.weight_ref = bf16[1024,1024]{1,0:T(8,128)(2,1)S(1)} collective-permute-done((bf16[1024,1024]{1,0:T(8,128)(2,1)}, bf16[1024,1024]{1,0:T(8,128)(2,1)S(1)}, u32[]{:S(2)}, u32[]{:S(2)}) %collective-permute-start.1) | collective-permute-done | bytes 2097184 | tf_op jit(solution)/shard_map/ppermute | solution.py:369
  84.6 0.0 copy-start.7
  84.6 2.4 %all-to-all-done.2 = bf16[16,64,512]{2,1,0:T(8,128)(2,1)S(1)} async-done(((bf16[16,64,512]{2,1,0:T(8,128)(2,1)}), bf16[16,64,512]{2,1,0:T(8,128)(2,1)S(1)}, u32[]{:S(2)}, u32[]{:S(2)}) %all-to-all-start.2) | async-done | bytes 1048608 | tf_op jit(solution)/shard_map/all_to_all | solution.py:365
  87.0 0.0 copy-start.13
  87.0 0.0 copy-done.7
  87.0 6.9 %all-to-all-start.1 = ((bf16[16,64,512]{2,1,0:T(8,128)(2,1)}), bf16[16,64,512]{2,1,0:T(8,128)(2,1)S(1)}, u32[]{:S(2)}, u32[]{:S(2)}) async-start(bf16[16,64,512]{2,1,0:T(8,128)(2,1)} %bitcast.17), calls=%async_computation.1 | async-start | bytes 2097152 | tf_op jit(solution)/shard_map/all_to_all | solution.py:365
  93.9 0.0 copy-done.13
  93.9 12.2 %correlate.1 = bf16[1024,512]{1,0:T(8,128)(2,1)} custom-call(bf16[1024,512]{1,0:T(8,128)(2,1)} %bitcast.16, bf16[128,128]{1,0:T(8,128)(2,1)} %constant.20.clone.enter_ref, f32[64,256]{1,0:T(8,128)} %constant.21.clone.turn_ref, bf16[1536,256]{1,0:T(8,128)(2,1)} %constant.22.clone.waves_ref, bf16[64,384]{1,0:T(8,128)(2,1)} %constant.23.clone.leave_ref, ...), custom_call_target="tpu_custom_call" | custom-call | flops 8589934592 | bytes 8388608 | tf_op jit(solution)/shard_map/correlate/pallas_call | solution.py:227
  106.1 10.7 %all-to-all-done.1.message_ref = bf16[16,64,512]{2,1,0:T(8,128)(2,1)S(1)} async-done(((bf16[16,64,512]{2,1,0:T(8,128)(2,1)}), bf16[16,64,512]{2,1,0:T(8,128)(2,1)S(1)}, u32[]{:S(2)}, u32[]{:S(2)}) %all-to-all-start.1) | async-done | bytes 1048608 | tf_op jit(solution)/shard_map/all_to_all | solution.py:365
  116.8 0.0 copy-start.1
  116.8 6.9 %all-to-all-start.3 = ((bf16[16,64,512]{2,1,0:T(8,128)(2,1)}), bf16[16,64,512]{2,1,0:T(8,128)(2,1)}, u32[]{:S(2)}, u32[]{:S(2)}) async-start(bf16[16,64,512]{2,1,0:T(8,128)(2,1)} %bitcast.15), calls=%async_computation.3 | async-start | bytes 2097152 | tf_op jit(solution)/shard_map/all_to_all | solution.py:365
  123.8 0.0 copy-done.1
  123.8 2.6 %shard_map.139 = bf16[512,512]{1,0:T(8,128)(2,1)} custom-call(bf16[16,64,512]{2,1,0:T(8,128)(2,1)} %copy-done.1, bf16[512,1024]{1,0:T(8,128)(2,1)} %key_ref.7, bf16[512,1024]{1,0:T(8,128)(2,1)} %value_ref.7, bf16[512,1024]{1,0:T(8,128)(2,1)} %query_ref.7, f32[1,1024]{1,0:T(1,128)} %bitcast.11), custom_call_target="tpu_custom_call" | custom-call | flops 2097152 | bytes 4722688 | tf_op jit(solution)/shard_map/pallas_call | solution.py:351
  126.4 0.0 copy-start.2
  126.4 0.0 copy-start.3
  126.4 0.0 copy-start.4
  126.4 0.0 copy-start.10
  126.4 1.6 %collective-permute-start.2 = (bf16[512,512]{1,0:T(8,128)(2,1)}, bf16[512,512]{1,0:T(8,128)(2,1)}, u32[]{:S(2)}, u32[]{:S(2)}) collective-permute-start(bf16[512,512]{1,0:T(8,128)(2,1)} %shard_map.139), channel_id=1, source_target_pairs={{0,1},{1,0},{2,3},{3,2},{4,5},{5,4},{6,7},{7,6},{8,9},{9,8},{10,11... | collective-permute-start | bytes 1572872 | tf_op jit(solution)/shard_map/ppermute | solution.py:369
  128.0 2.6 %shard_map.140 = bf16[512,512]{1,0:T(8,128)(2,1)} custom-call(bf16[16,64,512]{2,1,0:T(8,128)(2,1)} %copy-done.1, bf16[512,1024]{1,0:T(8,128)(2,1)} %key_ref.7, bf16[512,1024]{1,0:T(8,128)(2,1)} %value_ref.7, bf16[512,1024]{1,0:T(8,128)(2,1)} %query_ref.7, f32[1,1024]{1,0:T(1,128)} %bitcast.12), custom_call_target="tpu_custom_call" | custom-call | flops 2097152 | bytes 4722688 | tf_op jit(solution)/shard_map/pallas_call | solution.py:351
  130.6 0.8 collective-permute-start.3
  131.4 0.0 copy-done.2
  131.4 0.0 copy-done.3
  131.4 0.0 copy-done.4
  131.4 0.0 copy-done.10
  131.5 0.0 copy-start.5
  131.5 1.2 copy-done.5
  132.7 0.0 copy-start.12
  132.7 0.0 copy-start.14
  132.7 0.0 copy-start.15
  132.7 3.9 %shard_map.141 = (bf16[512,1024]{1,0:T(8,128)(2,1)}, bf16[512,3072]{1,0:T(8,128)(2,1)}) custom-call(bf16[16,64,512]{2,1,0:T(8,128)(2,1)S(1)} %copy-done.2, bf16[512,1024]{1,0:T(8,128)(2,1)S(1)} %copy-done.3, bf16[512,1024]{1,0:T(8,128)(2,1)S(1)} %copy-done.4, bf16[512,1024]{1,0:T(8,128)(2,1)S(1)} %copy-done.5, f32[1,1024]{1,0:T(1,128)S(1)} %bitcast.13, ...), custom_call_target="tpu_custom_call" | custom-call | flops 2097152 | bytes 10489856 | tf_op jit(solution)/shard_map/pallas_call | solution.py:351
  136.5 0.0 copy-done.12
  136.5 0.0 copy-done.14
  136.6 0.0 copy-done.15
  136.6 0.0 copy-start.8
  136.6 1.3 fusion.2
  137.8 0.0 copy-start
  137.8 3.7 %collective-permute-done.2 = bf16[512,512]{1,0:T(8,128)(2,1)} collective-permute-done((bf16[512,512]{1,0:T(8,128)(2,1)}, bf16[512,512]{1,0:T(8,128)(2,1)}, u32[]{:S(2)}, u32[]{:S(2)}) %collective-permute-start.2) | collective-permute-done | bytes 524320 | tf_op jit(solution)/shard_map/ppermute | solution.py:369
  141.5 0.0 copy-done.8
  141.5 3.2 %convolution_add_fusion.terms_ref = f32[512,1024]{1,0:T(8,128)} fusion(f32[512,1024]{1,0:T(8,128)S(1)} %fusion.2, bf16[512,512]{1,0:T(8,128)(2,1)} %collective-permute-done.2, bf16[1024,1024]{1,0:T(8,128)(2,1)S(1)} %copy-done.8), kind=kOutput, calls=%fused_computation.5 | convolution fusion | flops 537395200 | bytes 5767168 | tf_op jit(solution)/shard_map/dot_general | solution.py:433
  144.7 2.0 %all-to-all-done.3.message_ref = bf16[16,64,512]{2,1,0:T(8,128)(2,1)} async-done(((bf16[16,64,512]{2,1,0:T(8,128)(2,1)}), bf16[16,64,512]{2,1,0:T(8,128)(2,1)}, u32[]{:S(2)}, u32[]{:S(2)}) %all-to-all-start.3) | async-done | bytes 1048608 | tf_op jit(solution)/shard_map/all_to_all | solution.py:365
  146.7 0.0 copy-done
  146.7 0.0 copy-start.6
  146.7 0.0 copy-start.9
  146.7 3.7 %shard_map.143 = (bf16[512,1024]{1,0:T(8,128)(2,1)}, bf16[512,1024]{1,0:T(8,128)(2,1)}) custom-call(bf16[16,64,512]{2,1,0:T(8,128)(2,1)} %all-to-all-done.3.message_ref, bf16[512,3072]{1,0:T(8,128)(2,1)} %get-tuple-element.29.near_ref, f32[1,1024]{1,0:T(1,128)S(1)} %bitcast.14, f32[512,1024]{1,0:T(8,128)S(1)} %copy-done), custom_call_target="tpu_custom_call" | custom-call | flops 2097152 | bytes 8392704 | tf_op jit(solution)/shard_map/pallas_call | solution.py:351
  150.5 1.6 %collective-permute-done.3.gated_ref = bf16[512,512]{1,0:T(8,128)(2,1)S(1)} collective-permute-done((bf16[512,512]{1,0:T(8,128)(2,1)}, bf16[512,512]{1,0:T(8,128)(2,1)S(1)}, u32[]{:S(2)}, u32[]{:S(2)}) %collective-permute-start.3) | collective-permute-done | bytes 524320 | tf_op jit(solution)/shard_map/ppermute | solution.py:369
  152.1 0.0 copy-done.6
  152.1 0.0 copy-done.9
  152.1 1.9 %project.1 = bf16[512,1024]{1,0:T(8,128)(2,1)} custom-call(f32[512,1024]{1,0:T(8,128)S(1)} %copy-done.6, bf16[512,512]{1,0:T(8,128)(2,1)S(1)} %collective-permute-done.3.gated_ref, bf16[1024,1024]{1,0:T(8,128)(2,1)S(1)} %copy-done.9), custom_call_target="tpu_custom_call" | custom-call | flops 536870912 | bytes 3145728 | tf_op jit(solution)/shard_map/project/pallas_call | solution.py:313
Async XLA Ops:
  4.1 7.6 %copy-start.16 = (bf16[512,1024]{1,0:T(8,128)(2,1)S(1)}, bf16[512,1024]{1,0:T(8,128)(2,1)}, u32[]{:S(2)}) copy-start(bf16[512,1024]{1,0:T(8,128)(2,1)} %param.17) | copy-start | bytes 3145732
  4.1 48.7 %all-to-all-start = ((bf16[16,128,512]{2,1,0:T(8,128)(2,1)}), bf16[16,128,512]{2,1,0:T(8,128)(2,1)}, u32[]{:S(2)}, u32[]{:S(2)}) async-start(bf16[16,128,512]{2,1,0:T(8,128)(2,1)} %shard_map.138), calls=%async_computation | async-start | bytes 4194304 | tf_op jit(solution)/shard_map/all_to_all | solution.py:365
  11.7 25.5 %collective-permute-start = (bf16[512,1024]{1,0:T(8,128)(2,1)S(1)}, bf16[512,1024]{1,0:T(8,128)(2,1)S(1)}, u32[]{:S(2)}, u32[]{:S(2)}) collective-permute-start(bf16[512,1024]{1,0:T(8,128)(2,1)S(1)} %copy-done.16), channel_id=1, source_target_pairs={{0,1},{1,0},{2,3},{3,2},{4,5},{5,4},{6,7},{7,6},{8,9},{9,8},{10,11... | collective-permute-start | bytes 3145736 | tf_op jit(solution)/shard_map/ppermute | solution.py:369
  13.3 3.3 %copy-start.11 = (bf16[1024,2048]{1,0:T(8,128)(2,1)S(1)}, bf16[1024,2048]{1,0:T(8,128)(2,1)}, u32[]{:S(2)}) copy-start(bf16[1024,2048]{1,0:T(8,128)(2,1)} %param.16) | copy-start | bytes 12582916
  37.2 47.4 %collective-permute-start.1 = (bf16[1024,1024]{1,0:T(8,128)(2,1)}, bf16[1024,1024]{1,0:T(8,128)(2,1)S(1)}, u32[]{:S(2)}, u32[]{:S(2)}) collective-permute-start(bf16[1024,1024]{1,0:T(8,128)(2,1)} %constant_dynamic-slice_fusion), channel_id=1, source_target_pairs={{0,1},{1,0},{2,3},{3,2},{4,5},{5,4},{6,7},{7,6},{8,9},{9,8},{10,11... | collective-permute-start | bytes 6291464 | tf_op jit(solution)/shard_map/ppermute | solution.py:369
  52.8 34.2 %all-to-all-start.2 = ((bf16[16,64,512]{2,1,0:T(8,128)(2,1)}), bf16[16,64,512]{2,1,0:T(8,128)(2,1)S(1)}, u32[]{:S(2)}, u32[]{:S(2)}) async-start(bf16[16,64,512]{2,1,0:T(8,128)(2,1)} %shard_map.142), calls=%async_computation.2 | async-start | bytes 2097152 | tf_op jit(solution)/shard_map/all_to_all | solution.py:365
  84.6 2.4 %copy-start.7 = (bf16[1024,1024]{1,0:T(8,128)(2,1)}, bf16[1024,1024]{1,0:T(8,128)(2,1)S(1)}, u32[]{:S(2)}) copy-start(bf16[1024,1024]{1,0:T(8,128)(2,1)S(1)} %collective-permute-done.1.weight_ref) | copy-start | bytes 6291460
  87.0 6.9 %copy-start.13 = (bf16[16,64,512]{2,1,0:T(8,128)(2,1)}, bf16[16,64,512]{2,1,0:T(8,128)(2,1)S(1)}, u32[]{:S(2)}) copy-start(bf16[16,64,512]{2,1,0:T(8,128)(2,1)S(1)} %all-to-all-done.2) | copy-start | bytes 3145732
  87.0 29.8 %all-to-all-start.1 = ((bf16[16,64,512]{2,1,0:T(8,128)(2,1)}), bf16[16,64,512]{2,1,0:T(8,128)(2,1)S(1)}, u32[]{:S(2)}, u32[]{:S(2)}) async-start(bf16[16,64,512]{2,1,0:T(8,128)(2,1)} %bitcast.17), calls=%async_computation.1 | async-start | bytes 2097152 | tf_op jit(solution)/shard_map/all_to_all | solution.py:365
  116.8 6.9 %copy-start.1 = (bf16[16,64,512]{2,1,0:T(8,128)(2,1)}, bf16[16,64,512]{2,1,0:T(8,128)(2,1)S(1)}, u32[]{:S(2)}) copy-start(bf16[16,64,512]{2,1,0:T(8,128)(2,1)S(1)} %all-to-all-done.1.message_ref) | copy-start | bytes 3145732
  116.8 29.9 %all-to-all-start.3 = ((bf16[16,64,512]{2,1,0:T(8,128)(2,1)}), bf16[16,64,512]{2,1,0:T(8,128)(2,1)}, u32[]{:S(2)}, u32[]{:S(2)}) async-start(bf16[16,64,512]{2,1,0:T(8,128)(2,1)} %bitcast.15), calls=%async_computation.3 | async-start | bytes 2097152 | tf_op jit(solution)/shard_map/all_to_all | solution.py:365
  126.4 5.0 %copy-start.2 = (bf16[16,64,512]{2,1,0:T(8,128)(2,1)S(1)}, bf16[16,64,512]{2,1,0:T(8,128)(2,1)}, u32[]{:S(2)}) copy-start(bf16[16,64,512]{2,1,0:T(8,128)(2,1)} %copy-done.1) | copy-start | bytes 3145732
  126.4 5.0 %copy-start.3 = (bf16[512,1024]{1,0:T(8,128)(2,1)S(1)}, bf16[512,1024]{1,0:T(8,128)(2,1)}, u32[]{:S(2)}) copy-start(bf16[512,1024]{1,0:T(8,128)(2,1)} %key_ref.7) | copy-start | bytes 3145732
  126.4 5.0 %copy-start.4 = (bf16[512,1024]{1,0:T(8,128)(2,1)S(1)}, bf16[512,1024]{1,0:T(8,128)(2,1)}, u32[]{:S(2)}) copy-start(bf16[512,1024]{1,0:T(8,128)(2,1)} %value_ref.7) | copy-start | bytes 3145732
  126.4 5.0 %copy-start.10 = (f32[1024]{0:T(1024)S(1)}, f32[1024]{0:T(1024)}, u32[]{:S(2)}) copy-start(f32[1024]{0:T(1024)} %param.15) | copy-start | bytes 12292
  126.4 15.1 %collective-permute-start.2 = (bf16[512,512]{1,0:T(8,128)(2,1)}, bf16[512,512]{1,0:T(8,128)(2,1)}, u32[]{:S(2)}, u32[]{:S(2)}) collective-permute-start(bf16[512,512]{1,0:T(8,128)(2,1)} %shard_map.139), channel_id=1, source_target_pairs={{0,1},{1,0},{2,3},{3,2},{4,5},{5,4},{6,7},{7,6},{8,9},{9,8},{10,11... | collective-permute-start | bytes 1572872 | tf_op jit(solution)/shard_map/ppermute | solution.py:369
  130.6 21.4 %collective-permute-start.3 = (bf16[512,512]{1,0:T(8,128)(2,1)}, bf16[512,512]{1,0:T(8,128)(2,1)S(1)}, u32[]{:S(2)}, u32[]{:S(2)}) collective-permute-start(bf16[512,512]{1,0:T(8,128)(2,1)} %shard_map.140), channel_id=1, source_target_pairs={{0,1},{1,0},{2,3},{3,2},{4,5},{5,4},{6,7},{7,6},{8,9},{9,8},{10,11... | collective-permute-start | bytes 1572872 | tf_op jit(solution)/shard_map/ppermute | solution.py:369
  131.5 1.2 copy-start.5
  132.7 3.9 %copy-start.12 = (bf16[1024,2048]{1,0:T(8,128)(2,1)S(1)}, bf16[1024,2048]{1,0:T(8,128)(2,1)}, u32[]{:S(2)}) copy-start(bf16[1024,2048]{1,0:T(8,128)(2,1)} %param.16) | copy-start | bytes 12582916
  132.7 3.9 %copy-start.14 = (bf16[512,512]{1,0:T(8,128)(2,1)S(1)}, bf16[512,512]{1,0:T(8,128)(2,1)}, u32[]{:S(2)}) copy-start(bf16[512,512]{1,0:T(8,128)(2,1)} %shard_map.140) | copy-start | bytes 1572868
  132.7 3.9 %copy-start.15 = (bf16[512,512]{1,0:T(8,128)(2,1)S(1)}, bf16[512,512]{1,0:T(8,128)(2,1)}, u32[]{:S(2)}) copy-start(bf16[512,512]{1,0:T(8,128)(2,1)} %shard_map.139) | copy-start | bytes 1572868
  136.6 5.0 %copy-start.8 = (bf16[1024,1024]{1,0:T(8,128)(2,1)S(1)}, bf16[1024,1024]{1,0:T(8,128)(2,1)}, u32[]{:S(2)}) copy-start(bf16[1024,1024]{1,0:T(8,128)(2,1)} %copy-done.7) | copy-start | bytes 6291460
  137.8 8.9 %copy-start = (f32[512,1024]{1,0:T(8,128)S(1)}, f32[512,1024]{1,0:T(8,128)}, u32[]{:S(2)}) copy-start(f32[512,1024]{1,0:T(8,128)} %bitcast_add_fusion.grad_ref.gated_ref) | copy-start | bytes 6291460
  146.7 5.4 %copy-start.6 = (f32[512,1024]{1,0:T(8,128)S(1)}, f32[512,1024]{1,0:T(8,128)}, u32[]{:S(2)}) copy-start(f32[512,1024]{1,0:T(8,128)} %convolution_add_fusion.terms_ref) | copy-start | bytes 6291460
  146.7 5.4 %copy-start.9 = (bf16[1024,1024]{1,0:T(8,128)(2,1)S(1)}, bf16[1024,1024]{1,0:T(8,128)(2,1)}, u32[]{:S(2)}) copy-start(bf16[1024,1024]{1,0:T(8,128)(2,1)} %copy-done.7) | copy-start | bytes 6291460
